TPU v7x, 32 devices: a whole 2x2x4 slice. The times are simulated.
32 devices in a mesh: row: 8 (over y, x, core), col: 4 (over z).
Axes of the slice: x: 2, y: 2, z: 4, core: 2. Of those that a mesh axis runs over, the one named last changes fastest.
Arguments:
- covariance: bfloat16 [2048, 2048], P('row', 'col'), may hold values from -16 to 16
- reflectors: bfloat16 [2048, 128], P('row'), may hold values from -0.5 to 0.5
- factor: float32 [128, 128], replicated, may hold values from -0.5 to 2, as said below
Outputs:
- updated: float32 [2048, 2048], P('row', 'col')
Inputs may be any that keep to these rules, and one draw needn't show every extreme that they name: factor is upper triangular with a diagonal of 1 to 2.
All inputs are finite; a program needn't handle non-finite values.
Results may differ from a plain program's by a relative error of at most 0.0003.
Values may be sent and summed in bfloat16 or wider, within the bound.
No kernel may reach another device: no remote copies, remote signals or barrier semaphores. Data moves between devices by JAX's collectives and lax.ppermute only.
A program may use at most 64 MiB of HBM per device.

v0:
```python
import jax
import jax.numpy as jnp
from jax import lax
from jax.sharding import PartitionSpec as P


def shards(covariance, reflectors, factor):
    highest = lax.Precision.HIGHEST
    width = covariance.shape[1]
    col_start = lax.axis_index("col") * width
    whole_v = lax.all_gather(reflectors, "row", axis=0, tiled=True)
    v_cols = lax.dynamic_slice_in_dim(whole_v, col_start, width, 0)
    partial_value = jnp.dot(covariance, v_cols, preferred_element_type=jnp.float32)
    vectors = reflectors.astype(jnp.float32)
    summed = lax.psum(partial_value, "col")
    mixed = jnp.dot(summed, factor, precision=highest)
    gram = lax.psum(jnp.dot(vectors.T, mixed, precision=highest), "row")
    correction = jnp.dot(factor.T, gram, precision=highest)
    update_rows = mixed - 0.5 * jnp.dot(vectors, correction, precision=highest)
    v_cols_f = v_cols.astype(jnp.float32)
    back = lax.dot_general(
        covariance, reflectors, (((0,), (0,)), ((), ())), preferred_element_type=jnp.float32
    )
    back_sum = lax.psum(back, "row")
    update_cols = jnp.dot(back_sum, factor, precision=highest) - 0.5 * jnp.dot(
        v_cols_f, correction, precision=highest
    )
    updated = covariance.astype(jnp.float32) - jnp.dot(vectors, update_cols.T, precision=highest)
    return updated - jnp.dot(update_rows, v_cols_f.T, precision=highest)


def solution(mesh):
    in_specs = (P("row", "col"), P("row", None), P())
    out_specs = P("row", "col")
    return jax.shard_map(shards, mesh=mesh, in_specs=in_specs, out_specs=out_specs, check_vma=False)
```

profile of v0, /device:TPU:0, one launch (start us, length us, event | category | flops | bytes accessed | tf_op | source)
XLA Modules:
  0.0 122.0 jit_solution(16763747887274637904)
XLA Ops:
  6.5 0.0 copy-start
  6.5 0.0 all-reduce.4.cloned.1.call-start
  6.5 0.0 copy-start.1
  6.5 11.7 %all_gather.3 = bf16[2048,128]{1,0:T(8,128)(2,1)S(1)} all-gather(bf16[256,128]{1,0:T(8,128)(2,1)} %param.4), channel_id=1, replica_groups=mesh['row'=8,'col'=4] {'row'}, dimensions={0}, use_global_device_ids=true | all-gather | bytes 589824 | tf_op jit(solution)/shard_map/all_gather | solution.py:11
  18.3 0.0 copy-done.1
  18.3 0.9 convolution_bitcast_fusion.1
  19.1 0.0 copy-start.2
  19.1 0.0 all-reduce.4.cloned.1.call-update
  19.2 0.0 all-reduce.6.cloned.1.call-start
  19.2 0.8 copy-done.2
  20.0 1.0 fusion.10
  21.0 33.1 %all-reduce.4.cloned.1.call-done = f32[256,128]{0,1:T(8,128)} async-done(((f32[256,128]{0,1:T(8,128)}), f32[256,128]{0,1:T(8,128)}) %all-reduce.4.cloned.1.call-update) | async-done | bytes 131088 | tf_op jit(solution)/shard_map/psum | solution.py:15
  54.1 0.0 copy-done
  54.1 1.3 %fusion.12 = f32[256,128]{1,0:T(8,128)S(1)} fusion(f32[256,128]{0,1:T(8,128)} %all-reduce.4.cloned.1.call-done, f32[128,128]{1,0:T(8,128)S(1)} %copy-done), kind=kOutput, calls=%fused_computation.18 | convolution fusion | flops 50331648 | bytes 327680 | tf_op jit(solution)/shard_map/dot_general | solution.py:16
  55.4 0.9 convolution_bitcast_fusion.2
  56.3 0.0 all-reduce.6.cloned.1.call-update
  56.3 0.1 copy.4
  56.5 54.8 %all-reduce.6.cloned.1.call-done = (f32[512,128]{1,0:T(8,128)}, f32[128,128]{0,1:T(8,128)}) async-done(((f32[512,128]{1,0:T(8,128)}, f32[128,128]{0,1:T(8,128)}), (f32[512,128]{1,0:T(8,128)}, f32[128,128]{0,1:T(8,128)})) %all-reduce.6.cloned.1.call-update) | async-done | bytes 327696 | tf_op jit(solution)/shard_map/psum | solution.py:24
  111.3 0.0 copy-start.3
  111.3 1.3 %fusion.11 = f32[512,128]{1,0:T(8,128)S(1)} fusion(f32[512,128]{1,0:T(8,128)} %get-tuple-element.5, f32[128,128]{1,0:T(8,128)S(1)} %copy-done), kind=kOutput, calls=%fused_computation.17 | convolution fusion | flops 100663296 | bytes 589824 | tf_op jit(solution)/shard_map/dot_general | solution.py:25
  112.6 0.0 copy-done.3
  112.6 0.2 fusion.13
  112.8 0.2 fusion.3
  113.1 0.3 fusion.1
  113.4 0.4 fusion
  113.8 0.4 convolution_subtract_fusion
  114.1 1.0 copy.6
Async XLA Ops:
  6.5 47.6 %copy-start = (f32[128,128]{1,0:T(8,128)S(1)}, f32[128,128]{1,0:T(8,128)}, u32[]{:S(2)}) copy-start(f32[128,128]{1,0:T(8,128)} %param.5) | copy-start | bytes 196612
  6.5 47.6 %all-reduce.4.cloned.1.call-start = ((), (), s32[]{:S(2)}) async-start(), calls=%async_computation | async-start | bytes 262144 | tf_op jit(solution)/shard_map/psum | solution.py:15
  6.5 11.7 %copy-start.1 = (bf16[256,512]{1,0:T(8,128)(2,1)S(1)}, bf16[256,512]{1,0:T(8,128)(2,1)}, u32[]{:S(2)}) copy-start(bf16[256,512]{1,0:T(8,128)(2,1)} %param.3) | copy-start | bytes 786436
  19.1 0.8 copy-start.2
  19.2 92.1 %all-reduce.6.cloned.1.call-start = ((), (), s32[]{:S(2)}) async-start(), calls=%async_computation.1 | async-start | bytes 655360 | tf_op jit(solution)/shard_map/psum | solution.py:24
  111.3 1.4 %copy-start.3 = (f32[128,128]{0,1:T(8,128)S(1)}, f32[128,128]{0,1:T(8,128)}, u32[]{:S(2)}) copy-start(f32[128,128]{0,1:T(8,128)} %get-tuple-element.6) | copy-start | bytes 196612
Sparse Core Ops, SparseCore 0:
  19.3 34.7 all-reduce.3
  57.5 53.6 all-reduce.5
where the time goes:
time: 122 us
  waiting for transfers between devices  88 us (72%)
  between operations  13.5 us (11%)
  blocking collectives  11.7 us (10%)
  matrix products  6.88 us (6%)
  local copies, waits for them, and re-layouts  1.9 us (2%)
    psum x1, waiting for transfers between devices, shards(): back_sum = lax.psum(back, 'row')  54.8 us
    psum x1, waiting for transfers between devices, shards(): summed = lax.psum(partial_value, 'col')  33.1 us
    all_gather x1, blocking collectives, shards(): whole_v = lax.all_gather(reflectors, 'row', axis=0, tiled=True)  11.7 us
  transfers between devices with their start and end apart: 2, of which 2 were waited for; matrix products, arithmetic and copies ran while one was open for 1% of the time, Pallas kernels for 0%

commit v1 on v0

v1 whole, which is shorter than its diff:
```python
import jax
import jax.numpy as jnp
from jax import lax
from jax.sharding import PartitionSpec as P


def solution(mesh):
    n_row, n_col = mesh.shape["row"], mesh.shape["col"]
    q = n_row // n_col
    highest = lax.Precision.HIGHEST

    def device(k, h, c):
        return (k * q + h) * n_col + c

    mirror = [
        (device(c, h, k), device(k, h, c))
        for k in range(n_col) for h in range(q) for c in range(n_col)
    ]

    def member(x, s):
        return lax.ppermute(x, "row", [(r, r ^ s) for r in range(n_row)])

    def group(x, s):
        return lax.ppermute(x, "row", [(r, r ^ (s * q)) for r in range(n_row)])

    def plane(x, s):
        return lax.ppermute(x, "col", [(c, c ^ s) for c in range(n_col)])

    def from_mirror(x):
        return lax.ppermute(x, ("row", "col"), mirror)

    def dot(a, b, dims):
        return lax.dot_general(a, b, (dims, ((), ())), precision=highest, preferred_element_type=jnp.float32)

    def gathered(own, pieces, h):
        rows = own.shape[0]
        whole = jnp.zeros((q * rows, own.shape[1]), own.dtype)
        for s, piece in enumerate([own] + pieces):
            whole = lax.dynamic_update_slice_in_dim(whole, piece, (h ^ s) * rows, 0)
        return whole

    def shards(covariance, reflectors, factor):
        rows = covariance.shape[0]
        h = lax.rem(lax.axis_index("row"), q)
        back = lax.dot_general(
            covariance, reflectors, (((0,), (0,)), ((), ())), preferred_element_type=jnp.float32
        )
        piece = lax.dynamic_slice_in_dim(back, h * rows, rows, 0)
        for s in range(1, q):
            piece = piece + member(lax.dynamic_slice_in_dim(back, (h ^ s) * rows, rows, 0), s)
        total = piece
        for s in range(1, n_col):
            total = total + group(piece, s)
        v_piece = from_mirror(reflectors)
        v_cols = gathered(v_piece, [member(v_piece, s) for s in range(1, q)], h)
        p_cols = gathered(total, [member(total, s) for s in range(1, q)], h)
        p_rows = from_mirror(total)
        gram = dot(v_piece.astype(jnp.float32), total, ((0,), (0,)))
        summed = gram
        for s in range(1, n_col):
            summed = summed + plane(gram, s)
        whole = summed
        for s in range(1, q):
            whole = whole + member(summed, s)
        y_rows = dot(reflectors.astype(jnp.float32), factor, ((1,), (1,)))
        y_cols = dot(v_cols.astype(jnp.float32), factor, ((1,), (1,)))
        first = covariance.astype(jnp.float32) - dot(y_rows, p_cols, ((1,), (1,)))
        x_rows = p_rows - dot(y_rows, whole, ((1,), (0,)))
        return first - dot(x_rows, y_cols, ((1,), (1,)))

    in_specs = (P("row", "col"), P("row", None), P())
    return jax.shard_map(shards, mesh=mesh, in_specs=in_specs, out_specs=P("row", "col"), check_vma=False)
```

time: 122 us -> 41.6 us (0.34)
  the two profiles are of different devices: /device:TPU:0 before, /device:TPU:2 now
where the time goes in v1:
time: 41.6 us; the launch traced here: 41.3 us
  waiting for transfers between devices  21.8 us (52%)
  starting transfers between devices  14.2 us (34%)
  matrix products  4.28 us (10%)
  local copies, waits for them, and re-layouts  0.84 us (2%)
    ppermute x2, waiting for transfers between devices, from_mirror(): return lax.ppermute(x, ('row', 'col'), mirror)  11.3 us
    ppermute x3, waiting for transfers between devices, group(): return lax.ppermute(x, 'row', [(r, r ^ s * q) for r in range(n_row)])  6.61 us
    ppermute x2, starting transfers between devices, from_mirror(): return lax.ppermute(x, ('row', 'col'), mirror)  5.65 us
    ppermute x3, starting transfers between devices, plane(): return lax.ppermute(x, 'col', [(c, c ^ s) for c in range(n_col)])  4.45 us
    ppermute x3, starting transfers between devices, group(): return lax.ppermute(x, 'row', [(r, r ^ s * q) for r in range(n_row)])  3.84 us
    dot_general x6, matrix products, dot(): lax.dot_general(a, b, (dims, ((), ())), precision=highest, preferred_elem...  3.07 us
    ppermute x3, waiting for transfers between devices, plane(): return lax.ppermute(x, 'col', [(c, c ^ s) for c in range(n_col)])  2.7 us
    ppermute x4, waiting for transfers between devices, member(): return lax.ppermute(x, 'row', [(r, r ^ s) for r in range(n_row)])  1.21 us
  transfers between devices with their start and end apart: 12, of which 8 were waited for; matrix products, arithmetic and copies ran while one was open for 5% of the time, Pallas kernels for 0%

profile of v1, /device:TPU:2, one launch (start us, length us, event | category | flops | bytes accessed | tf_op | source)
XLA Modules:
  0.0 41.3 jit_solution(2699894028567229014)
XLA Ops:
  0.0 0.0 copy-start
  0.0 3.6 %collective-permute-start.6 = (bf16[256,128]{1,0:T(8,128)(2,1)}, bf16[256,128]{1,0:T(8,128)(2,1)S(1)}, u32[]{:S(2)}, u32[]{:S(2)}) collective-permute-start(bf16[256,128]{1,0:T(8,128)(2,1)} %param.4), channel_id=1, source_target_pairs={{0,0},{8,1},{16,2},{24,3},{4,4},{12,5},{20,6},{28,7},{1,8},{9,9},{... | collective-permute-start | bytes 196616 | tf_op jit(solution)/shard_map/ppermute | solution.py:30
  3.6 1.2 %fusion.6 = f32[512,128]{1,0:T(8,128)S(1)} fusion(bf16[256,512]{1,0:T(8,128)(2,1)} %param.3, bf16[256,128]{1,0:T(8,128)(2,1)} %param.4), kind=kOutput, calls=%fused_computation.16 | convolution fusion | flops 33554432 | bytes 589824 | tf_op jit(solution)/shard_map/dot_general | solution.py:45
  4.8 0.0 copy-start.2
  4.9 0.1 collective-permute-start
  4.9 0.0 copy-done
  4.9 0.7 %copy-done.2 = bf16[256,128]{1,0:T(8,128)(2,1)S(1)} copy-done((bf16[256,128]{1,0:T(8,128)(2,1)S(1)}, bf16[256,128]{1,0:T(8,128)(2,1)}, u32[]{:S(2)}) %copy-start.2) | copy-done | bytes 65560
  5.7 0.2 fusion.5
  5.9 3.4 %collective-permute-done.6 = bf16[256,128]{1,0:T(8,128)(2,1)S(1)} collective-permute-done((bf16[256,128]{1,0:T(8,128)(2,1)}, bf16[256,128]{1,0:T(8,128)(2,1)S(1)}, u32[]{:S(2)}, u32[]{:S(2)}) %collective-permute-start.6) | collective-permute-done | bytes 65568 | tf_op jit(solution)/shard_map/ppermute | solution.py:30
  9.3 0.0 collective-permute-start.11
  9.3 0.0 collective-permute-done
  9.3 0.1 collective-permute-start.1
  9.4 2.4 %collective-permute-start.2 = (f32[256,128]{1,0:T(8,128)S(1)}, f32[256,128]{1,0:T(8,128)S(1)}, u32[]{:S(2)}, u32[]{:S(2)}) collective-permute-start(f32[256,128]{1,0:T(8,128)S(1)} %dynamic-slice_add_fusion), channel_id=1, source_target_pairs={{0,16},{4,20},{8,24},{12,28},{16,0},{20,4},{24,8},{28,12},{1,17},{... | collective-permute-start | bytes 393224 | tf_op jit(solution)/shard_map/ppermute | solution.py:24
  11.8 1.4 %collective-permute-start.3 = (f32[256,128]{1,0:T(8,128)S(1)}, f32[256,128]{1,0:T(8,128)S(1)}, u32[]{:S(2)}, u32[]{:S(2)}) collective-permute-start(f32[256,128]{1,0:T(8,128)S(1)} %dynamic-slice_add_fusion), channel_id=1, source_target_pairs={{0,24},{4,28},{8,16},{12,20},{16,8},{20,12},{24,0},{28,4},{1,25},{... | collective-permute-start | bytes 393224 | tf_op jit(solution)/shard_map/ppermute | solution.py:24
  13.2 0.0 collective-permute-done.11
  13.3 2.4 %collective-permute-done.1 = f32[256,128]{1,0:T(8,128)S(1)} collective-permute-done((f32[256,128]{1,0:T(8,128)S(1)}, f32[256,128]{1,0:T(8,128)S(1)}, u32[]{:S(2)}, u32[]{:S(2)}) %collective-permute-start.1) | collective-permute-done | bytes 131104 | tf_op jit(solution)/shard_map/ppermute | solution.py:24
  15.7 2.3 %collective-permute-done.2 = f32[256,128]{1,0:T(8,128)S(1)} collective-permute-done((f32[256,128]{1,0:T(8,128)S(1)}, f32[256,128]{1,0:T(8,128)S(1)}, u32[]{:S(2)}, u32[]{:S(2)}) %collective-permute-start.2) | collective-permute-done | bytes 131104 | tf_op jit(solution)/shard_map/ppermute | solution.py:24
  18.0 1.8 %collective-permute-done.3 = f32[256,128]{1,0:T(8,128)S(1)} collective-permute-done((f32[256,128]{1,0:T(8,128)S(1)}, f32[256,128]{1,0:T(8,128)S(1)}, u32[]{:S(2)}, u32[]{:S(2)}) %collective-permute-start.3) | collective-permute-done | bytes 131104 | tf_op jit(solution)/shard_map/ppermute | solution.py:24
  19.9 0.3 convolution_bitcast_fusion
  20.2 0.1 collective-permute-start.7
  20.3 3.4 %collective-permute-start.8 = (f32[128,128]{0,1:T(8,128)S(1)}, f32[128,128]{0,1:T(8,128)S(1)}, u32[]{:S(2)}, u32[]{:S(2)}) collective-permute-start(f32[128,128]{0,1:T(8,128)S(1)} %convolution_bitcast_fusion), channel_id=1, source_target_pairs={{0,2},{1,3},{2,0},{3,1},{4,6},{5,7},{6,4},{7,5},{8,10},{9,11},{10,... | collective-permute-start | bytes 196616 | tf_op jit(solution)/shard_map/ppermute | solution.py:27
  23.8 0.9 %collective-permute-start.9 = (f32[128,128]{0,1:T(8,128)S(1)}, f32[128,128]{0,1:T(8,128)S(1)}, u32[]{:S(2)}, u32[]{:S(2)}) collective-permute-start(f32[128,128]{0,1:T(8,128)S(1)} %convolution_bitcast_fusion), channel_id=1, source_target_pairs={{0,3},{1,2},{2,1},{3,0},{4,7},{5,6},{6,5},{7,4},{8,11},{9,10},{10,... | collective-permute-start | bytes 196616 | tf_op jit(solution)/shard_map/ppermute | solution.py:27
  24.7 0.3 fusion.7
  25.0 0.1 collective-permute-start.4
  25.0 2.1 %collective-permute-start.5 = (f32[256,128]{1,0:T(8,128)S(1)}, f32[256,128]{1,0:T(8,128)S(1)}, u32[]{:S(2)}, u32[]{:S(2)}) collective-permute-start(f32[256,128]{1,0:T(8,128)S(1)} %get-tuple-element.6), channel_id=1, source_target_pairs={{0,0},{8,1},{16,2},{24,3},{4,4},{12,5},{20,6},{28,7},{1,8},{9,9},{... | collective-permute-start | bytes 393224 | tf_op jit(solution)/shard_map/ppermute | solution.py:30
  27.1 0.0 collective-permute-done.7
  27.1 0.7 %collective-permute-done.8 = f32[128,128]{0,1:T(8,128)S(1)} collective-permute-done((f32[128,128]{0,1:T(8,128)S(1)}, f32[128,128]{0,1:T(8,128)S(1)}, u32[]{:S(2)}, u32[]{:S(2)}) %collective-permute-start.8) | collective-permute-done | bytes 65568 | tf_op jit(solution)/shard_map/ppermute | solution.py:27
  27.8 2.0 %collective-permute-done.9 = f32[128,128]{0,1:T(8,128)S(1)} collective-permute-done((f32[128,128]{0,1:T(8,128)S(1)}, f32[128,128]{0,1:T(8,128)S(1)}, u32[]{:S(2)}, u32[]{:S(2)}) %collective-permute-start.9) | collective-permute-done | bytes 65568 | tf_op jit(solution)/shard_map/ppermute | solution.py:27
  29.8 0.1 collective-permute-start.10
  29.9 0.0 collective-permute-done.4
  29.9 1.2 %collective-permute-done.10 = f32[128,128]{0,1:T(8,128)S(1)} collective-permute-done((f32[128,128]{0,1:T(8,128)S(1)}, f32[128,128]{0,1:T(8,128)S(1)}, u32[]{:S(2)}, u32[]{:S(2)}) %collective-permute-start.10) | collective-permute-done | bytes 65568 | tf_op jit(solution)/shard_map/ppermute | solution.py:21
  31.2 0.3 fusion.3
  31.4 0.0 copy-start.1
  31.4 7.9 %collective-permute-done.5 = f32[256,128]{1,0:T(8,128)S(1)} collective-permute-done((f32[256,128]{1,0:T(8,128)S(1)}, f32[256,128]{1,0:T(8,128)S(1)}, u32[]{:S(2)}, u32[]{:S(2)}) %collective-permute-start.5) | collective-permute-done | bytes 131104 | tf_op jit(solution)/shard_map/ppermute | solution.py:30
  39.3 0.6 %fusion.1 = f32[256,512]{1,0:T(8,128)S(1)} fusion(f32[512,128]{1,0:T(8,128)S(1)} %fusion.7, f32[256,128]{1,0:T(8,128)S(1)} %collective-permute-done.5, f32[256,128]{1,0:T(8,128)S(1)} %fusion.3), kind=kOutput, calls=%fused_computation.3 | convolution fusion | flops 201359360 | bytes 1048576 | tf_op jit(solution)/shard_map/dot_general | solution.py:33
  39.9 0.0 copy-done.1
  39.9 1.4 %fusion = f32[256,512]{1,0:T(8,128)} fusion(f32[256,512]{1,0:T(8,128)S(1)} %fusion.1, f32[256,128]{1,0:T(8,128)S(1)} %fusion.5, f32[512,128]{1,0:T(8,128)S(1)} %constant_dynamic-update-slice_fusion.2, bf16[256,512]{1,0:T(8,128)(2,1)S(1)} %copy-done.1), kind=kOutput, calls=%fused_computation.1 | convolution fusion | flops 201719808 | bytes 1703936 | tf_op jit(solution)/shard_map/dot_general | solution.py:33
  (9 shorter events, 0.2 us)
Async XLA Ops:
  0.0 4.9 %copy-start = (f32[128,128]{1,0:T(8,128)S(1)}, f32[128,128]{1,0:T(8,128)}, u32[]{:S(2)}) copy-start(f32[128,128]{1,0:T(8,128)} %param.5) | copy-start | bytes 196612
  0.0 9.3 %collective-permute-start.6 = (bf16[256,128]{1,0:T(8,128)(2,1)}, bf16[256,128]{1,0:T(8,128)(2,1)S(1)}, u32[]{:S(2)}, u32[]{:S(2)}) collective-permute-start(bf16[256,128]{1,0:T(8,128)(2,1)} %param.4), channel_id=1, source_target_pairs={{0,0},{8,1},{16,2},{24,3},{4,4},{12,5},{20,6},{28,7},{1,8},{9,9},{... | collective-permute-start | bytes 196616 | tf_op jit(solution)/shard_map/ppermute | solution.py:30
  4.8 0.8 %copy-start.2 = (bf16[256,128]{1,0:T(8,128)(2,1)S(1)}, bf16[256,128]{1,0:T(8,128)(2,1)}, u32[]{:S(2)}) copy-start(bf16[256,128]{1,0:T(8,128)(2,1)} %param.4) | copy-start | bytes 196612
  4.9 4.4 %collective-permute-start = (f32[256,128]{1,0:T(8,128)S(1)}, f32[256,128]{1,0:T(8,128)S(1)}, u32[]{:S(2)}, u32[]{:S(2)}) collective-permute-start(f32[256,128]{1,0:T(8,128)S(1)} %constant_dynamic-slice_fusion), channel_id=1, source_target_pairs={{0,4},{4,0},{8,12},{12,8},{16,20},{20,16},{24,28},{28,24},{1,5},{5... | collective-permute-start | bytes 393224 | tf_op jit(solution)/shard_map/ppermute | solution.py:21
  9.3 3.9 %collective-permute-start.11 = (bf16[256,128]{1,0:T(8,128)(2,1)S(1)}, bf16[256,128]{1,0:T(8,128)(2,1)S(1)}, u32[]{:S(2)}, u32[]{:S(2)}) collective-permute-start(bf16[256,128]{1,0:T(8,128)(2,1)S(1)} %collective-permute-done.6), channel_id=1, source_target_pairs={{0,4},{4,0},{8,12},{12,8},{16,20},{20,16},{24,28},{28,24},{1,5},{5... | collective-permute-start | bytes 196616 | tf_op jit(solution)/shard_map/ppermute | solution.py:21
  9.3 6.4 %collective-permute-start.1 = (f32[256,128]{1,0:T(8,128)S(1)}, f32[256,128]{1,0:T(8,128)S(1)}, u32[]{:S(2)}, u32[]{:S(2)}) collective-permute-start(f32[256,128]{1,0:T(8,128)S(1)} %dynamic-slice_add_fusion), channel_id=1, source_target_pairs={{0,8},{4,12},{8,0},{12,4},{16,24},{20,28},{24,16},{28,20},{1,9},{5... | collective-permute-start | bytes 393224 | tf_op jit(solution)/shard_map/ppermute | solution.py:24
  9.4 8.6 %collective-permute-start.2 = (f32[256,128]{1,0:T(8,128)S(1)}, f32[256,128]{1,0:T(8,128)S(1)}, u32[]{:S(2)}, u32[]{:S(2)}) collective-permute-start(f32[256,128]{1,0:T(8,128)S(1)} %dynamic-slice_add_fusion), channel_id=1, source_target_pairs={{0,16},{4,20},{8,24},{12,28},{16,0},{20,4},{24,8},{28,12},{1,17},{... | collective-permute-start | bytes 393224 | tf_op jit(solution)/shard_map/ppermute | solution.py:24
  11.8 8.1 %collective-permute-start.3 = (f32[256,128]{1,0:T(8,128)S(1)}, f32[256,128]{1,0:T(8,128)S(1)}, u32[]{:S(2)}, u32[]{:S(2)}) collective-permute-start(f32[256,128]{1,0:T(8,128)S(1)} %dynamic-slice_add_fusion), channel_id=1, source_target_pairs={{0,24},{4,28},{8,16},{12,20},{16,8},{20,12},{24,0},{28,4},{1,25},{... | collective-permute-start | bytes 393224 | tf_op jit(solution)/shard_map/ppermute | solution.py:24
  20.2 6.9 %collective-permute-start.7 = (f32[128,128]{0,1:T(8,128)S(1)}, f32[128,128]{0,1:T(8,128)S(1)}, u32[]{:S(2)}, u32[]{:S(2)}) collective-permute-start(f32[128,128]{0,1:T(8,128)S(1)} %convolution_bitcast_fusion), channel_id=1, source_target_pairs={{0,1},{1,0},{2,3},{3,2},{4,5},{5,4},{6,7},{7,6},{8,9},{9,8},{10,11... | collective-permute-start | bytes 196616 | tf_op jit(solution)/shard_map/ppermute | solution.py:27
  20.3 7.5 %collective-permute-start.8 = (f32[128,128]{0,1:T(8,128)S(1)}, f32[128,128]{0,1:T(8,128)S(1)}, u32[]{:S(2)}, u32[]{:S(2)}) collective-permute-start(f32[128,128]{0,1:T(8,128)S(1)} %convolution_bitcast_fusion), channel_id=1, source_target_pairs={{0,2},{1,3},{2,0},{3,1},{4,6},{5,7},{6,4},{7,5},{8,10},{9,11},{10,... | collective-permute-start | bytes 196616 | tf_op jit(solution)/shard_map/ppermute | solution.py:27
  23.8 6.1 %collective-permute-start.9 = (f32[128,128]{0,1:T(8,128)S(1)}, f32[128,128]{0,1:T(8,128)S(1)}, u32[]{:S(2)}, u32[]{:S(2)}) collective-permute-start(f32[128,128]{0,1:T(8,128)S(1)} %convolution_bitcast_fusion), channel_id=1, source_target_pairs={{0,3},{1,2},{2,1},{3,0},{4,7},{5,6},{6,5},{7,4},{8,11},{9,10},{10,... | collective-permute-start | bytes 196616 | tf_op jit(solution)/shard_map/ppermute | solution.py:27
  25.0 5.0 %collective-permute-start.4 = (f32[256,128]{1,0:T(8,128)S(1)}, f32[256,128]{1,0:T(8,128)S(1)}, u32[]{:S(2)}, u32[]{:S(2)}) collective-permute-start(f32[256,128]{1,0:T(8,128)S(1)} %get-tuple-element.6), channel_id=1, source_target_pairs={{0,4},{4,0},{8,12},{12,8},{16,20},{20,16},{24,28},{28,24},{1,5},{5... | collective-permute-start | bytes 393224 | tf_op jit(solution)/shard_map/ppermute | solution.py:21
  25.0 14.3 %collective-permute-start.5 = (f32[256,128]{1,0:T(8,128)S(1)}, f32[256,128]{1,0:T(8,128)S(1)}, u32[]{:S(2)}, u32[]{:S(2)}) collective-permute-start(f32[256,128]{1,0:T(8,128)S(1)} %get-tuple-element.6), channel_id=1, source_target_pairs={{0,0},{8,1},{16,2},{24,3},{4,4},{12,5},{20,6},{28,7},{1,8},{9,9},{... | collective-permute-start | bytes 393224 | tf_op jit(solution)/shard_map/ppermute | solution.py:30
  29.8 1.3 %collective-permute-start.10 = (f32[128,128]{0,1:T(8,128)S(1)}, f32[128,128]{0,1:T(8,128)S(1)}, u32[]{:S(2)}, u32[]{:S(2)}) collective-permute-start(f32[128,128]{0,1:T(8,128)S(1)} %add_add_fusion.1), channel_id=1, source_target_pairs={{0,4},{4,0},{8,12},{12,8},{16,20},{20,16},{24,28},{28,24},{1,5},{5... | collective-permute-start | bytes 196616 | tf_op jit(solution)/shard_map/ppermute | solution.py:21
  31.4 8.5 %copy-start.1 = (bf16[256,512]{1,0:T(8,128)(2,1)S(1)}, bf16[256,512]{1,0:T(8,128)(2,1)}, u32[]{:S(2)}) copy-start(bf16[256,512]{1,0:T(8,128)(2,1)} %param.3) | copy-start | bytes 786436

commit v2 on v1

v2 whole, which is shorter than its diff:
```python
import jax
import jax.numpy as jnp
from jax import lax
from jax.sharding import PartitionSpec as P

TOP = 30719.0
LEAST = -100.0
TILE = 16


def scale_of(ratio, exponent):
    return ratio.astype(jnp.float32) * jnp.exp2(exponent.astype(jnp.float32))


def encode(x):
    top = jnp.max(jnp.abs(x), axis=0, keepdims=True)
    exponent = jnp.maximum(jnp.ceil(jnp.log2(top)), LEAST).astype(jnp.float16)
    ratio = jnp.minimum(top * jnp.exp2(-exponent.astype(jnp.float32)) * 1.001, 2.0).astype(jnp.float16)
    ratio = jnp.maximum(ratio, jnp.float16(0.25))
    step = TOP / scale_of(ratio, exponent)
    code = jnp.minimum(jnp.abs(x) * step + 0.5, TOP).astype(jnp.int32)
    power = lax.shift_left(jnp.int32(1), lax.shift_right_logical(code, 10)).astype(jnp.float32)
    size = (jnp.bitwise_and(code, 1023) + 1024).astype(jnp.float32) * power * 2.0**-24
    coded = jnp.where(x < 0, -size, size).astype(jnp.float16)
    width = x.shape[1]
    tail = jnp.concatenate(
        [jnp.broadcast_to(ratio, (TILE // 2, width)), jnp.broadcast_to(exponent, (TILE // 2, width))], 0
    )
    return jnp.concatenate([coded, tail], 0)


def decode(message):
    rows = message.shape[0] - TILE
    y = message[:rows].astype(jnp.float32)
    size = jnp.abs(y) * 2.0**14
    order = 31 - lax.clz(size.astype(jnp.int32))
    inverse = lax.shift_left(jnp.int32(1), 30 - order).astype(jnp.float32) * 2.0**-30
    code = 1024.0 * (order.astype(jnp.float32) + (size * inverse - 1.0))
    step = scale_of(message[rows : rows + 1], message[rows + TILE // 2 : rows + TILE // 2 + 1]) * (1.0 / TOP)
    return jnp.where(y < 0, -code, code) * step


def solution(mesh):
    n_row, n_col = mesh.shape["row"], mesh.shape["col"]
    q = n_row // n_col
    highest = lax.Precision.HIGHEST

    def member(x, s):
        return lax.ppermute(x, "row", [(r, r ^ s) for r in range(n_row)])

    def group(x, s):
        return lax.ppermute(x, "row", [(r, r ^ (s * q)) for r in range(n_row)])

    def plane(x, s):
        return lax.ppermute(x, "col", [(c, c ^ s) for c in range(n_col)])

    def dot(a, b, dims):
        return lax.dot_general(a, b, (dims, ((), ())), precision=highest, preferred_element_type=jnp.float32)

    def placed(pieces, me):
        rows = pieces[0].shape[0]
        whole = jnp.zeros((len(pieces) * rows, pieces[0].shape[1]), pieces[0].dtype)
        for s, piece in enumerate(pieces):
            whole = lax.dynamic_update_slice_in_dim(whole, piece, (me ^ s) * rows, 0)
        return whole

    def shards(covariance, reflectors, factor):
        rows = covariance.shape[0]
        row, c = lax.axis_index("row"), lax.axis_index("col")
        k, h = lax.div(row, q), lax.rem(row, q)
        back = lax.dot_general(
            covariance, reflectors, (((0,), (0,)), ((), ())), preferred_element_type=jnp.float32
        )
        piece = lax.dynamic_slice_in_dim(back, h * rows, rows, 0)
        for s in range(1, q):
            piece = piece + member(lax.dynamic_slice_in_dim(back, (h ^ s) * rows, rows, 0), s)
        message = encode(piece)
        others = [group(message, s) for s in range(1, n_col)]
        held, _ = lax.optimization_barrier((reflectors, message))
        v_mates = placed([held] + [group(held, s) for s in range(1, n_col)], k)
        total = piece
        for other in others:
            total = total + decode(other)
        message = encode(total)
        p_mates = placed([total] + [decode(plane(message, s)) for s in range(1, n_col)], c)
        p_cols = placed([total] + [member(total, s) for s in range(1, q)], h)
        v_piece = lax.dynamic_slice_in_dim(v_mates, c * rows, rows, 0)
        v_cols = placed([v_piece] + [member(v_piece, s) for s in range(1, q)], h)
        gram = dot(v_mates.astype(jnp.float32), p_mates, ((0,), (0,)))
        whole = gram
        for s in range(1, q):
            whole = whole + member(gram, s)
        p_rows = lax.dynamic_slice_in_dim(p_mates, k * rows, rows, 0)
        y_rows = dot(reflectors.astype(jnp.float32), factor, ((1,), (1,)))
        y_cols = dot(v_cols.astype(jnp.float32), factor, ((1,), (1,)))
        first = covariance.astype(jnp.float32) - dot(y_rows, p_cols, ((1,), (1,)))
        x_rows = p_rows - dot(y_rows, whole, ((1,), (0,)))
        return first - dot(x_rows, y_cols, ((1,), (1,)))

    in_specs = (P("row", "col"), P("row", None), P())
    return jax.shard_map(shards, mesh=mesh, in_specs=in_specs, out_specs=P("row", "col"), check_vma=False)
```

time: 41.6 us -> 33.9 us (0.81)
  the two profiles are of different devices: /device:TPU:2 before, /device:TPU:0 now
where the time goes in v2:
time: 33.9 us; the launch traced here: 33.7 us
  starting transfers between devices  15.1 us (45%)
  waiting for transfers between devices  11.9 us (35%)
  matrix products  4.45 us (13%)
  other arithmetic  0.98 us (3%)
  local copies, waits for them, and re-layouts  0.96 us (3%)
    ppermute x6, starting transfers between devices, group(): return lax.ppermute(x, 'row', [(r, r ^ s * q) for r in range(n_row)])  9.96 us
    ppermute x3, waiting for transfers between devices, plane(): return lax.ppermute(x, 'col', [(c, c ^ s) for c in range(n_col)])  5.6 us
    ppermute x6, waiting for transfers between devices, group(): return lax.ppermute(x, 'row', [(r, r ^ s * q) for r in range(n_row)])  4.69 us
    ppermute x3, starting transfers between devices, plane(): return lax.ppermute(x, 'col', [(c, c ^ s) for c in range(n_col)])  4.45 us
    dot_general x6, matrix products, dot(): lax.dot_general(a, b, (dims, ((), ())), precision=highest, preferred_elem...  3.21 us
    ppermute x4, waiting for transfers between devices, member(): return lax.ppermute(x, 'row', [(r, r ^ s) for r in range(n_row)])  1.64 us
    dot_general x1, matrix products, shards(): lax.dot_general(covariance, reflectors, (((0,), (0,)), ((), ())), preferr...  1.24 us
  transfers between devices with their start and end apart: 13, of which 6 were waited for; matrix products, arithmetic and copies ran while one was open for 6% of the time, Pallas kernels for 0%

profile of v2, /device:TPU:0, one launch (start us, length us, event | category | flops | bytes accessed | tf_op | source)
XLA Modules:
  0.0 33.7 jit_solution(16529783527459458797)
XLA Ops:
  0.0 0.0 copy-start
  0.0 1.2 %fusion.114 = f32[512,128]{1,0:T(8,128)S(1)} fusion(bf16[256,512]{1,0:T(8,128)(2,1)} %param.3, bf16[256,128]{1,0:T(8,128)(2,1)} %param.4), kind=kOutput, calls=%fused_computation.175 | convolution fusion | flops 33554432 | bytes 589824 | tf_op jit(solution)/shard_map/dot_general | solution.py:71
  1.3 0.0 copy-start.2
  1.3 0.5 %collective-permute-start = (f32[256,128]{1,0:T(8,128)S(1)}, f32[256,128]{1,0:T(8,128)S(1)}, u32[]{:S(2)}, u32[]{:S(2)}) collective-permute-start(f32[256,128]{1,0:T(8,128)S(1)} %constant_dynamic-slice_fusion.1), channel_id=1, source_target_pairs={{0,4},{4,0},{8,12},{12,8},{16,20},{20,16},{24,28},{28,24},{1,5},{5... | collective-permute-start | bytes 393224 | tf_op jit(solution)/shard_map/ppermute | solution.py:49
  1.8 0.0 copy-done
  1.8 0.3 copy-done.2
  2.1 0.2 fusion.113
  2.4 0.4 %collective-permute-done = f32[256,128]{1,0:T(8,128)S(1)} collective-permute-done((f32[256,128]{1,0:T(8,128)S(1)}, f32[256,128]{1,0:T(8,128)S(1)}, u32[]{:S(2)}, u32[]{:S(2)}) %collective-permute-start) | collective-permute-done | bytes 131104 | tf_op jit(solution)/shard_map/ppermute | solution.py:49
  2.9 0.1 fusion.91
  3.0 3.9 %collective-permute-start.3 = (f16[272,128]{1,0:T(8,128)(2,1)S(1)}, f16[272,128]{1,0:T(8,128)(2,1)S(1)}, u32[]{:S(2)}, u32[]{:S(2)}) collective-permute-start(f16[272,128]{1,0:T(8,128)(2,1)S(1)} %pad_maximum_fusion), channel_id=1, source_target_pairs={{0,24},{4,28},{8,16},{12,20},{16,8},{20,12},{24,0},{28,4},{1,25},{... | collective-permute-start | bytes 208904 | tf_op jit(solution)/shard_map/ppermute | solution.py:52
  6.9 0.5 %collective-permute-start.2 = (f16[272,128]{1,0:T(8,128)(2,1)S(1)}, f16[272,128]{1,0:T(8,128)(2,1)S(1)}, u32[]{:S(2)}, u32[]{:S(2)}) collective-permute-start(f16[272,128]{1,0:T(8,128)(2,1)S(1)} %pad_maximum_fusion), channel_id=1, source_target_pairs={{0,16},{4,20},{8,24},{12,28},{16,0},{20,4},{24,8},{28,12},{1,17},{... | collective-permute-start | bytes 208904 | tf_op jit(solution)/shard_map/ppermute | solution.py:52
  7.4 0.1 collective-permute-start.1
  7.5 1.9 %collective-permute-start.8 = (bf16[256,128]{1,0:T(8,128)(2,1)S(1)}, bf16[256,128]{1,0:T(8,128)(2,1)S(1)}, u32[]{:S(2)}, u32[]{:S(2)}) collective-permute-start(bf16[256,128]{1,0:T(8,128)(2,1)S(1)} %copy-done.2), channel_id=1, source_target_pairs={{0,8},{4,12},{8,0},{12,4},{16,24},{20,28},{24,16},{28,20},{1,9},{5... | collective-permute-start | bytes 196616 | tf_op jit(solution)/shard_map/ppermute | solution.py:52
  9.4 1.5 %collective-permute-start.9 = (bf16[256,128]{1,0:T(8,128)(2,1)S(1)}, bf16[256,128]{1,0:T(8,128)(2,1)S(1)}, u32[]{:S(2)}, u32[]{:S(2)}) collective-permute-start(bf16[256,128]{1,0:T(8,128)(2,1)S(1)} %copy-done.2), channel_id=1, source_target_pairs={{0,16},{4,20},{8,24},{12,28},{16,0},{20,4},{24,8},{28,12},{1,17},{... | collective-permute-start | bytes 196616 | tf_op jit(solution)/shard_map/ppermute | solution.py:52
  11.0 1.6 %collective-permute-done.8 = bf16[256,128]{1,0:T(8,128)(2,1)S(1)} collective-permute-done((bf16[256,128]{1,0:T(8,128)(2,1)S(1)}, bf16[256,128]{1,0:T(8,128)(2,1)S(1)}, u32[]{:S(2)}, u32[]{:S(2)}) %collective-permute-start.8) | collective-permute-done | bytes 65568 | tf_op jit(solution)/shard_map/ppermute | solution.py:52
  12.6 2.0 %collective-permute-start.10 = (bf16[256,128]{1,0:T(8,128)(2,1)S(1)}, bf16[256,128]{1,0:T(8,128)(2,1)S(1)}, u32[]{:S(2)}, u32[]{:S(2)}) collective-permute-start(bf16[256,128]{1,0:T(8,128)(2,1)S(1)} %copy-done.2), channel_id=1, source_target_pairs={{0,24},{4,28},{8,16},{12,20},{16,8},{20,12},{24,0},{28,4},{1,25},{... | collective-permute-start | bytes 196616 | tf_op jit(solution)/shard_map/ppermute | solution.py:52
  14.7 0.0 collective-permute-done.9
  14.7 3.1 %collective-permute-done.10 = bf16[256,128]{1,0:T(8,128)(2,1)S(1)} collective-permute-done((bf16[256,128]{1,0:T(8,128)(2,1)S(1)}, bf16[256,128]{1,0:T(8,128)(2,1)S(1)}, u32[]{:S(2)}, u32[]{:S(2)}) %collective-permute-start.10) | collective-permute-done | bytes 65568 | tf_op jit(solution)/shard_map/ppermute | solution.py:52
  17.8 0.1 collective-permute-start.12
  17.9 0.0 collective-permute-done.3
  17.9 0.0 collective-permute-done.2
  18.0 0.0 collective-permute-done.1
  18.0 0.3 constant_dynamic-update-slice_fusion.8
  18.4 0.1 fusion.92
  18.6 1.6 %collective-permute-start.5 = (f16[272,128]{1,0:T(8,128)(2,1)S(1)}, f16[272,128]{1,0:T(8,128)(2,1)S(1)}, u32[]{:S(2)}, u32[]{:S(2)}) collective-permute-start(f16[272,128]{1,0:T(8,128)(2,1)S(1)} %pad_maximum_fusion.1), channel_id=1, source_target_pairs={{0,1},{1,0},{2,3},{3,2},{4,5},{5,4},{6,7},{7,6},{8,9},{9,8},{10,11... | collective-permute-start | bytes 208904 | tf_op jit(solution)/shard_map/ppermute | solution.py:55
  20.2 2.6 %collective-permute-start.6 = (f16[272,128]{1,0:T(8,128)(2,1)S(1)}, f16[272,128]{1,0:T(8,128)(2,1)S(1)}, u32[]{:S(2)}, u32[]{:S(2)}) collective-permute-start(f16[272,128]{1,0:T(8,128)(2,1)S(1)} %pad_maximum_fusion.1), channel_id=1, source_target_pairs={{0,2},{1,3},{2,0},{3,1},{4,6},{5,7},{6,4},{7,5},{8,10},{9,11},{10,... | collective-permute-start | bytes 208904 | tf_op jit(solution)/shard_map/ppermute | solution.py:55
  22.8 0.2 collective-permute-start.7
  23.0 0.0 collective-permute-start.4
  23.0 0.0 collective-permute-done.12
  23.0 0.3 fusion.116
  23.3 0.0 collective-permute-done.5
  23.4 4.7 %collective-permute-done.6 = f16[272,128]{1,0:T(8,128)(2,1)S(1)} collective-permute-done((f16[272,128]{1,0:T(8,128)(2,1)S(1)}, f16[272,128]{1,0:T(8,128)(2,1)S(1)}, u32[]{:S(2)}, u32[]{:S(2)}) %collective-permute-start.6) | collective-permute-done | bytes 69664 | tf_op jit(solution)/shard_map/ppermute | solution.py:55
  28.1 0.9 %collective-permute-done.7 = f16[272,128]{1,0:T(8,128)(2,1)S(1)} collective-permute-done((f16[272,128]{1,0:T(8,128)(2,1)S(1)}, f16[272,128]{1,0:T(8,128)(2,1)S(1)}, u32[]{:S(2)}, u32[]{:S(2)}) %collective-permute-start.7) | collective-permute-done | bytes 69664 | tf_op jit(solution)/shard_map/ppermute | solution.py:55
  29.0 0.1 fusion.60
  29.1 0.1 fusion.75
  29.2 0.1 fusion.90
  29.3 0.4 %fusion.115 = f32[128,128]{1,0:T(8,128)S(1)} fusion(bf16[1024,128]{1,0:T(8,128)(2,1)S(1)} %constant_dynamic-update-slice_fusion.2, f32[1024,128]{1,0:T(8,128)S(1)} %fusion.90), kind=kOutput, calls=%fused_computation.176 | convolution fusion | flops 201326592 | bytes 851968 | tf_op jit(solution)/shard_map/dot_general | solution.py:58
  29.7 0.1 collective-permute-start.11
  29.8 0.0 collective-permute-done.4
  29.8 1.2 %collective-permute-done.11 = f32[128,128]{1,0:T(8,128)S(1)} collective-permute-done((f32[128,128]{1,0:T(8,128)S(1)}, f32[128,128]{1,0:T(8,128)S(1)}, u32[]{:S(2)}, u32[]{:S(2)}) %collective-permute-start.11) | collective-permute-done | bytes 65568 | tf_op jit(solution)/shard_map/ppermute | solution.py:49
  31.1 0.3 convolution_subtract_fusion.1
  31.3 0.0 copy-start.1
  31.3 0.6 %fusion.117 = f32[256,512]{1,0:T(8,128)S(1)} fusion(f32[256,128]{1,0:T(8,128)S(1)} %convolution_subtract_fusion.1, f32[512,128]{1,0:T(8,128)S(1)} %fusion.116), kind=kOutput, calls=%fused_computation.178 | convolution fusion | flops 201326592 | bytes 917504 | tf_op jit(solution)/shard_map/dot_general | solution.py:58
  31.9 0.4 %copy-done.1 = bf16[256,512]{1,0:T(8,128)(2,1)S(1)} copy-done((bf16[256,512]{1,0:T(8,128)(2,1)S(1)}, bf16[256,512]{1,0:T(8,128)(2,1)}, u32[]{:S(2)}) %copy-start.1) | copy-done | bytes 262168
  32.3 1.4 %fusion = f32[256,512]{1,0:T(8,128)} fusion(f32[256,512]{1,0:T(8,128)S(1)} %fusion.117, f32[256,128]{1,0:T(8,128)S(1)} %fusion.113, f32[512,128]{1,0:T(8,128)S(1)} %constant_dynamic-update-slice_fusion.7, bf16[256,512]{1,0:T(8,128)(2,1)S(1)} %copy-done.1), kind=kOutput, calls=%fused_computation.1 | convolution fusion | flops 201719808 | bytes 1703936 | tf_op jit(solution)/shard_map/dot_general | solution.py:58
  (28 shorter events, 0.5 us)
Async XLA Ops:
  0.0 1.8 %copy-start = (f32[128,128]{1,0:T(8,128)S(1)}, f32[128,128]{1,0:T(8,128)}, u32[]{:S(2)}) copy-start(f32[128,128]{1,0:T(8,128)} %param.5) | copy-start | bytes 196612
  1.3 0.8 %copy-start.2 = (bf16[256,128]{1,0:T(8,128)(2,1)S(1)}, bf16[256,128]{1,0:T(8,128)(2,1)}, u32[]{:S(2)}) copy-start(bf16[256,128]{1,0:T(8,128)(2,1)} %param.4) | copy-start | bytes 196612
  1.3 1.5 %collective-permute-start = (f32[256,128]{1,0:T(8,128)S(1)}, f32[256,128]{1,0:T(8,128)S(1)}, u32[]{:S(2)}, u32[]{:S(2)}) collective-permute-start(f32[256,128]{1,0:T(8,128)S(1)} %constant_dynamic-slice_fusion.1), channel_id=1, source_target_pairs={{0,4},{4,0},{8,12},{12,8},{16,20},{20,16},{24,28},{28,24},{1,5},{5... | collective-permute-start | bytes 393224 | tf_op jit(solution)/shard_map/ppermute | solution.py:49
  3.0 14.9 %collective-permute-start.3 = (f16[272,128]{1,0:T(8,128)(2,1)S(1)}, f16[272,128]{1,0:T(8,128)(2,1)S(1)}, u32[]{:S(2)}, u32[]{:S(2)}) collective-permute-start(f16[272,128]{1,0:T(8,128)(2,1)S(1)} %pad_maximum_fusion), channel_id=1, source_target_pairs={{0,24},{4,28},{8,16},{12,20},{16,8},{20,12},{24,0},{28,4},{1,25},{... | collective-permute-start | bytes 208904 | tf_op jit(solution)/shard_map/ppermute | solution.py:52
  6.9 11.1 %collective-permute-start.2 = (f16[272,128]{1,0:T(8,128)(2,1)S(1)}, f16[272,128]{1,0:T(8,128)(2,1)S(1)}, u32[]{:S(2)}, u32[]{:S(2)}) collective-permute-start(f16[272,128]{1,0:T(8,128)(2,1)S(1)} %pad_maximum_fusion), channel_id=1, source_target_pairs={{0,16},{4,20},{8,24},{12,28},{16,0},{20,4},{24,8},{28,12},{1,17},{... | collective-permute-start | bytes 208904 | tf_op jit(solution)/shard_map/ppermute | solution.py:52
  7.4 10.6 %collective-permute-start.1 = (f16[272,128]{1,0:T(8,128)(2,1)S(1)}, f16[272,128]{1,0:T(8,128)(2,1)S(1)}, u32[]{:S(2)}, u32[]{:S(2)}) collective-permute-start(f16[272,128]{1,0:T(8,128)(2,1)S(1)} %pad_maximum_fusion), channel_id=1, source_target_pairs={{0,8},{4,12},{8,0},{12,4},{16,24},{20,28},{24,16},{28,20},{1,9},{5... | collective-permute-start | bytes 208904 | tf_op jit(solution)/shard_map/ppermute | solution.py:52
  7.5 5.1 %collective-permute-start.8 = (bf16[256,128]{1,0:T(8,128)(2,1)S(1)}, bf16[256,128]{1,0:T(8,128)(2,1)S(1)}, u32[]{:S(2)}, u32[]{:S(2)}) collective-permute-start(bf16[256,128]{1,0:T(8,128)(2,1)S(1)} %copy-done.2), channel_id=1, source_target_pairs={{0,8},{4,12},{8,0},{12,4},{16,24},{20,28},{24,16},{28,20},{1,9},{5... | collective-permute-start | bytes 196616 | tf_op jit(solution)/shard_map/ppermute | solution.py:52
  9.4 5.2 %collective-permute-start.9 = (bf16[256,128]{1,0:T(8,128)(2,1)S(1)}, bf16[256,128]{1,0:T(8,128)(2,1)S(1)}, u32[]{:S(2)}, u32[]{:S(2)}) collective-permute-start(bf16[256,128]{1,0:T(8,128)(2,1)S(1)} %copy-done.2), channel_id=1, source_target_pairs={{0,16},{4,20},{8,24},{12,28},{16,0},{20,4},{24,8},{28,12},{1,17},{... | collective-permute-start | bytes 196616 | tf_op jit(solution)/shard_map/ppermute | solution.py:52
  12.6 5.2 %collective-permute-start.10 = (bf16[256,128]{1,0:T(8,128)(2,1)S(1)}, bf16[256,128]{1,0:T(8,128)(2,1)S(1)}, u32[]{:S(2)}, u32[]{:S(2)}) collective-permute-start(bf16[256,128]{1,0:T(8,128)(2,1)S(1)} %copy-done.2), channel_id=1, source_target_pairs={{0,24},{4,28},{8,16},{12,20},{16,8},{20,12},{24,0},{28,4},{1,25},{... | collective-permute-start | bytes 196616 | tf_op jit(solution)/shard_map/ppermute | solution.py:52
  17.8 5.2 %collective-permute-start.12 = (bf16[256,128]{1,0:T(8,128)(2,1)S(1)}, bf16[256,128]{1,0:T(8,128)(2,1)S(1)}, u32[]{:S(2)}, u32[]{:S(2)}) collective-permute-start(bf16[256,128]{1,0:T(8,128)(2,1)S(1)} %get-tuple-element.10), channel_id=1, source_target_pairs={{0,4},{4,0},{8,12},{12,8},{16,20},{20,16},{24,28},{28,24},{1,5},{5... | collective-permute-start | bytes 196616 | tf_op jit(solution)/shard_map/ppermute | solution.py:49
  18.6 4.8 %collective-permute-start.5 = (f16[272,128]{1,0:T(8,128)(2,1)S(1)}, f16[272,128]{1,0:T(8,128)(2,1)S(1)}, u32[]{:S(2)}, u32[]{:S(2)}) collective-permute-start(f16[272,128]{1,0:T(8,128)(2,1)S(1)} %pad_maximum_fusion.1), channel_id=1, source_target_pairs={{0,1},{1,0},{2,3},{3,2},{4,5},{5,4},{6,7},{7,6},{8,9},{9,8},{10,11... | collective-permute-start | bytes 208904 | tf_op jit(solution)/shard_map/ppermute | solution.py:55
  20.2 7.9 %collective-permute-start.6 = (f16[272,128]{1,0:T(8,128)(2,1)S(1)}, f16[272,128]{1,0:T(8,128)(2,1)S(1)}, u32[]{:S(2)}, u32[]{:S(2)}) collective-permute-start(f16[272,128]{1,0:T(8,128)(2,1)S(1)} %pad_maximum_fusion.1), channel_id=1, source_target_pairs={{0,2},{1,3},{2,0},{3,1},{4,6},{5,7},{6,4},{7,5},{8,10},{9,11},{10,... | collective-permute-start | bytes 208904 | tf_op jit(solution)/shard_map/ppermute | solution.py:55
  22.8 6.2 %collective-permute-start.7 = (f16[272,128]{1,0:T(8,128)(2,1)S(1)}, f16[272,128]{1,0:T(8,128)(2,1)S(1)}, u32[]{:S(2)}, u32[]{:S(2)}) collective-permute-start(f16[272,128]{1,0:T(8,128)(2,1)S(1)} %pad_maximum_fusion.1), channel_id=1, source_target_pairs={{0,3},{1,2},{2,1},{3,0},{4,7},{5,6},{6,5},{7,4},{8,11},{9,10},{10,... | collective-permute-start | bytes 208904 | tf_op jit(solution)/shard_map/ppermute | solution.py:55
  23.0 6.8 %collective-permute-start.4 = (f32[256,128]{1,0:T(8,128)S(1)}, f32[256,128]{1,0:T(8,128)S(1)}, u32[]{:S(2)}, u32[]{:S(2)}) collective-permute-start(f32[256,128]{1,0:T(8,128)S(1)} %get-tuple-element.8), channel_id=1, source_target_pairs={{0,4},{4,0},{8,12},{12,8},{16,20},{20,16},{24,28},{28,24},{1,5},{5... | collective-permute-start | bytes 393224 | tf_op jit(solution)/shard_map/ppermute | solution.py:49
  29.7 1.3 %collective-permute-start.11 = (f32[128,128]{1,0:T(8,128)S(1)}, f32[128,128]{1,0:T(8,128)S(1)}, u32[]{:S(2)}, u32[]{:S(2)}) collective-permute-start(f32[128,128]{1,0:T(8,128)S(1)} %fusion.115), channel_id=1, source_target_pairs={{0,4},{4,0},{8,12},{12,8},{16,20},{20,16},{24,28},{28,24},{1,5},{5... | collective-permute-start | bytes 196616 | tf_op jit(solution)/shard_map/ppermute | solution.py:49
  31.3 1.0 %copy-start.1 = (bf16[256,512]{1,0:T(8,128)(2,1)S(1)}, bf16[256,512]{1,0:T(8,128)(2,1)}, u32[]{:S(2)}) copy-start(bf16[256,512]{1,0:T(8,128)(2,1)} %param.3) | copy-start | bytes 786436

commit v3 on v2

--- a/solution.py
+++ b/solution.py
@@ -14,9 +14,9 @@
 
 def encode(x):
     top = jnp.max(jnp.abs(x), axis=0, keepdims=True)
-    exponent = jnp.maximum(jnp.ceil(jnp.log2(top)), LEAST).astype(jnp.float16)
-    ratio = jnp.minimum(top * jnp.exp2(-exponent.astype(jnp.float32)) * 1.001, 2.0).astype(jnp.float16)
-    ratio = jnp.maximum(ratio, jnp.float16(0.25))
+    exponent = lax.reduce_precision(jnp.maximum(jnp.ceil(jnp.log2(top)), LEAST), 5, 10).astype(jnp.float16)
+    ratio = jnp.clip(top * jnp.exp2(-exponent.astype(jnp.float32)) * 1.001, 0.25, 2.0)
+    ratio = lax.reduce_precision(ratio, 5, 10).astype(jnp.float16)
     step = TOP / scale_of(ratio, exponent)
     code = jnp.minimum(jnp.abs(x) * step + 0.5, TOP).astype(jnp.int32)
     power = lax.shift_left(jnp.int32(1), lax.shift_right_logical(code, 10)).astype(jnp.float32)
@@ -76,14 +76,22 @@
             piece = piece + member(lax.dynamic_slice_in_dim(back, (h ^ s) * rows, rows, 0), s)
         message = encode(piece)
         others = [group(message, s) for s in range(1, n_col)]
-        held, _ = lax.optimization_barrier((reflectors, message))
-        v_mates = placed([held] + [group(held, s) for s in range(1, n_col)], k)
+        pieces, _ = lax.optimization_barrier((reflectors, message))
+        pieces = jnp.concatenate([pieces, group(pieces, 1)], 0)
         total = piece
         for other in others:
             total = total + decode(other)
         message = encode(total)
-        p_mates = placed([total] + [decode(plane(message, s)) for s in range(1, n_col)], c)
-        p_cols = placed([total] + [member(total, s) for s in range(1, q)], h)
+        step = 2
+        while step < n_col:
+            held, _ = lax.optimization_barrier((pieces, message))
+            pieces = jnp.concatenate([pieces, group(held, step)], 0)
+            step *= 2
+        v_mates = placed(jnp.split(pieces, n_col, 0), k)
+        mates = [plane(message, s) for s in range(1, n_col)]
+        held, _ = lax.optimization_barrier((total, mates[0]))
+        p_cols = placed([total] + [member(held, s) for s in range(1, q)], h)
+        p_mates = placed([total] + [decode(mate) for mate in mates], c)
         v_piece = lax.dynamic_slice_in_dim(v_mates, c * rows, rows, 0)
         v_cols = placed([v_piece] + [member(v_piece, s) for s in range(1, q)], h)
         gram = dot(v_mates.astype(jnp.float32), p_mates, ((0,), (0,)))

time: 33.9 us -> 29.6 us (0.87)
  waiting for transfers between devices: 11.9 us -> 8.63 us
  starting transfers between devices: 15.1 us -> 13.5 us
  local copies, waits for them, and re-layouts: 0.96 us -> 1.51 us
    ppermute x6 -> x5, starting transfers between devices: 9.96 us -> 7.79 us  [group(): return lax.ppermute(x, 'row', [(r, r ^ s * q) for r in range(n_row)])]
    ppermute x6 -> x5, waiting for transfers between devices: 4.69 us -> 3.13 us  [group(): return lax.ppermute(x, 'row', [(r, r ^ s * q) for r in range(n_row)])]
    ppermute x3, waiting for transfers between devices: 5.6 us -> 4.47 us  [plane(): return lax.ppermute(x, 'col', [(c, c ^ s) for c in range(n_col)])]
    ppermute x4, waiting for transfers between devices: 1.64 us -> 1.03 us  [member(): return lax.ppermute(x, 'row', [(r, r ^ s) for r in range(n_row)])]
    unnamed x6, local copies, waits for them, and re-layouts: 0.68 us -> 1.23 us
    ppermute x4, starting transfers between devices: 0.66 us -> 1.15 us  [member(): return lax.ppermute(x, 'row', [(r, r ^ s) for r in range(n_row)])]
  transfers between devices with their start and end apart: 13 -> 12, of which waited for: 6 -> 6; matrix products, arithmetic and copies ran while one was open for 6% -> 8% of each run, Pallas kernels for 0% -> 0%
where the time goes in v3:
time: 29.6 us; the launch traced here: 29.4 us
  starting transfers between devices  13.5 us (46%)
  waiting for transfers between devices  8.63 us (29%)
  matrix products  4.45 us (15%)
  local copies, waits for them, and re-layouts  1.51 us (5%)
  other arithmetic  1.02 us (3%)
    ppermute x5, starting transfers between devices, group(): return lax.ppermute(x, 'row', [(r, r ^ s * q) for r in range(n_row)])  7.79 us
    ppermute x3, starting transfers between devices, plane(): return lax.ppermute(x, 'col', [(c, c ^ s) for c in range(n_col)])  4.52 us
    ppermute x3, waiting for transfers between devices, plane(): return lax.ppermute(x, 'col', [(c, c ^ s) for c in range(n_col)])  4.47 us
    dot_general x6, matrix products, dot(): lax.dot_general(a, b, (dims, ((), ())), precision=highest, preferred_elem...  3.22 us
    ppermute x5, waiting for transfers between devices, group(): return lax.ppermute(x, 'row', [(r, r ^ s * q) for r in range(n_row)])  3.13 us
    dot_general x1, matrix products, shards(): lax.dot_general(covariance, reflectors, (((0,), (0,)), ((), ())), preferr...  1.24 us
    unnamed x6, local copies, waits for them, and re-layouts  1.23 us
    ppermute x4, starting transfers between devices, member(): return lax.ppermute(x, 'row', [(r, r ^ s) for r in range(n_row)])  1.15 us
  transfers between devices with their start and end apart: 12, of which 6 were waited for; matrix products, arithmetic and copies ran while one was open for 8% of the time, Pallas kernels for 0%

profile of v3, /device:TPU:0, one launch (start us, length us, event | category | flops | bytes accessed | tf_op | source)
XLA Modules:
  0.0 29.4 jit_solution(17295932865345239089)
XLA Ops:
  0.0 0.0 copy-start
  0.0 1.2 %fusion.114 = f32[512,128]{1,0:T(8,128)S(1)} fusion(bf16[256,512]{1,0:T(8,128)(2,1)} %param.3, bf16[256,128]{1,0:T(8,128)(2,1)} %param.4), kind=kOutput, calls=%fused_computation.176 | convolution fusion | flops 33554432 | bytes 589824 | tf_op jit(solution)/shard_map/dot_general | solution.py:71
  1.3 0.0 copy-start.1
  1.3 0.5 %collective-permute-start = (f32[256,128]{1,0:T(8,128)S(1)}, f32[256,128]{1,0:T(8,128)S(1)}, u32[]{:S(2)}, u32[]{:S(2)}) collective-permute-start(f32[256,128]{1,0:T(8,128)S(1)} %constant_dynamic-slice_fusion.1), channel_id=1, source_target_pairs={{0,4},{4,0},{8,12},{12,8},{16,20},{20,16},{24,28},{28,24},{1,5},{5... | collective-permute-start | bytes 393224 | tf_op jit(solution)/shard_map/ppermute | solution.py:49
  1.8 0.0 copy-done
  1.8 0.3 %copy-done.1 = bf16[256,128]{1,0:T(8,128)(2,1)S(1)} copy-done((bf16[256,128]{1,0:T(8,128)(2,1)S(1)}, bf16[256,128]{1,0:T(8,128)(2,1)}, u32[]{:S(2)}) %copy-start.1) | copy-done | bytes 65560
  2.1 0.2 fusion.113
  2.4 0.4 %collective-permute-done = f32[256,128]{1,0:T(8,128)S(1)} collective-permute-done((f32[256,128]{1,0:T(8,128)S(1)}, f32[256,128]{1,0:T(8,128)S(1)}, u32[]{:S(2)}, u32[]{:S(2)}) %collective-permute-start) | collective-permute-done | bytes 131104 | tf_op jit(solution)/shard_map/ppermute | solution.py:49
  2.9 0.1 fusion.91
  3.0 3.9 %collective-permute-start.3 = (f16[272,128]{1,0:T(8,128)(2,1)S(1)}, f16[272,128]{1,0:T(8,128)(2,1)S(1)}, u32[]{:S(2)}, u32[]{:S(2)}) collective-permute-start(f16[272,128]{1,0:T(8,128)(2,1)S(1)} %pad_maximum_fusion.1), channel_id=1, source_target_pairs={{0,24},{4,28},{8,16},{12,20},{16,8},{20,12},{24,0},{28,4},{1,25},{... | collective-permute-start | bytes 208904 | tf_op jit(solution)/shard_map/ppermute | solution.py:52
  6.9 0.5 %collective-permute-start.2 = (f16[272,128]{1,0:T(8,128)(2,1)S(1)}, f16[272,128]{1,0:T(8,128)(2,1)S(1)}, u32[]{:S(2)}, u32[]{:S(2)}) collective-permute-start(f16[272,128]{1,0:T(8,128)(2,1)S(1)} %pad_maximum_fusion.1), channel_id=1, source_target_pairs={{0,16},{4,20},{8,24},{12,28},{16,0},{20,4},{24,8},{28,12},{1,17},{... | collective-permute-start | bytes 208904 | tf_op jit(solution)/shard_map/ppermute | solution.py:52
  7.4 0.1 collective-permute-start.1
  7.5 1.9 %collective-permute-start.8 = (bf16[256,128]{1,0:T(8,128)(2,1)S(1)}, bf16[256,128]{1,0:T(8,128)(2,1)S(1)}, u32[]{:S(2)}, u32[]{:S(2)}) collective-permute-start(bf16[256,128]{1,0:T(8,128)(2,1)S(1)} %copy-done.1), channel_id=1, source_target_pairs={{0,8},{4,12},{8,0},{12,4},{16,24},{20,28},{24,16},{28,20},{1,9},{5... | collective-permute-start | bytes 196616 | tf_op jit(solution)/shard_map/ppermute | solution.py:52
  9.5 3.1 %collective-permute-done.8 = bf16[256,128]{1,0:T(8,128)(2,1)S(1)} collective-permute-done((bf16[256,128]{1,0:T(8,128)(2,1)S(1)}, bf16[256,128]{1,0:T(8,128)(2,1)S(1)}, u32[]{:S(2)}, u32[]{:S(2)}) %collective-permute-start.8) | collective-permute-done | bytes 65568 | tf_op jit(solution)/shard_map/ppermute | solution.py:52
  12.6 0.0 collective-permute-done.3
  12.7 0.0 collective-permute-done.2
  12.7 0.0 collective-permute-done.1
  12.7 0.3 constant_dynamic-update-slice_fusion.6
  13.1 0.1 fusion.92
  13.3 1.6 %collective-permute-start.4 = (f16[272,128]{1,0:T(8,128)(2,1)S(1)}, f16[272,128]{1,0:T(8,128)(2,1)S(1)}, u32[]{:S(2)}, u32[]{:S(2)}) collective-permute-start(f16[272,128]{1,0:T(8,128)(2,1)S(1)} %pad_maximum_fusion.2), channel_id=1, source_target_pairs={{0,1},{1,0},{2,3},{3,2},{4,5},{5,4},{6,7},{7,6},{8,9},{9,8},{10,11... | collective-permute-start | bytes 208904 | tf_op jit(solution)/shard_map/ppermute | solution.py:55
  15.0 2.7 %collective-permute-start.6 = (f16[272,128]{1,0:T(8,128)(2,1)S(1)}, f16[272,128]{1,0:T(8,128)(2,1)S(1)}, u32[]{:S(2)}, u32[]{:S(2)}) collective-permute-start(f16[272,128]{1,0:T(8,128)(2,1)S(1)} %pad_maximum_fusion.2), channel_id=1, source_target_pairs={{0,2},{1,3},{2,0},{3,1},{4,6},{5,7},{6,4},{7,5},{8,10},{9,11},{10,... | collective-permute-start | bytes 208904 | tf_op jit(solution)/shard_map/ppermute | solution.py:55
  17.6 0.2 collective-permute-start.7
  17.8 1.4 %collective-permute-start.9 = (bf16[512,128]{1,0:T(8,128)(2,1)S(1)}, bf16[512,128]{1,0:T(8,128)(2,1)S(1)}, u32[]{:S(2)}, u32[]{:S(2)}) collective-permute-start(bf16[512,128]{1,0:T(8,128)(2,1)S(1)} %pad_maximum_fusion), channel_id=1, source_target_pairs={{0,16},{4,20},{8,24},{12,28},{16,0},{20,4},{24,8},{28,12},{1,17},{... | collective-permute-start | bytes 393224 | tf_op jit(solution)/shard_map/ppermute | solution.py:52
  19.2 0.0 collective-permute-done.4
  19.2 0.0 collective-permute-start.5
  19.2 2.5 %collective-permute-done.6 = f16[272,128]{1,0:T(8,128)(2,1)S(1)} collective-permute-done((f16[272,128]{1,0:T(8,128)(2,1)S(1)}, f16[272,128]{1,0:T(8,128)(2,1)S(1)}, u32[]{:S(2)}, u32[]{:S(2)}) %collective-permute-start.6) | collective-permute-done | bytes 69664 | tf_op jit(solution)/shard_map/ppermute | solution.py:55
  21.7 2.0 %collective-permute-done.7 = f16[272,128]{1,0:T(8,128)(2,1)S(1)} collective-permute-done((f16[272,128]{1,0:T(8,128)(2,1)S(1)}, f16[272,128]{1,0:T(8,128)(2,1)S(1)}, u32[]{:S(2)}, u32[]{:S(2)}) %collective-permute-start.7) | collective-permute-done | bytes 69664 | tf_op jit(solution)/shard_map/ppermute | solution.py:55
  23.7 0.1 fusion.60
  23.8 0.1 fusion.75
  23.9 0.1 fusion.90
  24.0 0.0 collective-permute-done.9
  24.2 0.1 collective-permute-start.11
  24.2 0.4 %fusion.115 = f32[128,128]{1,0:T(8,128)S(1)} fusion(bf16[1024,128]{1,0:T(8,128)(2,1)S(1)} %slice_dynamic-update-slice_fusion, f32[1024,128]{1,0:T(8,128)S(1)} %fusion.90), kind=kOutput, calls=%fused_computation.177 | convolution fusion | flops 201326592 | bytes 851968 | tf_op jit(solution)/shard_map/dot_general | solution.py:58
  24.7 0.6 %collective-permute-start.10 = (f32[128,128]{1,0:T(8,128)S(1)}, f32[128,128]{1,0:T(8,128)S(1)}, u32[]{:S(2)}, u32[]{:S(2)}) collective-permute-start(f32[128,128]{1,0:T(8,128)S(1)} %fusion.115), channel_id=1, source_target_pairs={{0,4},{4,0},{8,12},{12,8},{16,20},{20,16},{24,28},{28,24},{1,5},{5... | collective-permute-start | bytes 196616 | tf_op jit(solution)/shard_map/ppermute | solution.py:49
  25.2 0.2 collective-permute-done.11
  25.5 0.3 fusion.116
  25.8 0.4 %collective-permute-done.10 = f32[128,128]{1,0:T(8,128)S(1)} collective-permute-done((f32[128,128]{1,0:T(8,128)S(1)}, f32[128,128]{1,0:T(8,128)S(1)}, u32[]{:S(2)}, u32[]{:S(2)}) %collective-permute-start.10) | collective-permute-done | bytes 65568 | tf_op jit(solution)/shard_map/ppermute | solution.py:49
  26.1 0.3 convolution_subtract_fusion.1
  26.4 0.6 %fusion.117 = f32[256,512]{1,0:T(8,128)S(1)} fusion(f32[256,128]{1,0:T(8,128)S(1)} %convolution_subtract_fusion.1, f32[512,128]{1,0:T(8,128)S(1)} %fusion.116), kind=kOutput, calls=%fused_computation.179 | convolution fusion | flops 201326592 | bytes 917504 | tf_op jit(solution)/shard_map/dot_general | solution.py:58
  27.0 0.0 copy-start.2
  27.0 0.0 collective-permute-done.5
  27.0 0.9 %copy-done.2 = bf16[256,512]{1,0:T(8,128)(2,1)S(1)} copy-done((bf16[256,512]{1,0:T(8,128)(2,1)S(1)}, bf16[256,512]{1,0:T(8,128)(2,1)}, u32[]{:S(2)}) %copy-start.2) | copy-done | bytes 262168
  28.0 1.4 %fusion = f32[256,512]{1,0:T(8,128)} fusion(f32[256,512]{1,0:T(8,128)S(1)} %fusion.117, f32[256,128]{1,0:T(8,128)S(1)} %fusion.113, f32[512,128]{1,0:T(8,128)S(1)} %constant_dynamic-update-slice_fusion.5, bf16[256,512]{1,0:T(8,128)(2,1)S(1)} %copy-done.2), kind=kOutput, calls=%fused_computation.1 | convolution fusion | flops 201719808 | bytes 1703936 | tf_op jit(solution)/shard_map/dot_general | solution.py:58
  (29 shorter events, 0.5 us)
Async XLA Ops:
  0.0 1.8 %copy-start = (f32[128,128]{1,0:T(8,128)S(1)}, f32[128,128]{1,0:T(8,128)}, u32[]{:S(2)}) copy-start(f32[128,128]{1,0:T(8,128)} %param.5) | copy-start | bytes 196612
  1.3 0.8 %copy-start.1 = (bf16[256,128]{1,0:T(8,128)(2,1)S(1)}, bf16[256,128]{1,0:T(8,128)(2,1)}, u32[]{:S(2)}) copy-start(bf16[256,128]{1,0:T(8,128)(2,1)} %param.4) | copy-start | bytes 196612
  1.3 1.5 %collective-permute-start = (f32[256,128]{1,0:T(8,128)S(1)}, f32[256,128]{1,0:T(8,128)S(1)}, u32[]{:S(2)}, u32[]{:S(2)}) collective-permute-start(f32[256,128]{1,0:T(8,128)S(1)} %constant_dynamic-slice_fusion.1), channel_id=1, source_target_pairs={{0,4},{4,0},{8,12},{12,8},{16,20},{20,16},{24,28},{28,24},{1,5},{5... | collective-permute-start | bytes 393224 | tf_op jit(solution)/shard_map/ppermute | solution.py:49
  3.0 9.6 %collective-permute-start.3 = (f16[272,128]{1,0:T(8,128)(2,1)S(1)}, f16[272,128]{1,0:T(8,128)(2,1)S(1)}, u32[]{:S(2)}, u32[]{:S(2)}) collective-permute-start(f16[272,128]{1,0:T(8,128)(2,1)S(1)} %pad_maximum_fusion.1), channel_id=1, source_target_pairs={{0,24},{4,28},{8,16},{12,20},{16,8},{20,12},{24,0},{28,4},{1,25},{... | collective-permute-start | bytes 208904 | tf_op jit(solution)/shard_map/ppermute | solution.py:52
  6.9 5.8 %collective-permute-start.2 = (f16[272,128]{1,0:T(8,128)(2,1)S(1)}, f16[272,128]{1,0:T(8,128)(2,1)S(1)}, u32[]{:S(2)}, u32[]{:S(2)}) collective-permute-start(f16[272,128]{1,0:T(8,128)(2,1)S(1)} %pad_maximum_fusion.1), channel_id=1, source_target_pairs={{0,16},{4,20},{8,24},{12,28},{16,0},{20,4},{24,8},{28,12},{1,17},{... | collective-permute-start | bytes 208904 | tf_op jit(solution)/shard_map/ppermute | solution.py:52
  7.4 5.3 %collective-permute-start.1 = (f16[272,128]{1,0:T(8,128)(2,1)S(1)}, f16[272,128]{1,0:T(8,128)(2,1)S(1)}, u32[]{:S(2)}, u32[]{:S(2)}) collective-permute-start(f16[272,128]{1,0:T(8,128)(2,1)S(1)} %pad_maximum_fusion.1), channel_id=1, source_target_pairs={{0,8},{4,12},{8,0},{12,4},{16,24},{20,28},{24,16},{28,20},{1,9},{5... | collective-permute-start | bytes 208904 | tf_op jit(solution)/shard_map/ppermute | solution.py:52
  7.5 5.1 %collective-permute-start.8 = (bf16[256,128]{1,0:T(8,128)(2,1)S(1)}, bf16[256,128]{1,0:T(8,128)(2,1)S(1)}, u32[]{:S(2)}, u32[]{:S(2)}) collective-permute-start(bf16[256,128]{1,0:T(8,128)(2,1)S(1)} %copy-done.1), channel_id=1, source_target_pairs={{0,8},{4,12},{8,0},{12,4},{16,24},{20,28},{24,16},{28,20},{1,9},{5... | collective-permute-start | bytes 196616 | tf_op jit(solution)/shard_map/ppermute | solution.py:52
  13.3 5.9 %collective-permute-start.4 = (f16[272,128]{1,0:T(8,128)(2,1)S(1)}, f16[272,128]{1,0:T(8,128)(2,1)S(1)}, u32[]{:S(2)}, u32[]{:S(2)}) collective-permute-start(f16[272,128]{1,0:T(8,128)(2,1)S(1)} %pad_maximum_fusion.2), channel_id=1, source_target_pairs={{0,1},{1,0},{2,3},{3,2},{4,5},{5,4},{6,7},{7,6},{8,9},{9,8},{10,11... | collective-permute-start | bytes 208904 | tf_op jit(solution)/shard_map/ppermute | solution.py:55
  15.0 6.8 %collective-permute-start.6 = (f16[272,128]{1,0:T(8,128)(2,1)S(1)}, f16[272,128]{1,0:T(8,128)(2,1)S(1)}, u32[]{:S(2)}, u32[]{:S(2)}) collective-permute-start(f16[272,128]{1,0:T(8,128)(2,1)S(1)} %pad_maximum_fusion.2), channel_id=1, source_target_pairs={{0,2},{1,3},{2,0},{3,1},{4,6},{5,7},{6,4},{7,5},{8,10},{9,11},{10,... | collective-permute-start | bytes 208904 | tf_op jit(solution)/shard_map/ppermute | solution.py:55
  17.6 6.1 %collective-permute-start.7 = (f16[272,128]{1,0:T(8,128)(2,1)S(1)}, f16[272,128]{1,0:T(8,128)(2,1)S(1)}, u32[]{:S(2)}, u32[]{:S(2)}) collective-permute-start(f16[272,128]{1,0:T(8,128)(2,1)S(1)} %pad_maximum_fusion.2), channel_id=1, source_target_pairs={{0,3},{1,2},{2,1},{3,0},{4,7},{5,6},{6,5},{7,4},{8,11},{9,10},{10,... | collective-permute-start | bytes 208904 | tf_op jit(solution)/shard_map/ppermute | solution.py:55
  17.8 6.2 %collective-permute-start.9 = (bf16[512,128]{1,0:T(8,128)(2,1)S(1)}, bf16[512,128]{1,0:T(8,128)(2,1)S(1)}, u32[]{:S(2)}, u32[]{:S(2)}) collective-permute-start(bf16[512,128]{1,0:T(8,128)(2,1)S(1)} %pad_maximum_fusion), channel_id=1, source_target_pairs={{0,16},{4,20},{8,24},{12,28},{16,0},{20,4},{24,8},{28,12},{1,17},{... | collective-permute-start | bytes 393224 | tf_op jit(solution)/shard_map/ppermute | solution.py:52
  19.2 7.8 %collective-permute-start.5 = (f32[256,128]{1,0:T(8,128)S(1)}, f32[256,128]{1,0:T(8,128)S(1)}, u32[]{:S(2)}, u32[]{:S(2)}) collective-permute-start(f32[256,128]{1,0:T(8,128)S(1)} %get-tuple-element.8), channel_id=1, source_target_pairs={{0,4},{4,0},{8,12},{12,8},{16,20},{20,16},{24,28},{28,24},{1,5},{5... | collective-permute-start | bytes 393224 | tf_op jit(solution)/shard_map/ppermute | solution.py:49
  24.2 1.3 %collective-permute-start.11 = (bf16[256,128]{1,0:T(8,128)(2,1)S(1)}, bf16[256,128]{1,0:T(8,128)(2,1)S(1)}, u32[]{:S(2)}, u32[]{:S(2)}) collective-permute-start(bf16[256,128]{1,0:T(8,128)(2,1)S(1)} %get-tuple-element.14), channel_id=1, source_target_pairs={{0,4},{4,0},{8,12},{12,8},{16,20},{20,16},{24,28},{28,24},{1,5},{5... | collective-permute-start | bytes 196616 | tf_op jit(solution)/shard_map/ppermute | solution.py:49
  24.7 1.5 %collective-permute-start.10 = (f32[128,128]{1,0:T(8,128)S(1)}, f32[128,128]{1,0:T(8,128)S(1)}, u32[]{:S(2)}, u32[]{:S(2)}) collective-permute-start(f32[128,128]{1,0:T(8,128)S(1)} %fusion.115), channel_id=1, source_target_pairs={{0,4},{4,0},{8,12},{12,8},{16,20},{20,16},{24,28},{28,24},{1,5},{5... | collective-permute-start | bytes 196616 | tf_op jit(solution)/shard_map/ppermute | solution.py:49
  27.0 1.0 %copy-start.2 = (bf16[256,512]{1,0:T(8,128)(2,1)S(1)}, bf16[256,512]{1,0:T(8,128)(2,1)}, u32[]{:S(2)}) copy-start(bf16[256,512]{1,0:T(8,128)(2,1)} %param.3) | copy-start | bytes 786436

commit v4 on v3

--- a/solution.py
+++ b/solution.py
@@ -1,11 +1,16 @@
+import functools
+
 import jax
 import jax.numpy as jnp
 from jax import lax
+from jax.experimental import pallas as pl
+from jax.experimental.pallas import tpu as pltpu
 from jax.sharding import PartitionSpec as P
 
 TOP = 30719.0
 LEAST = -100.0
-TILE = 16
+TILE = 8
+CHUNKS = 4
 
 
 def scale_of(ratio, exponent):
@@ -40,6 +45,52 @@
     return jnp.where(y < 0, -code, code) * step
 
 
+def halves(x):
+    high = x.astype(jnp.bfloat16)
+    return high, (x - high.astype(jnp.float32)).astype(jnp.bfloat16)
+
+
+def dot3(a, b):
+    ah, al = halves(a)
+    bh, bl = halves(b)
+    left = jnp.concatenate([ah, ah, al], 1)
+    right = jnp.concatenate([bh, bl, bh], 0)
+    return jnp.dot(left, right, preferred_element_type=jnp.float32)
+
+
+def finish(q, h_ref, a_ref, v_ref, y_ref, t_ref, p_ref, w_ref, piece_ref, g_ref, *rest):
+    others, (out_ref, left, right, held, sems) = rest[: q - 1], rest[q - 1 :]
+    rows, band = p_ref.shape
+    h = h_ref[0]
+    gram = g_ref[...]
+    for other in others:
+        gram = gram + other[pl.ds(0, band), :]
+    wide = dot3(p_ref[...] - dot3(y_ref[...], gram), t_ref[...])
+    high, low = halves(wide)
+    left[...] = jnp.concatenate([v_ref[...], v_ref[...], high, low], 1)
+    high, low = halves(w_ref[...])
+    right[:, 0:band] = high
+    right[:, band : 2 * band] = low
+    for s in range(q):
+        v = piece_ref[...] if s == 0 else others[s - 1][pl.ds(band, rows), :].astype(jnp.bfloat16)
+        at = pl.ds(pl.multiple_of((h ^ s) * rows, rows), rows)
+        right[at, 2 * band : 3 * band] = v
+        right[at, 3 * band : 4 * band] = v
+    part = rows // CHUNKS
+    copies = []
+    for i in range(CHUNKS):
+        at = pl.ds(i * part, part)
+        product = lax.dot_general(
+            left[at, :], right[...], (((1,), (1,)), ((), ())), preferred_element_type=jnp.float32
+        )
+        held[at, :] = a_ref[at, :].astype(jnp.float32) - product
+        copy = pltpu.make_async_copy(held.at[at, :], out_ref.at[at, :], sems.at[i])
+        copy.start()
+        copies.append(copy)
+    for copy in copies:
+        copy.wait()
+
+
 def solution(mesh):
     n_row, n_col = mesh.shape["row"], mesh.shape["col"]
     q = n_row // n_col
@@ -65,15 +116,19 @@
         return whole
 
     def shards(covariance, reflectors, factor):
-        rows = covariance.shape[0]
+        rows, cols = covariance.shape
+        band = reflectors.shape[1]
         row, c = lax.axis_index("row"), lax.axis_index("col")
         k, h = lax.div(row, q), lax.rem(row, q)
         back = lax.dot_general(
             covariance, reflectors, (((0,), (0,)), ((), ())), preferred_element_type=jnp.float32
         )
         piece = lax.dynamic_slice_in_dim(back, h * rows, rows, 0)
+        y_rows = dot(reflectors.astype(jnp.float32), factor, ((1,), (1,)))
         for s in range(1, q):
-            piece = piece + member(lax.dynamic_slice_in_dim(back, (h ^ s) * rows, rows, 0), s)
+            other = member(lax.dynamic_slice_in_dim(back, (h ^ s) * rows, rows, 0), s)
+            other, y_rows = lax.optimization_barrier((other, y_rows))
+            piece = piece + other
         message = encode(piece)
         others = [group(message, s) for s in range(1, n_col)]
         pieces, _ = lax.optimization_barrier((reflectors, message))
@@ -87,23 +142,47 @@
             held, _ = lax.optimization_barrier((pieces, message))
             pieces = jnp.concatenate([pieces, group(held, step)], 0)
             step *= 2
+        order = sorted(range(1, n_col), key=lambda s: (s < n_col // 2, s))
+        mates = {s: plane(message, s) for s in order}
+        held, _ = lax.optimization_barrier((total, mates[order[0]]))
+        p_cols = placed([total] + [member(held, s) for s in range(1, q)], h)
+        w_cols = dot(p_cols, factor, ((1,), (0,)))
+        values = {0: total}
+        for s in order[:-1]:
+            values[s] = decode(mates[s])
+        last, pieces, w_cols, values = lax.optimization_barrier((mates[order[-1]], pieces, w_cols, values))
+        values[order[-1]] = decode(last)
         v_mates = placed(jnp.split(pieces, n_col, 0), k)
-        mates = [plane(message, s) for s in range(1, n_col)]
-        held, _ = lax.optimization_barrier((total, mates[0]))
-        p_cols = placed([total] + [member(held, s) for s in range(1, q)], h)
-        p_mates = placed([total] + [decode(mate) for mate in mates], c)
-        v_piece = lax.dynamic_slice_in_dim(v_mates, c * rows, rows, 0)
-        v_cols = placed([v_piece] + [member(v_piece, s) for s in range(1, q)], h)
+
+        def v_tile(index):
+            return lax.dynamic_slice_in_dim(v_mates, index * rows, rows, 0)
+
+        p_rows = total
+        for s in order:
+            p_rows = jnp.where((k ^ c) == s, values[s], p_rows)
+        p_mates = placed([values[s] for s in range(n_col)], c)
         gram = dot(v_mates.astype(jnp.float32), p_mates, ((0,), (0,)))
-        whole = gram
-        for s in range(1, q):
-            whole = whole + member(gram, s)
-        p_rows = lax.dynamic_slice_in_dim(p_mates, k * rows, rows, 0)
-        y_rows = dot(reflectors.astype(jnp.float32), factor, ((1,), (1,)))
-        y_cols = dot(v_cols.astype(jnp.float32), factor, ((1,), (1,)))
-        first = covariance.astype(jnp.float32) - dot(y_rows, p_cols, ((1,), (1,)))
-        x_rows = p_rows - dot(y_rows, whole, ((1,), (0,)))
-        return first - dot(x_rows, y_cols, ((1,), (1,)))
+        v_piece = v_tile(c)
+        packed = jnp.concatenate([gram, v_piece.astype(jnp.float32)], 0)
+        received = [member(packed, s) for s in range(1, q)]
+        size = 4 * rows * cols + 2 * rows * cols + 16 * band * (rows + 2 * cols) + (q + 4) * 8 * rows * band
+        vmem = pl.BlockSpec(memory_space=pltpu.VMEM)
+        return pl.pallas_call(
+            functools.partial(finish, q),
+            out_shape=jax.ShapeDtypeStruct((rows, cols), jnp.float32),
+            in_specs=[pl.BlockSpec(memory_space=pltpu.SMEM)] + [vmem] * (7 + q),
+            out_specs=pl.BlockSpec(memory_space=pl.ANY),
+            scratch_shapes=[
+                pltpu.VMEM((rows, 4 * band), jnp.bfloat16),
+                pltpu.VMEM((cols, 4 * band), jnp.bfloat16),
+                pltpu.VMEM((rows, cols), jnp.float32),
+                pltpu.SemaphoreType.DMA((CHUNKS,)),
+            ],
+            compiler_params=pltpu.CompilerParams(vmem_limit_bytes=size + (8 << 20)),
+            cost_estimate=pl.CostEstimate(
+                flops=2 * rows * cols * 4 * band, bytes_accessed=6 * rows * cols, transcendentals=0
+            ),
+        )(jnp.full((1,), h, jnp.int32), covariance, reflectors, y_rows, factor, p_rows, w_cols, v_piece, gram, *received)
 
     in_specs = (P("row", "col"), P("row", None), P())
     return jax.shard_map(shards, mesh=mesh, in_specs=in_specs, out_specs=P("row", "col"), check_vma=False)

time: 29.6 us -> 26.5 us (0.90)
  matrix products: 4.45 us -> 2.25 us
  Pallas kernels: 0 us -> 1.66 us
  waiting for transfers between devices: 8.63 us -> 7.59 us
  local copies, waits for them, and re-layouts: 1.51 us -> 0.59 us
  starting transfers between devices: 13.5 us -> 12.8 us
    dot_general x6 -> x3, matrix products: 3.22 us -> 1.04 us  [dot(): lax.dot_general(a, b, (dims, ((), ())), precision=highest, preferred_elem...]
    pallas_call x0 -> x1, Pallas kernels: none -> 1.66 us  [shards(): pl.pallas_call(functools.partial(finish, q), out_shape=jax.ShapeDtypeStru...]
    ppermute x3, waiting for transfers between devices: 4.47 us -> 3.11 us  [plane(): return lax.ppermute(x, 'col', [(c, c ^ s) for c in range(n_col)])]
    unnamed x6, local copies, waits for them, and re-layouts: 1.23 us -> 0.33 us
    ppermute x4 -> x3, waiting for transfers between devices: 1.03 us -> 1.86 us  [member(): return lax.ppermute(x, 'row', [(r, r ^ s) for r in range(n_row)])]
    ppermute x4 -> x3, starting transfers between devices: 1.15 us -> 0.59 us  [member(): return lax.ppermute(x, 'row', [(r, r ^ s) for r in range(n_row)])]
    ppermute x5, waiting for transfers between devices: 3.13 us -> 2.62 us  [group(): return lax.ppermute(x, 'row', [(r, r ^ s * q) for r in range(n_row)])]
  transfers between devices with their start and end apart: 12 -> 11, of which waited for: 6 -> 7; matrix products, arithmetic and copies ran while one was open for 8% -> 5% of each run, Pallas kernels for 0% -> 0%
where the time goes in v4:
time: 26.5 us; the launch traced here: 26.3 us
  starting transfers between devices  12.8 us (48%)
  waiting for transfers between devices  7.59 us (29%)
  matrix products  2.25 us (8%)
  Pallas kernels  1.66 us (6%)
  other arithmetic  1.2 us (5%)
  local copies, waits for them, and re-layouts  0.59 us (2%)
  between operations  0.28 us (1%)
    ppermute x5, starting transfers between devices, group(): return lax.ppermute(x, 'row', [(r, r ^ s * q) for r in range(n_row)])  7.81 us
    ppermute x3, starting transfers between devices, plane(): return lax.ppermute(x, 'col', [(c, c ^ s) for c in range(n_col)])  4.37 us
    ppermute x3, waiting for transfers between devices, plane(): return lax.ppermute(x, 'col', [(c, c ^ s) for c in range(n_col)])  3.11 us
    ppermute x5, waiting for transfers between devices, group(): return lax.ppermute(x, 'row', [(r, r ^ s * q) for r in range(n_row)])  2.62 us
    ppermute x3, waiting for transfers between devices, member(): return lax.ppermute(x, 'row', [(r, r ^ s) for r in range(n_row)])  1.86 us
    pallas_call x1, Pallas kernels, shards(): pl.pallas_call(functools.partial(finish, q), out_shape=jax.ShapeDtypeStru...  1.66 us
    dot_general x1, matrix products, shards(): lax.dot_general(covariance, reflectors, (((0,), (0,)), ((), ())), preferr...  1.21 us
    dot_general x3, matrix products, dot(): lax.dot_general(a, b, (dims, ((), ())), precision=highest, preferred_elem...  1.04 us
  transfers between devices with their start and end apart: 11, of which 7 were waited for; matrix products, arithmetic and copies ran while one was open for 5% of the time, Pallas kernels for 0%

profile of v4, /device:TPU:0, one launch (start us, length us, event | category | flops | bytes accessed | tf_op | source)
XLA Modules:
  0.0 26.3 jit_solution(5886442148499647030)
XLA Ops:
  0.0 1.2 %fusion.106 = f32[512,128]{1,0:T(8,128)S(1)} fusion(bf16[256,512]{1,0:T(8,128)(2,1)} %a_ref.1, bf16[256,128]{1,0:T(8,128)(2,1)} %v_ref.1), kind=kOutput, calls=%fused_computation.168 | convolution fusion | flops 33554432 | bytes 589824 | tf_op jit(solution)/shard_map/dot_general | solution.py:123
  1.2 0.0 copy-start
  1.2 0.0 copy-start.2
  1.3 0.5 %collective-permute-start = (f32[256,128]{1,0:T(8,128)S(1)}, f32[256,128]{1,0:T(8,128)S(1)}, u32[]{:S(2)}, u32[]{:S(2)}) collective-permute-start(f32[256,128]{1,0:T(8,128)S(1)} %constant_dynamic-slice_fusion.1), channel_id=1, source_target_pairs={{0,4},{4,0},{8,12},{12,8},{16,20},{20,16},{24,28},{28,24},{1,5},{5... | collective-permute-start | bytes 393224 | tf_op jit(solution)/shard_map/ppermute | solution.py:100
  1.8 0.3 %copy-done = bf16[256,128]{1,0:T(8,128)(2,1)S(1)} copy-done((bf16[256,128]{1,0:T(8,128)(2,1)S(1)}, bf16[256,128]{1,0:T(8,128)(2,1)}, u32[]{:S(2)}) %copy-start) | copy-done | bytes 65560
  2.1 0.0 copy-done.2
  2.1 0.2 fusion.107.y_ref
  2.3 0.4 %collective-permute-done = f32[256,128]{1,0:T(8,128)S(1)} collective-permute-done((f32[256,128]{1,0:T(8,128)S(1)}, f32[256,128]{1,0:T(8,128)S(1)}, u32[]{:S(2)}, u32[]{:S(2)}) %collective-permute-start) | collective-permute-done | bytes 131104 | tf_op jit(solution)/shard_map/ppermute | solution.py:100
  2.8 0.1 fusion.87
  3.0 3.9 %collective-permute-start.3 = (f16[264,128]{1,0:T(8,128)(2,1)S(1)}, f16[264,128]{1,0:T(8,128)(2,1)S(1)}, u32[]{:S(2)}, u32[]{:S(2)}) collective-permute-start(f16[264,128]{1,0:T(8,128)(2,1)S(1)} %pad_maximum_fusion.3), channel_id=1, source_target_pairs={{0,24},{4,28},{8,16},{12,20},{16,8},{20,12},{24,0},{28,4},{1,25},{... | collective-permute-start | bytes 202760 | tf_op jit(solution)/shard_map/ppermute | solution.py:103
  6.9 0.5 %collective-permute-start.2 = (f16[264,128]{1,0:T(8,128)(2,1)S(1)}, f16[264,128]{1,0:T(8,128)(2,1)S(1)}, u32[]{:S(2)}, u32[]{:S(2)}) collective-permute-start(f16[264,128]{1,0:T(8,128)(2,1)S(1)} %pad_maximum_fusion.3), channel_id=1, source_target_pairs={{0,16},{4,20},{8,24},{12,28},{16,0},{20,4},{24,8},{28,12},{1,17},{... | collective-permute-start | bytes 202760 | tf_op jit(solution)/shard_map/ppermute | solution.py:103
  7.4 0.2 collective-permute-start.1
  7.6 1.8 %collective-permute-start.5 = (bf16[256,128]{1,0:T(8,128)(2,1)S(1)}, bf16[256,128]{1,0:T(8,128)(2,1)S(1)}, u32[]{:S(2)}, u32[]{:S(2)}) collective-permute-start(bf16[256,128]{1,0:T(8,128)(2,1)S(1)} %copy-done), channel_id=1, source_target_pairs={{0,8},{4,12},{8,0},{12,4},{16,24},{20,28},{24,16},{28,20},{1,9},{5... | collective-permute-start | bytes 196616 | tf_op jit(solution)/shard_map/ppermute | solution.py:103
  9.4 0.0 collective-permute-done.3
  9.4 1.7 %collective-permute-done.2 = f16[264,128]{1,0:T(8,128)(2,1)S(1)} collective-permute-done((f16[264,128]{1,0:T(8,128)(2,1)S(1)}, f16[264,128]{1,0:T(8,128)(2,1)S(1)}, u32[]{:S(2)}, u32[]{:S(2)}) %collective-permute-start.2) | collective-permute-done | bytes 67616 | tf_op jit(solution)/shard_map/ppermute | solution.py:103
  11.2 0.6 %collective-permute-done.1 = f16[264,128]{1,0:T(8,128)(2,1)S(1)} collective-permute-done((f16[264,128]{1,0:T(8,128)(2,1)S(1)}, f16[264,128]{1,0:T(8,128)(2,1)S(1)}, u32[]{:S(2)}, u32[]{:S(2)}) %collective-permute-start.1) | collective-permute-done | bytes 67616 | tf_op jit(solution)/shard_map/ppermute | solution.py:103
  11.9 0.3 %constant_dynamic-update-slice_fusion.5 = (f32[512,128]{1,0:T(8,128)S(1)}, f32[256,128]{1,0:T(8,128)S(1)}) fusion(f32[512,128]{1,0:T(8,128)S(1)} %broadcast_in_dim.39, s32[]{:T(128)S(6)} %select_n.80, f32[128]{0:T(128)S(1)} %multiply_bitcast_fusion.3, f16[264,128]{1,0:T(8,128)(2,1)S(1)} %collective-permute-done.3, f32[128]{0:T(128)S(1)} %multiply_bitcast_fusion.4, ...), kind=kLoop, calls=%fused_computation.128 | loop fusion | flops 1966080 | bytes 591364 | tf_op jit(solution)/shard_map/dynamic_update_slice | solution.py:115
  12.2 0.1 fusion.88
  12.4 2.7 %collective-permute-start.7 = (f16[264,128]{1,0:T(8,128)(2,1)S(1)}, f16[264,128]{1,0:T(8,128)(2,1)S(1)}, u32[]{:S(2)}, u32[]{:S(2)}) collective-permute-start(f16[264,128]{1,0:T(8,128)(2,1)S(1)} %pad_maximum_fusion.4), channel_id=1, source_target_pairs={{0,2},{1,3},{2,0},{3,1},{4,6},{5,7},{6,4},{7,5},{8,10},{9,11},{10,... | collective-permute-start | bytes 202760 | tf_op jit(solution)/shard_map/ppermute | solution.py:106
  15.0 0.0 collective-permute-done.5
  15.1 1.4 %collective-permute-start.9 = (f16[264,128]{1,0:T(8,128)(2,1)S(1)}, f16[264,128]{1,0:T(8,128)(2,1)S(1)}, u32[]{:S(2)}, u32[]{:S(2)}) collective-permute-start(f16[264,128]{1,0:T(8,128)(2,1)S(1)} %pad_maximum_fusion.4), channel_id=1, source_target_pairs={{0,3},{1,2},{2,1},{3,0},{4,7},{5,6},{6,5},{7,4},{8,11},{9,10},{10,... | collective-permute-start | bytes 202760 | tf_op jit(solution)/shard_map/ppermute | solution.py:106
  16.5 0.3 %collective-permute-start.4 = (f16[264,128]{1,0:T(8,128)(2,1)S(1)}, f16[264,128]{1,0:T(8,128)(2,1)S(1)}, u32[]{:S(2)}, u32[]{:S(2)}) collective-permute-start(f16[264,128]{1,0:T(8,128)(2,1)S(1)} %pad_maximum_fusion.4), channel_id=1, source_target_pairs={{0,1},{1,0},{2,3},{3,2},{4,5},{5,4},{6,7},{7,6},{8,9},{9,8},{10,11... | collective-permute-start | bytes 202760 | tf_op jit(solution)/shard_map/ppermute | solution.py:106
  16.8 1.4 %collective-permute-start.6 = (bf16[512,128]{1,0:T(8,128)(2,1)S(1)}, bf16[512,128]{1,0:T(8,128)(2,1)S(1)}, u32[]{:S(2)}, u32[]{:S(2)}) collective-permute-start(bf16[512,128]{1,0:T(8,128)(2,1)S(1)} %pad_maximum_fusion.2), channel_id=1, source_target_pairs={{0,16},{4,20},{8,24},{12,28},{16,0},{20,4},{24,8},{28,12},{1,17},{... | collective-permute-start | bytes 393224 | tf_op jit(solution)/shard_map/ppermute | solution.py:103
  18.2 1.5 %collective-permute-done.7 = f16[264,128]{1,0:T(8,128)(2,1)S(1)} collective-permute-done((f16[264,128]{1,0:T(8,128)(2,1)S(1)}, f16[264,128]{1,0:T(8,128)(2,1)S(1)}, u32[]{:S(2)}, u32[]{:S(2)}) %collective-permute-start.7) | collective-permute-done | bytes 67616 | tf_op jit(solution)/shard_map/ppermute | solution.py:106
  19.7 0.0 collective-permute-start.8
  19.8 1.6 %collective-permute-done.9 = f16[264,128]{1,0:T(8,128)(2,1)S(1)} collective-permute-done((f16[264,128]{1,0:T(8,128)(2,1)S(1)}, f16[264,128]{1,0:T(8,128)(2,1)S(1)}, u32[]{:S(2)}, u32[]{:S(2)}) %collective-permute-start.9) | collective-permute-done | bytes 67616 | tf_op jit(solution)/shard_map/ppermute | solution.py:106
  21.3 0.1 fusion.72
  21.4 0.1 fusion.58
  21.5 0.2 collective-permute-done.6
  21.8 0.0 collective-permute-done.8
  21.8 0.4 %fusion.108.w_ref = f32[512,128]{1,0:T(8,128)S(1)} fusion(f32[512,128]{1,0:T(8,128)S(1)} %constant_dynamic-update-slice_fusion.4, f32[128,128]{1,0:T(8,128)S(1)} %copy-done.2), kind=kOutput, calls=%fused_computation.170 | convolution fusion | flops 100663296 | bytes 589824 | tf_op jit(solution)/shard_map/dot_general | solution.py:109
  22.2 0.0 collective-permute-done.4
  22.4 0.1 constant_dynamic-update-slice_fusion.2
  22.6 0.1 constant_dynamic-update-slice_fusion
  22.7 0.4 %fusion.109.g_ref = f32[128,128]{1,0:T(8,128)S(1)} fusion(bf16[1024,128]{1,0:T(8,128)(2,1)S(1)} %slice_dynamic-update-slice_fusion, f32[1024,128]{1,0:T(8,128)S(1)} %get-tuple-element.39), kind=kOutput, calls=%fused_computation.171 | convolution fusion | flops 201326592 | bytes 851968 | tf_op jit(solution)/shard_map/dot_general | solution.py:109
  23.1 0.0 copy-start.1
  23.2 0.1 collective-permute-start.10
  23.2 1.4 %collective-permute-done.10.rest_0_ = f32[384,128]{1,0:T(8,128)S(1)} collective-permute-done((f32[384,128]{1,0:T(8,128)S(1)}, f32[384,128]{1,0:T(8,128)S(1)}, u32[]{:S(2)}, u32[]{:S(2)}) %collective-permute-start.10) | collective-permute-done | bytes 196640 | tf_op jit(solution)/shard_map/ppermute | solution.py:100
  24.7 0.0 copy-done.1
  24.7 1.7 %shard_map.37 = f32[256,512]{1,0:T(8,128)} custom-call(s32[1]{0:T(128)} %bitcast.h_ref, bf16[256,512]{1,0:T(8,128)(2,1)S(1)} %copy-done.1, bf16[256,128]{1,0:T(8,128)(2,1)S(1)} %copy-done, f32[256,128]{1,0:T(8,128)S(1)} %fusion.107.y_ref, f32[128,128]{1,0:T(8,128)S(1)} %copy-done.2, f32[256,128]{1,0:T(8,128)S(1)} %get-tuple-element.40.p_ref, ...), custom_call_target="tpu_custom_call" | custom-call | flops 134217728 | bytes 786432 | tf_op jit(solution)/shard_map/pallas_call | solution.py:170
  (31 shorter events, 0.6 us)
Async XLA Ops:
  1.2 0.8 %copy-start = (bf16[256,128]{1,0:T(8,128)(2,1)S(1)}, bf16[256,128]{1,0:T(8,128)(2,1)}, u32[]{:S(2)}) copy-start(bf16[256,128]{1,0:T(8,128)(2,1)} %v_ref.1) | copy-start | bytes 196612
  1.2 0.9 %copy-start.2 = (f32[128,128]{1,0:T(8,128)S(1)}, f32[128,128]{1,0:T(8,128)}, u32[]{:S(2)}) copy-start(f32[128,128]{1,0:T(8,128)} %t_ref.1) | copy-start | bytes 196612
  1.3 1.5 %collective-permute-start = (f32[256,128]{1,0:T(8,128)S(1)}, f32[256,128]{1,0:T(8,128)S(1)}, u32[]{:S(2)}, u32[]{:S(2)}) collective-permute-start(f32[256,128]{1,0:T(8,128)S(1)} %constant_dynamic-slice_fusion.1), channel_id=1, source_target_pairs={{0,4},{4,0},{8,12},{12,8},{16,20},{20,16},{24,28},{28,24},{1,5},{5... | collective-permute-start | bytes 393224 | tf_op jit(solution)/shard_map/ppermute | solution.py:100
  3.0 6.4 %collective-permute-start.3 = (f16[264,128]{1,0:T(8,128)(2,1)S(1)}, f16[264,128]{1,0:T(8,128)(2,1)S(1)}, u32[]{:S(2)}, u32[]{:S(2)}) collective-permute-start(f16[264,128]{1,0:T(8,128)(2,1)S(1)} %pad_maximum_fusion.3), channel_id=1, source_target_pairs={{0,24},{4,28},{8,16},{12,20},{16,8},{20,12},{24,0},{28,4},{1,25},{... | collective-permute-start | bytes 202760 | tf_op jit(solution)/shard_map/ppermute | solution.py:103
  6.9 4.3 %collective-permute-start.2 = (f16[264,128]{1,0:T(8,128)(2,1)S(1)}, f16[264,128]{1,0:T(8,128)(2,1)S(1)}, u32[]{:S(2)}, u32[]{:S(2)}) collective-permute-start(f16[264,128]{1,0:T(8,128)(2,1)S(1)} %pad_maximum_fusion.3), channel_id=1, source_target_pairs={{0,16},{4,20},{8,24},{12,28},{16,0},{20,4},{24,8},{28,12},{1,17},{... | collective-permute-start | bytes 202760 | tf_op jit(solution)/shard_map/ppermute | solution.py:103
  7.4 4.4 %collective-permute-start.1 = (f16[264,128]{1,0:T(8,128)(2,1)S(1)}, f16[264,128]{1,0:T(8,128)(2,1)S(1)}, u32[]{:S(2)}, u32[]{:S(2)}) collective-permute-start(f16[264,128]{1,0:T(8,128)(2,1)S(1)} %pad_maximum_fusion.3), channel_id=1, source_target_pairs={{0,8},{4,12},{8,0},{12,4},{16,24},{20,28},{24,16},{28,20},{1,9},{5... | collective-permute-start | bytes 202760 | tf_op jit(solution)/shard_map/ppermute | solution.py:103
  7.6 7.5 %collective-permute-start.5 = (bf16[256,128]{1,0:T(8,128)(2,1)S(1)}, bf16[256,128]{1,0:T(8,128)(2,1)S(1)}, u32[]{:S(2)}, u32[]{:S(2)}) collective-permute-start(bf16[256,128]{1,0:T(8,128)(2,1)S(1)} %copy-done), channel_id=1, source_target_pairs={{0,8},{4,12},{8,0},{12,4},{16,24},{20,28},{24,16},{28,20},{1,9},{5... | collective-permute-start | bytes 196616 | tf_op jit(solution)/shard_map/ppermute | solution.py:103
  12.4 7.4 %collective-permute-start.7 = (f16[264,128]{1,0:T(8,128)(2,1)S(1)}, f16[264,128]{1,0:T(8,128)(2,1)S(1)}, u32[]{:S(2)}, u32[]{:S(2)}) collective-permute-start(f16[264,128]{1,0:T(8,128)(2,1)S(1)} %pad_maximum_fusion.4), channel_id=1, source_target_pairs={{0,2},{1,3},{2,0},{3,1},{4,6},{5,7},{6,4},{7,5},{8,10},{9,11},{10,... | collective-permute-start | bytes 202760 | tf_op jit(solution)/shard_map/ppermute | solution.py:106
  15.1 6.3 %collective-permute-start.9 = (f16[264,128]{1,0:T(8,128)(2,1)S(1)}, f16[264,128]{1,0:T(8,128)(2,1)S(1)}, u32[]{:S(2)}, u32[]{:S(2)}) collective-permute-start(f16[264,128]{1,0:T(8,128)(2,1)S(1)} %pad_maximum_fusion.4), channel_id=1, source_target_pairs={{0,3},{1,2},{2,1},{3,0},{4,7},{5,6},{6,5},{7,4},{8,11},{9,10},{10,... | collective-permute-start | bytes 202760 | tf_op jit(solution)/shard_map/ppermute | solution.py:106
  16.5 5.7 %collective-permute-start.4 = (f16[264,128]{1,0:T(8,128)(2,1)S(1)}, f16[264,128]{1,0:T(8,128)(2,1)S(1)}, u32[]{:S(2)}, u32[]{:S(2)}) collective-permute-start(f16[264,128]{1,0:T(8,128)(2,1)S(1)} %pad_maximum_fusion.4), channel_id=1, source_target_pairs={{0,1},{1,0},{2,3},{3,2},{4,5},{5,4},{6,7},{7,6},{8,9},{9,8},{10,11... | collective-permute-start | bytes 202760 | tf_op jit(solution)/shard_map/ppermute | solution.py:106
  16.8 5.0 %collective-permute-start.6 = (bf16[512,128]{1,0:T(8,128)(2,1)S(1)}, bf16[512,128]{1,0:T(8,128)(2,1)S(1)}, u32[]{:S(2)}, u32[]{:S(2)}) collective-permute-start(bf16[512,128]{1,0:T(8,128)(2,1)S(1)} %pad_maximum_fusion.2), channel_id=1, source_target_pairs={{0,16},{4,20},{8,24},{12,28},{16,0},{20,4},{24,8},{28,12},{1,17},{... | collective-permute-start | bytes 393224 | tf_op jit(solution)/shard_map/ppermute | solution.py:103
  19.7 2.0 %collective-permute-start.8 = (f32[256,128]{1,0:T(8,128)S(1)}, f32[256,128]{1,0:T(8,128)S(1)}, u32[]{:S(2)}, u32[]{:S(2)}) collective-permute-start(f32[256,128]{1,0:T(8,128)S(1)} %get-tuple-element.26), channel_id=1, source_target_pairs={{0,4},{4,0},{8,12},{12,8},{16,20},{20,16},{24,28},{28,24},{1,5},{5... | collective-permute-start | bytes 393224 | tf_op jit(solution)/shard_map/ppermute | solution.py:100
  23.1 1.5 %copy-start.1 = (bf16[256,512]{1,0:T(8,128)(2,1)S(1)}, bf16[256,512]{1,0:T(8,128)(2,1)}, u32[]{:S(2)}) copy-start(bf16[256,512]{1,0:T(8,128)(2,1)} %a_ref.1) | copy-start | bytes 786436
  23.2 1.5 %collective-permute-start.10 = (f32[384,128]{1,0:T(8,128)S(1)}, f32[384,128]{1,0:T(8,128)S(1)}, u32[]{:S(2)}, u32[]{:S(2)}) collective-permute-start(f32[384,128]{1,0:T(8,128)S(1)} %pad_maximum_fusion.1), channel_id=1, source_target_pairs={{0,4},{4,0},{8,12},{12,8},{16,20},{20,16},{24,28},{28,24},{1,5},{5... | collective-permute-start | bytes 589832 | tf_op jit(solution)/shard_map/ppermute | solution.py:100

commit v5 on v4

--- a/solution.py
+++ b/solution.py
@@ -10,15 +10,14 @@
 TOP = 30719.0
 LEAST = -100.0
 TILE = 8
-CHUNKS = 4
+CHUNKS = 2
 
 
 def scale_of(ratio, exponent):
     return ratio.astype(jnp.float32) * jnp.exp2(exponent.astype(jnp.float32))
 
 
-def encode(x):
-    top = jnp.max(jnp.abs(x), axis=0, keepdims=True)
+def encode(x, top):
     exponent = lax.reduce_precision(jnp.maximum(jnp.ceil(jnp.log2(top)), LEAST), 5, 10).astype(jnp.float16)
     ratio = jnp.clip(top * jnp.exp2(-exponent.astype(jnp.float32)) * 1.001, 0.25, 2.0)
     ratio = lax.reduce_precision(ratio, 5, 10).astype(jnp.float16)
@@ -34,6 +33,11 @@
     return jnp.concatenate([coded, tail], 0)
 
 
+def scale_in(message):
+    rows = message.shape[0] - TILE
+    return scale_of(message[rows : rows + 1], message[rows + TILE // 2 : rows + TILE // 2 + 1])
+
+
 def decode(message):
     rows = message.shape[0] - TILE
     y = message[:rows].astype(jnp.float32)
@@ -41,7 +45,7 @@
     order = 31 - lax.clz(size.astype(jnp.int32))
     inverse = lax.shift_left(jnp.int32(1), 30 - order).astype(jnp.float32) * 2.0**-30
     code = 1024.0 * (order.astype(jnp.float32) + (size * inverse - 1.0))
-    step = scale_of(message[rows : rows + 1], message[rows + TILE // 2 : rows + TILE // 2 + 1]) * (1.0 / TOP)
+    step = scale_in(message) * (1.0 / TOP)
     return jnp.where(y < 0, -code, code) * step
 
 
@@ -76,15 +80,15 @@
         at = pl.ds(pl.multiple_of((h ^ s) * rows, rows), rows)
         right[at, 2 * band : 3 * band] = v
         right[at, 3 * band : 4 * band] = v
-    part = rows // CHUNKS
+    part = a_ref.shape[1] // CHUNKS
     copies = []
     for i in range(CHUNKS):
         at = pl.ds(i * part, part)
         product = lax.dot_general(
-            left[at, :], right[...], (((1,), (1,)), ((), ())), preferred_element_type=jnp.float32
+            left[...], right[at, :], (((1,), (1,)), ((), ())), preferred_element_type=jnp.float32
         )
-        held[at, :] = a_ref[at, :].astype(jnp.float32) - product
-        copy = pltpu.make_async_copy(held.at[at, :], out_ref.at[at, :], sems.at[i])
+        held[:, at] = a_ref[:, at].astype(jnp.float32) - product
+        copy = pltpu.make_async_copy(held.at[:, at], out_ref.at[:, at], sems.at[i])
         copy.start()
         copies.append(copy)
     for copy in copies:
@@ -120,23 +124,26 @@
         band = reflectors.shape[1]
         row, c = lax.axis_index("row"), lax.axis_index("col")
         k, h = lax.div(row, q), lax.rem(row, q)
-        back = lax.dot_general(
-            covariance, reflectors, (((0,), (0,)), ((), ())), preferred_element_type=jnp.float32
-        )
-        piece = lax.dynamic_slice_in_dim(back, h * rows, rows, 0)
         y_rows = dot(reflectors.astype(jnp.float32), factor, ((1,), (1,)))
+
+        def chip_part(tile, vectors):
+            half = lax.dynamic_slice_in_dim(tile, h * rows, rows, 1)
+            return lax.dot_general(half, vectors, (((0,), (0,)), ((), ())), preferred_element_type=jnp.float32)
+
+        piece = chip_part(covariance, reflectors)
         for s in range(1, q):
-            other = member(lax.dynamic_slice_in_dim(back, (h ^ s) * rows, rows, 0), s)
-            other, y_rows = lax.optimization_barrier((other, y_rows))
-            piece = piece + other
-        message = encode(piece)
+            tile, vectors, piece = lax.optimization_barrier((member(covariance, s), member(reflectors, s), piece))
+            piece = piece + chip_part(tile, vectors)
+        message = encode(piece, jnp.max(jnp.abs(piece), axis=0, keepdims=True))
+        top = scale_in(message)
         others = [group(message, s) for s in range(1, n_col)]
         pieces, _ = lax.optimization_barrier((reflectors, message))
         pieces = jnp.concatenate([pieces, group(pieces, 1)], 0)
-        total = piece
+        total, others[-1], y_rows = lax.optimization_barrier((piece, others[-1], y_rows))
         for other in others:
             total = total + decode(other)
-        message = encode(total)
+            top = top + scale_in(other)
+        message = encode(total, top)
         step = 2
         while step < n_col:
             held, _ = lax.optimization_barrier((pieces, message))
@@ -149,20 +156,23 @@
         w_cols = dot(p_cols, factor, ((1,), (0,)))
         values = {0: total}
         for s in order[:-1]:
-            values[s] = decode(mates[s])
-        last, pieces, w_cols, values = lax.optimization_barrier((mates[order[-1]], pieces, w_cols, values))
+            mate = mates[s]
+            values[s] = decode(mate)
+        last, pieces, values = lax.optimization_barrier((mates[order[-1]], pieces, values))
         values[order[-1]] = decode(last)
-        v_mates = placed(jnp.split(pieces, n_col, 0), k)
-
-        def v_tile(index):
-            return lax.dynamic_slice_in_dim(v_mates, index * rows, rows, 0)
-
+        tiles = jnp.split(pieces, n_col, 0)
+        bit = 1
+        while bit < n_col:
+            swap = ((k ^ c) & bit) != 0
+            tiles = [jnp.where(swap, tiles[s ^ bit], tiles[s]) for s in range(n_col)]
+            bit *= 2
+        v_mates = jnp.concatenate(tiles, 0)
         p_rows = total
         for s in order:
             p_rows = jnp.where((k ^ c) == s, values[s], p_rows)
-        p_mates = placed([values[s] for s in range(n_col)], c)
+        p_mates = jnp.concatenate([values[s] for s in range(n_col)], 0)
         gram = dot(v_mates.astype(jnp.float32), p_mates, ((0,), (0,)))
-        v_piece = v_tile(c)
+        v_piece = tiles[0]
         packed = jnp.concatenate([gram, v_piece.astype(jnp.float32)], 0)
         received = [member(packed, s) for s in range(1, q)]
         size = 4 * rows * cols + 2 * rows * cols + 16 * band * (rows + 2 * cols) + (q + 4) * 8 * rows * band

time: 26.5 us -> 24.9 us (0.940)
  local copies, waits for them, and re-layouts: 0.59 us -> 0.08 us
  waiting for transfers between devices: 7.59 us -> 7.18 us
  starting transfers between devices: 12.8 us -> 12.4 us
  Pallas kernels: 1.66 us -> 1.35 us
    ppermute x3 -> x4, waiting for transfers between devices: 1.86 us -> 1.29 us  [member(): return lax.ppermute(x, 'row', [(r, r ^ s) for r in range(n_row)])]
    ppermute x3, waiting for transfers between devices: 3.11 us -> 3.59 us  [plane(): return lax.ppermute(x, 'col', [(c, c ^ s) for c in range(n_col)])]
    ppermute x5, starting transfers between devices: 7.81 us -> 7.41 us  [group(): return lax.ppermute(x, 'row', [(r, r ^ s * q) for r in range(n_row)])]
    ppermute x5, waiting for transfers between devices: 2.62 us -> 2.29 us  [group(): return lax.ppermute(x, 'row', [(r, r ^ s * q) for r in range(n_row)])]
    unnamed x6, local copies, waits for them, and re-layouts: 0.33 us -> 0.02 us
    pallas_call x1, Pallas kernels: 1.66 us -> 1.35 us  [shards(): pl.pallas_call(functools.partial(finish, q), out_shape=jax.ShapeDtypeStru...]
    dot_general x1 -> x2, matrix products: 1.21 us -> 1.35 us  [chip_part(): lax.dot_general(half, vectors, (((0,), (0,)), ((), ())), preferred_elemen...]
    ppermute x3 -> x4, starting transfers between devices: 0.59 us -> 0.58 us  [member(): return lax.ppermute(x, 'row', [(r, r ^ s) for r in range(n_row)])]
  transfers between devices with their start and end apart: 11 -> 12, of which waited for: 7 -> 6; matrix products, arithmetic and copies ran while one was open for 5% -> 13% of each run, Pallas kernels for 0% -> 0%
where the time goes in v5:
time: 24.9 us; the launch traced here: 24.7 us
  starting transfers between devices  12.4 us (50%)
  waiting for transfers between devices  7.18 us (29%)
  matrix products  2.39 us (10%)
  Pallas kernels  1.35 us (5%)
  other arithmetic  1.11 us (4%)
  between operations  0.25 us (1%)
    ppermute x5, starting transfers between devices, group(): return lax.ppermute(x, 'row', [(r, r ^ s * q) for r in range(n_row)])  7.41 us
    ppermute x3, starting transfers between devices, plane(): return lax.ppermute(x, 'col', [(c, c ^ s) for c in range(n_col)])  4.37 us
    ppermute x3, waiting for transfers between devices, plane(): return lax.ppermute(x, 'col', [(c, c ^ s) for c in range(n_col)])  3.59 us
    ppermute x5, waiting for transfers between devices, group(): return lax.ppermute(x, 'row', [(r, r ^ s * q) for r in range(n_row)])  2.29 us
    pallas_call x1, Pallas kernels, shards(): pl.pallas_call(functools.partial(finish, q), out_shape=jax.ShapeDtypeStru...  1.35 us
    dot_general x2, matrix products, chip_part(): lax.dot_general(half, vectors, (((0,), (0,)), ((), ())), preferred_elemen...  1.35 us
    ppermute x4, waiting for transfers between devices, member(): return lax.ppermute(x, 'row', [(r, r ^ s) for r in range(n_row)])  1.29 us
    dot_general x3, matrix products, dot(): lax.dot_general(a, b, (dims, ((), ())), precision=highest, preferred_elem...  1.04 us
  transfers between devices with their start and end apart: 12, of which 6 were waited for; matrix products, arithmetic and copies ran while one was open for 13% of the time, Pallas kernels for 0%

profile of v5, /device:TPU:0, one launch (start us, length us, event | category | flops | bytes accessed | tf_op | source)
XLA Modules:
  0.0 24.7 jit_solution(10936460857183459272)
XLA Ops:
  0.0 0.5 %collective-permute-start = (bf16[256,512]{1,0:T(8,128)(2,1)}, bf16[256,512]{1,0:T(8,128)(2,1)S(1)}, u32[]{:S(2)}, u32[]{:S(2)}) collective-permute-start(bf16[256,512]{1,0:T(8,128)(2,1)} %a_ref.1), channel_id=1, source_target_pairs={{0,4},{4,0},{8,12},{12,8},{16,20},{20,16},{24,28},{28,24},{1,5},{5... | collective-permute-start | bytes 786440 | tf_op jit(solution)/shard_map/ppermute | solution.py:104
  0.5 0.1 collective-permute-start.1
  0.5 1.1 %fusion.106 = f32[256,128]{1,0:T(8,128)S(1)} fusion(bf16[256,128]{1,0:T(8,128)(2,1)} %v_ref.1, bf16[256,512]{1,0:T(8,128)(2,1)} %a_ref.1, s32[]{:T(128)S(6)} %select_n.91), kind=kOutput, calls=%fused_computation.130 | convolution fusion | flops 16777216 | bytes 327684 | tf_op jit(solution)/shard_map/dot_general | solution.py:131
  1.6 0.3 %collective-permute-done.1 = bf16[256,128]{1,0:T(8,128)(2,1)S(1)} collective-permute-done((bf16[256,128]{1,0:T(8,128)(2,1)}, bf16[256,128]{1,0:T(8,128)(2,1)S(1)}, u32[]{:S(2)}, u32[]{:S(2)}) %collective-permute-start.1) | collective-permute-done | bytes 65568 | tf_op jit(solution)/shard_map/ppermute | solution.py:104
  1.9 0.0 collective-permute-done
  1.9 0.2 fusion.104
  2.2 0.1 fusion.102
  2.4 0.0 copy-start
  2.4 0.0 copy-start.2
  2.4 3.9 %collective-permute-start.2 = (f16[264,128]{1,0:T(8,128)(2,1)S(1)}, f16[264,128]{1,0:T(8,128)(2,1)S(1)}, u32[]{:S(2)}, u32[]{:S(2)}) collective-permute-start(f16[264,128]{1,0:T(8,128)(2,1)S(1)} %pad_maximum_fusion.3), channel_id=1, source_target_pairs={{0,24},{4,28},{8,16},{12,20},{16,8},{20,12},{24,0},{28,4},{1,25},{... | collective-permute-start | bytes 202760 | tf_op jit(solution)/shard_map/ppermute | solution.py:107
  6.3 0.5 %collective-permute-start.3 = (f16[264,128]{1,0:T(8,128)(2,1)S(1)}, f16[264,128]{1,0:T(8,128)(2,1)S(1)}, u32[]{:S(2)}, u32[]{:S(2)}) collective-permute-start(f16[264,128]{1,0:T(8,128)(2,1)S(1)} %pad_maximum_fusion.3), channel_id=1, source_target_pairs={{0,8},{4,12},{8,0},{12,4},{16,24},{20,28},{24,16},{28,20},{1,9},{5... | collective-permute-start | bytes 202760 | tf_op jit(solution)/shard_map/ppermute | solution.py:107
  6.8 0.1 collective-permute-start.4
  6.9 0.0 copy-done
  7.0 0.0 copy-done.2
  7.0 0.2 fusion.134.y_ref
  7.2 2.0 %collective-permute-start.6 = (bf16[256,128]{1,0:T(8,128)(2,1)S(1)}, bf16[256,128]{1,0:T(8,128)(2,1)S(1)}, u32[]{:S(2)}, u32[]{:S(2)}) collective-permute-start(bf16[256,128]{1,0:T(8,128)(2,1)S(1)} %copy-done), channel_id=1, source_target_pairs={{0,8},{4,12},{8,0},{12,4},{16,24},{20,28},{24,16},{28,20},{1,9},{5... | collective-permute-start | bytes 196616 | tf_op jit(solution)/shard_map/ppermute | solution.py:107
  9.2 0.0 collective-permute-done.2
  9.2 2.1 %collective-permute-done.3 = f16[264,128]{1,0:T(8,128)(2,1)S(1)} collective-permute-done((f16[264,128]{1,0:T(8,128)(2,1)S(1)}, f16[264,128]{1,0:T(8,128)(2,1)S(1)}, u32[]{:S(2)}, u32[]{:S(2)}) %collective-permute-start.3) | collective-permute-done | bytes 67616 | tf_op jit(solution)/shard_map/ppermute | solution.py:107
  11.3 0.0 collective-permute-done.4
  11.3 0.1 divide_bitcast_fusion
  11.4 0.3 %constant_dynamic-update-slice_fusion.1 = (f32[512,128]{1,0:T(8,128)S(1)}, f32[256,128]{1,0:T(8,128)S(1)}) fusion(f32[512,128]{1,0:T(8,128)S(1)} %broadcast_in_dim.38, s32[]{:T(128)S(6)} %select_n.91, f32[128]{0:T(128)S(1)} %get-tuple-element.54, f16[264,128]{1,0:T(8,128)(2,1)S(1)} %collective-permute-done.2, f32[128]{0:T(128)S(1)} %get-tuple-element.53, ...), kind=kLoop, calls=%fused_computation.144 | loop fusion | flops 1966080 | bytes 591364 | tf_op jit(solution)/shard_map/dynamic_update_slice | solution.py:119
  11.7 0.1 fusion.103
  11.8 2.7 %collective-permute-start.8 = (f16[264,128]{1,0:T(8,128)(2,1)S(1)}, f16[264,128]{1,0:T(8,128)(2,1)S(1)}, u32[]{:S(2)}, u32[]{:S(2)}) collective-permute-start(f16[264,128]{1,0:T(8,128)(2,1)S(1)} %pad_maximum_fusion.4), channel_id=1, source_target_pairs={{0,2},{1,3},{2,0},{3,1},{4,6},{5,7},{6,4},{7,5},{8,10},{9,11},{10,... | collective-permute-start | bytes 202760 | tf_op jit(solution)/shard_map/ppermute | solution.py:110
  14.5 0.0 collective-permute-done.6
  14.5 1.4 %collective-permute-start.9 = (f16[264,128]{1,0:T(8,128)(2,1)S(1)}, f16[264,128]{1,0:T(8,128)(2,1)S(1)}, u32[]{:S(2)}, u32[]{:S(2)}) collective-permute-start(f16[264,128]{1,0:T(8,128)(2,1)S(1)} %pad_maximum_fusion.4), channel_id=1, source_target_pairs={{0,3},{1,2},{2,1},{3,0},{4,7},{5,6},{6,5},{7,4},{8,11},{9,10},{10,... | collective-permute-start | bytes 202760 | tf_op jit(solution)/shard_map/ppermute | solution.py:110
  15.9 0.3 %collective-permute-start.5 = (f16[264,128]{1,0:T(8,128)(2,1)S(1)}, f16[264,128]{1,0:T(8,128)(2,1)S(1)}, u32[]{:S(2)}, u32[]{:S(2)}) collective-permute-start(f16[264,128]{1,0:T(8,128)(2,1)S(1)} %pad_maximum_fusion.4), channel_id=1, source_target_pairs={{0,1},{1,0},{2,3},{3,2},{4,5},{5,4},{6,7},{7,6},{8,9},{9,8},{10,11... | collective-permute-start | bytes 202760 | tf_op jit(solution)/shard_map/ppermute | solution.py:110
  16.2 0.9 %collective-permute-start.7 = (bf16[512,128]{1,0:T(8,128)(2,1)S(1)}, bf16[512,128]{1,0:T(8,128)(2,1)S(1)}, u32[]{:S(2)}, u32[]{:S(2)}) collective-permute-start(bf16[512,128]{1,0:T(8,128)(2,1)S(1)} %pad_maximum_fusion.2), channel_id=1, source_target_pairs={{0,16},{4,20},{8,24},{12,28},{16,0},{20,4},{24,8},{28,12},{1,17},{... | collective-permute-start | bytes 393224 | tf_op jit(solution)/shard_map/ppermute | solution.py:107
  17.2 1.8 %collective-permute-done.8 = f16[264,128]{1,0:T(8,128)(2,1)S(1)} collective-permute-done((f16[264,128]{1,0:T(8,128)(2,1)S(1)}, f16[264,128]{1,0:T(8,128)(2,1)S(1)}, u32[]{:S(2)}, u32[]{:S(2)}) %collective-permute-start.8) | collective-permute-done | bytes 67616 | tf_op jit(solution)/shard_map/ppermute | solution.py:110
  19.0 0.0 collective-permute-start.10
  19.0 1.8 %collective-permute-done.9 = f16[264,128]{1,0:T(8,128)(2,1)S(1)} collective-permute-done((f16[264,128]{1,0:T(8,128)(2,1)S(1)}, f16[264,128]{1,0:T(8,128)(2,1)S(1)}, u32[]{:S(2)}, u32[]{:S(2)}) %collective-permute-start.9) | collective-permute-done | bytes 67616 | tf_op jit(solution)/shard_map/ppermute | solution.py:110
  20.8 0.1 fusion.87
  20.9 0.1 fusion.73
  21.0 0.2 collective-permute-done.7
  21.2 0.0 collective-permute-done.5
  21.3 0.1 fusion.101
  21.4 0.4 %fusion.g_ref = f32[128,128]{1,0:T(8,128)S(1)} fusion(f32[256,128]{1,0:T(8,128)S(1)} %fusion.87, f32[256,128]{1,0:T(8,128)S(1)} %fusion.73, f32[256,128]{1,0:T(8,128)S(1)} %get-tuple-element.50, f32[256,128]{1,0:T(8,128)S(1)} %get-tuple-element.32, bf16[256,128]{1,0:T(8,128)(2,1)S(1)} %get-tuple-element.47, bf16[256,128]{1,0:T(8,128)(2,1)S(1)} %get-tuple-element.46, ...), kind=kOutput, calls=%fused_computation | convolution fusion | flops 202768384 | bytes 851968 | tf_op jit(solution)/shard_map/dot_general | solution.py:113
  21.9 0.1 collective-permute-start.11
  22.0 0.0 collective-permute-done.10
  22.0 0.0 copy-start.1
  22.0 0.4 %fusion.135.w_ref = f32[512,128]{1,0:T(8,128)S(1)} fusion(f32[512,128]{1,0:T(8,128)S(1)} %constant_dynamic-update-slice_fusion, f32[128,128]{1,0:T(8,128)S(1)} %copy-done.2), kind=kOutput, calls=%fused_computation.197 | convolution fusion | flops 100663296 | bytes 589824 | tf_op jit(solution)/shard_map/dot_general | solution.py:113
  22.4 1.0 %collective-permute-done.11.rest_0_ = f32[384,128]{1,0:T(8,128)S(1)} collective-permute-done((f32[384,128]{1,0:T(8,128)S(1)}, f32[384,128]{1,0:T(8,128)S(1)}, u32[]{:S(2)}, u32[]{:S(2)}) %collective-permute-start.11) | collective-permute-done | bytes 196640 | tf_op jit(solution)/shard_map/ppermute | solution.py:104
  23.4 0.0 copy-done.1
  23.4 1.4 %shard_map.37 = f32[256,512]{1,0:T(8,128)} custom-call(s32[1]{0:T(128)} %bitcast.h_ref, bf16[256,512]{1,0:T(8,128)(2,1)S(1)} %copy-done.1, bf16[256,128]{1,0:T(8,128)(2,1)S(1)} %copy-done, f32[256,128]{1,0:T(8,128)S(1)} %fusion.134.y_ref, f32[128,128]{1,0:T(8,128)S(1)} %copy-done.2, f32[256,128]{1,0:T(8,128)S(1)} %get-tuple-element.51.p_ref, ...), custom_call_target="tpu_custom_call" | custom-call | flops 134217728 | bytes 786432 | tf_op jit(solution)/shard_map/pallas_call | solution.py:180
  (18 shorter events, 0.3 us)
Async XLA Ops:
  0.0 1.9 %collective-permute-start = (bf16[256,512]{1,0:T(8,128)(2,1)}, bf16[256,512]{1,0:T(8,128)(2,1)S(1)}, u32[]{:S(2)}, u32[]{:S(2)}) collective-permute-start(bf16[256,512]{1,0:T(8,128)(2,1)} %a_ref.1), channel_id=1, source_target_pairs={{0,4},{4,0},{8,12},{12,8},{16,20},{20,16},{24,28},{28,24},{1,5},{5... | collective-permute-start | bytes 786440 | tf_op jit(solution)/shard_map/ppermute | solution.py:104
  0.5 1.5 %collective-permute-start.1 = (bf16[256,128]{1,0:T(8,128)(2,1)}, bf16[256,128]{1,0:T(8,128)(2,1)S(1)}, u32[]{:S(2)}, u32[]{:S(2)}) collective-permute-start(bf16[256,128]{1,0:T(8,128)(2,1)} %v_ref.1), channel_id=1, source_target_pairs={{0,4},{4,0},{8,12},{12,8},{16,20},{20,16},{24,28},{28,24},{1,5},{5... | collective-permute-start | bytes 196616 | tf_op jit(solution)/shard_map/ppermute | solution.py:104
  2.4 4.6 %copy-start = (bf16[256,128]{1,0:T(8,128)(2,1)S(1)}, bf16[256,128]{1,0:T(8,128)(2,1)}, u32[]{:S(2)}) copy-start(bf16[256,128]{1,0:T(8,128)(2,1)} %v_ref.1) | copy-start | bytes 196612
  2.4 4.6 %copy-start.2 = (f32[128,128]{1,0:T(8,128)S(1)}, f32[128,128]{1,0:T(8,128)}, u32[]{:S(2)}) copy-start(f32[128,128]{1,0:T(8,128)} %t_ref.1) | copy-start | bytes 196612
  2.4 6.8 %collective-permute-start.2 = (f16[264,128]{1,0:T(8,128)(2,1)S(1)}, f16[264,128]{1,0:T(8,128)(2,1)S(1)}, u32[]{:S(2)}, u32[]{:S(2)}) collective-permute-start(f16[264,128]{1,0:T(8,128)(2,1)S(1)} %pad_maximum_fusion.3), channel_id=1, source_target_pairs={{0,24},{4,28},{8,16},{12,20},{16,8},{20,12},{24,0},{28,4},{1,25},{... | collective-permute-start | bytes 202760 | tf_op jit(solution)/shard_map/ppermute | solution.py:107
  6.3 4.9 %collective-permute-start.3 = (f16[264,128]{1,0:T(8,128)(2,1)S(1)}, f16[264,128]{1,0:T(8,128)(2,1)S(1)}, u32[]{:S(2)}, u32[]{:S(2)}) collective-permute-start(f16[264,128]{1,0:T(8,128)(2,1)S(1)} %pad_maximum_fusion.3), channel_id=1, source_target_pairs={{0,8},{4,12},{8,0},{12,4},{16,24},{20,28},{24,16},{28,20},{1,9},{5... | collective-permute-start | bytes 202760 | tf_op jit(solution)/shard_map/ppermute | solution.py:107
  6.8 4.4 %collective-permute-start.4 = (f16[264,128]{1,0:T(8,128)(2,1)S(1)}, f16[264,128]{1,0:T(8,128)(2,1)S(1)}, u32[]{:S(2)}, u32[]{:S(2)}) collective-permute-start(f16[264,128]{1,0:T(8,128)(2,1)S(1)} %pad_maximum_fusion.3), channel_id=1, source_target_pairs={{0,16},{4,20},{8,24},{12,28},{16,0},{20,4},{24,8},{28,12},{1,17},{... | collective-permute-start | bytes 202760 | tf_op jit(solution)/shard_map/ppermute | solution.py:107
  7.2 7.3 %collective-permute-start.6 = (bf16[256,128]{1,0:T(8,128)(2,1)S(1)}, bf16[256,128]{1,0:T(8,128)(2,1)S(1)}, u32[]{:S(2)}, u32[]{:S(2)}) collective-permute-start(bf16[256,128]{1,0:T(8,128)(2,1)S(1)} %copy-done), channel_id=1, source_target_pairs={{0,8},{4,12},{8,0},{12,4},{16,24},{20,28},{24,16},{28,20},{1,9},{5... | collective-permute-start | bytes 196616 | tf_op jit(solution)/shard_map/ppermute | solution.py:107
  11.8 7.2 %collective-permute-start.8 = (f16[264,128]{1,0:T(8,128)(2,1)S(1)}, f16[264,128]{1,0:T(8,128)(2,1)S(1)}, u32[]{:S(2)}, u32[]{:S(2)}) collective-permute-start(f16[264,128]{1,0:T(8,128)(2,1)S(1)} %pad_maximum_fusion.4), channel_id=1, source_target_pairs={{0,2},{1,3},{2,0},{3,1},{4,6},{5,7},{6,4},{7,5},{8,10},{9,11},{10,... | collective-permute-start | bytes 202760 | tf_op jit(solution)/shard_map/ppermute | solution.py:110
  14.5 6.3 %collective-permute-start.9 = (f16[264,128]{1,0:T(8,128)(2,1)S(1)}, f16[264,128]{1,0:T(8,128)(2,1)S(1)}, u32[]{:S(2)}, u32[]{:S(2)}) collective-permute-start(f16[264,128]{1,0:T(8,128)(2,1)S(1)} %pad_maximum_fusion.4), channel_id=1, source_target_pairs={{0,3},{1,2},{2,1},{3,0},{4,7},{5,6},{6,5},{7,4},{8,11},{9,10},{10,... | collective-permute-start | bytes 202760 | tf_op jit(solution)/shard_map/ppermute | solution.py:110
  15.9 5.3 %collective-permute-start.5 = (f16[264,128]{1,0:T(8,128)(2,1)S(1)}, f16[264,128]{1,0:T(8,128)(2,1)S(1)}, u32[]{:S(2)}, u32[]{:S(2)}) collective-permute-start(f16[264,128]{1,0:T(8,128)(2,1)S(1)} %pad_maximum_fusion.4), channel_id=1, source_target_pairs={{0,1},{1,0},{2,3},{3,2},{4,5},{5,4},{6,7},{7,6},{8,9},{9,8},{10,11... | collective-permute-start | bytes 202760 | tf_op jit(solution)/shard_map/ppermute | solution.py:110
  16.2 5.0 %collective-permute-start.7 = (bf16[512,128]{1,0:T(8,128)(2,1)S(1)}, bf16[512,128]{1,0:T(8,128)(2,1)S(1)}, u32[]{:S(2)}, u32[]{:S(2)}) collective-permute-start(bf16[512,128]{1,0:T(8,128)(2,1)S(1)} %pad_maximum_fusion.2), channel_id=1, source_target_pairs={{0,16},{4,20},{8,24},{12,28},{16,0},{20,4},{24,8},{28,12},{1,17},{... | collective-permute-start | bytes 393224 | tf_op jit(solution)/shard_map/ppermute | solution.py:107
  19.0 3.0 %collective-permute-start.10 = (f32[256,128]{1,0:T(8,128)S(1)}, f32[256,128]{1,0:T(8,128)S(1)}, u32[]{:S(2)}, u32[]{:S(2)}) collective-permute-start(f32[256,128]{1,0:T(8,128)S(1)} %get-tuple-element.32), channel_id=1, source_target_pairs={{0,4},{4,0},{8,12},{12,8},{16,20},{20,16},{24,28},{28,24},{1,5},{5... | collective-permute-start | bytes 393224 | tf_op jit(solution)/shard_map/ppermute | solution.py:104
  21.9 1.5 %collective-permute-start.11 = (f32[384,128]{1,0:T(8,128)S(1)}, f32[384,128]{1,0:T(8,128)S(1)}, u32[]{:S(2)}, u32[]{:S(2)}) collective-permute-start(f32[384,128]{1,0:T(8,128)S(1)} %pad_maximum_fusion.1), channel_id=1, source_target_pairs={{0,4},{4,0},{8,12},{12,8},{16,20},{20,16},{24,28},{28,24},{1,5},{5... | collective-permute-start | bytes 589832 | tf_op jit(solution)/shard_map/ppermute | solution.py:104
  22.0 1.4 %copy-start.1 = (bf16[256,512]{1,0:T(8,128)(2,1)S(1)}, bf16[256,512]{1,0:T(8,128)(2,1)}, u32[]{:S(2)}) copy-start(bf16[256,512]{1,0:T(8,128)(2,1)} %a_ref.1) | copy-start | bytes 786436

commit v6 on v5

--- a/solution.py
+++ b/solution.py
@@ -68,7 +68,7 @@
     h = h_ref[0]
     gram = g_ref[...]
     for other in others:
-        gram = gram + other[pl.ds(0, band), :]
+        gram = gram + other[pl.ds(0, band), :].astype(jnp.float32) + other[pl.ds(band, band), :].astype(jnp.float32)
     wide = dot3(p_ref[...] - dot3(y_ref[...], gram), t_ref[...])
     high, low = halves(wide)
     left[...] = jnp.concatenate([v_ref[...], v_ref[...], high, low], 1)
@@ -76,7 +76,7 @@
     right[:, 0:band] = high
     right[:, band : 2 * band] = low
     for s in range(q):
-        v = piece_ref[...] if s == 0 else others[s - 1][pl.ds(band, rows), :].astype(jnp.bfloat16)
+        v = piece_ref[...] if s == 0 else others[s - 1][pl.ds(2 * band, rows), :]
         at = pl.ds(pl.multiple_of((h ^ s) * rows, rows), rows)
         right[at, 2 * band : 3 * band] = v
         right[at, 3 * band : 4 * band] = v
@@ -173,7 +173,8 @@
         p_mates = jnp.concatenate([values[s] for s in range(n_col)], 0)
         gram = dot(v_mates.astype(jnp.float32), p_mates, ((0,), (0,)))
         v_piece = tiles[0]
-        packed = jnp.concatenate([gram, v_piece.astype(jnp.float32)], 0)
+        high = lax.reduce_precision(gram, 8, 7)
+        packed = jnp.concatenate([high.astype(jnp.bfloat16), (gram - high).astype(jnp.bfloat16), v_piece], 0)
         received = [member(packed, s) for s in range(1, q)]
         size = 4 * rows * cols + 2 * rows * cols + 16 * band * (rows + 2 * cols) + (q + 4) * 8 * rows * band
         vmem = pl.BlockSpec(memory_space=pltpu.VMEM)

time: 24.9 us -> 24.8 us (level)
  no operation moved by 1% of the time
where the time goes in v6:
time: 24.8 us; the launch traced here: 24.7 us
  starting transfers between devices  12.4 us (50%)
  waiting for transfers between devices  7.09 us (29%)
  matrix products  2.4 us (10%)
  Pallas kernels  1.37 us (6%)
  other arithmetic  1.1 us (4%)
  between operations  0.25 us (1%)
    ppermute x5, starting transfers between devices, group(): return lax.ppermute(x, 'row', [(r, r ^ s * q) for r in range(n_row)])  7.41 us
    ppermute x3, starting transfers between devices, plane(): return lax.ppermute(x, 'col', [(c, c ^ s) for c in range(n_col)])  4.37 us
    ppermute x3, waiting for transfers between devices, plane(): return lax.ppermute(x, 'col', [(c, c ^ s) for c in range(n_col)])  3.59 us
    ppermute x5, waiting for transfers between devices, group(): return lax.ppermute(x, 'row', [(r, r ^ s * q) for r in range(n_row)])  2.29 us
    pallas_call x1, Pallas kernels, shards(): pl.pallas_call(functools.partial(finish, q), out_shape=jax.ShapeDtypeStru...  1.37 us
    dot_general x2, matrix products, chip_part(): lax.dot_general(half, vectors, (((0,), (0,)), ((), ())), preferred_elemen...  1.35 us
    ppermute x4, waiting for transfers between devices, member(): return lax.ppermute(x, 'row', [(r, r ^ s) for r in range(n_row)])  1.2 us
    dot_general x3, matrix products, dot(): lax.dot_general(a, b, (dims, ((), ())), precision=highest, preferred_elem...  1.05 us
  transfers between devices with their start and end apart: 12, of which 6 were waited for; matrix products, arithmetic and copies ran while one was open for 13% of the time, Pallas kernels for 0%

profile of v6, /device:TPU:0, one launch (start us, length us, event | category | flops | bytes accessed | tf_op | source)
XLA Modules:
  0.0 24.7 jit_solution(17329858143196492032)
XLA Ops:
  0.0 0.5 %collective-permute-start = (bf16[256,512]{1,0:T(8,128)(2,1)}, bf16[256,512]{1,0:T(8,128)(2,1)S(1)}, u32[]{:S(2)}, u32[]{:S(2)}) collective-permute-start(bf16[256,512]{1,0:T(8,128)(2,1)} %a_ref.1), channel_id=1, source_target_pairs={{0,4},{4,0},{8,12},{12,8},{16,20},{20,16},{24,28},{28,24},{1,5},{5... | collective-permute-start | bytes 786440 | tf_op jit(solution)/shard_map/ppermute | solution.py:104
  0.5 0.1 collective-permute-start.1
  0.5 1.1 %fusion.106 = f32[256,128]{1,0:T(8,128)S(1)} fusion(bf16[256,128]{1,0:T(8,128)(2,1)} %v_ref.1, bf16[256,512]{1,0:T(8,128)(2,1)} %a_ref.1, s32[]{:T(128)S(6)} %select_n.91), kind=kOutput, calls=%fused_computation.130 | convolution fusion | flops 16777216 | bytes 327684 | tf_op jit(solution)/shard_map/dot_general | solution.py:131
  1.6 0.3 %collective-permute-done.1 = bf16[256,128]{1,0:T(8,128)(2,1)S(1)} collective-permute-done((bf16[256,128]{1,0:T(8,128)(2,1)}, bf16[256,128]{1,0:T(8,128)(2,1)S(1)}, u32[]{:S(2)}, u32[]{:S(2)}) %collective-permute-start.1) | collective-permute-done | bytes 65568 | tf_op jit(solution)/shard_map/ppermute | solution.py:104
  1.9 0.0 collective-permute-done
  1.9 0.2 fusion.104
  2.2 0.1 fusion.102
  2.4 0.0 copy-start
  2.4 0.0 copy-start.2
  2.4 3.9 %collective-permute-start.2 = (f16[264,128]{1,0:T(8,128)(2,1)S(1)}, f16[264,128]{1,0:T(8,128)(2,1)S(1)}, u32[]{:S(2)}, u32[]{:S(2)}) collective-permute-start(f16[264,128]{1,0:T(8,128)(2,1)S(1)} %pad_maximum_fusion.3), channel_id=1, source_target_pairs={{0,24},{4,28},{8,16},{12,20},{16,8},{20,12},{24,0},{28,4},{1,25},{... | collective-permute-start | bytes 202760 | tf_op jit(solution)/shard_map/ppermute | solution.py:107
  6.3 0.5 %collective-permute-start.3 = (f16[264,128]{1,0:T(8,128)(2,1)S(1)}, f16[264,128]{1,0:T(8,128)(2,1)S(1)}, u32[]{:S(2)}, u32[]{:S(2)}) collective-permute-start(f16[264,128]{1,0:T(8,128)(2,1)S(1)} %pad_maximum_fusion.3), channel_id=1, source_target_pairs={{0,8},{4,12},{8,0},{12,4},{16,24},{20,28},{24,16},{28,20},{1,9},{5... | collective-permute-start | bytes 202760 | tf_op jit(solution)/shard_map/ppermute | solution.py:107
  6.8 0.1 collective-permute-start.4
  6.9 0.0 copy-done
  7.0 0.0 copy-done.2
  7.0 0.2 fusion.134.y_ref
  7.2 2.0 %collective-permute-start.6 = (bf16[256,128]{1,0:T(8,128)(2,1)S(1)}, bf16[256,128]{1,0:T(8,128)(2,1)S(1)}, u32[]{:S(2)}, u32[]{:S(2)}) collective-permute-start(bf16[256,128]{1,0:T(8,128)(2,1)S(1)} %copy-done), channel_id=1, source_target_pairs={{0,8},{4,12},{8,0},{12,4},{16,24},{20,28},{24,16},{28,20},{1,9},{5... | collective-permute-start | bytes 196616 | tf_op jit(solution)/shard_map/ppermute | solution.py:107
  9.2 0.0 collective-permute-done.2
  9.2 2.1 %collective-permute-done.3 = f16[264,128]{1,0:T(8,128)(2,1)S(1)} collective-permute-done((f16[264,128]{1,0:T(8,128)(2,1)S(1)}, f16[264,128]{1,0:T(8,128)(2,1)S(1)}, u32[]{:S(2)}, u32[]{:S(2)}) %collective-permute-start.3) | collective-permute-done | bytes 67616 | tf_op jit(solution)/shard_map/ppermute | solution.py:107
  11.3 0.0 collective-permute-done.4
  11.3 0.1 divide_bitcast_fusion
  11.4 0.3 %constant_dynamic-update-slice_fusion.1 = (f32[512,128]{1,0:T(8,128)S(1)}, f32[256,128]{1,0:T(8,128)S(1)}) fusion(f32[512,128]{1,0:T(8,128)S(1)} %broadcast_in_dim.38, s32[]{:T(128)S(6)} %select_n.91, f32[128]{0:T(128)S(1)} %get-tuple-element.51, f16[264,128]{1,0:T(8,128)(2,1)S(1)} %collective-permute-done.2, f32[128]{0:T(128)S(1)} %get-tuple-element.50, ...), kind=kLoop, calls=%fused_computation.147 | loop fusion | flops 1966080 | bytes 591364 | tf_op jit(solution)/shard_map/dynamic_update_slice | solution.py:119
  11.7 0.1 fusion.103
  11.8 2.7 %collective-permute-start.8 = (f16[264,128]{1,0:T(8,128)(2,1)S(1)}, f16[264,128]{1,0:T(8,128)(2,1)S(1)}, u32[]{:S(2)}, u32[]{:S(2)}) collective-permute-start(f16[264,128]{1,0:T(8,128)(2,1)S(1)} %pad_maximum_fusion.4), channel_id=1, source_target_pairs={{0,2},{1,3},{2,0},{3,1},{4,6},{5,7},{6,4},{7,5},{8,10},{9,11},{10,... | collective-permute-start | bytes 202760 | tf_op jit(solution)/shard_map/ppermute | solution.py:110
  14.5 0.0 collective-permute-done.6
  14.5 1.4 %collective-permute-start.9 = (f16[264,128]{1,0:T(8,128)(2,1)S(1)}, f16[264,128]{1,0:T(8,128)(2,1)S(1)}, u32[]{:S(2)}, u32[]{:S(2)}) collective-permute-start(f16[264,128]{1,0:T(8,128)(2,1)S(1)} %pad_maximum_fusion.4), channel_id=1, source_target_pairs={{0,3},{1,2},{2,1},{3,0},{4,7},{5,6},{6,5},{7,4},{8,11},{9,10},{10,... | collective-permute-start | bytes 202760 | tf_op jit(solution)/shard_map/ppermute | solution.py:110
  15.9 0.3 %collective-permute-start.5 = (f16[264,128]{1,0:T(8,128)(2,1)S(1)}, f16[264,128]{1,0:T(8,128)(2,1)S(1)}, u32[]{:S(2)}, u32[]{:S(2)}) collective-permute-start(f16[264,128]{1,0:T(8,128)(2,1)S(1)} %pad_maximum_fusion.4), channel_id=1, source_target_pairs={{0,1},{1,0},{2,3},{3,2},{4,5},{5,4},{6,7},{7,6},{8,9},{9,8},{10,11... | collective-permute-start | bytes 202760 | tf_op jit(solution)/shard_map/ppermute | solution.py:110
  16.2 0.9 %collective-permute-start.7 = (bf16[512,128]{1,0:T(8,128)(2,1)S(1)}, bf16[512,128]{1,0:T(8,128)(2,1)S(1)}, u32[]{:S(2)}, u32[]{:S(2)}) collective-permute-start(bf16[512,128]{1,0:T(8,128)(2,1)S(1)} %pad_maximum_fusion.1), channel_id=1, source_target_pairs={{0,16},{4,20},{8,24},{12,28},{16,0},{20,4},{24,8},{28,12},{1,17},{... | collective-permute-start | bytes 393224 | tf_op jit(solution)/shard_map/ppermute | solution.py:107
  17.2 1.8 %collective-permute-done.8 = f16[264,128]{1,0:T(8,128)(2,1)S(1)} collective-permute-done((f16[264,128]{1,0:T(8,128)(2,1)S(1)}, f16[264,128]{1,0:T(8,128)(2,1)S(1)}, u32[]{:S(2)}, u32[]{:S(2)}) %collective-permute-start.8) | collective-permute-done | bytes 67616 | tf_op jit(solution)/shard_map/ppermute | solution.py:110
  19.0 0.0 collective-permute-start.10
  19.0 1.8 %collective-permute-done.9 = f16[264,128]{1,0:T(8,128)(2,1)S(1)} collective-permute-done((f16[264,128]{1,0:T(8,128)(2,1)S(1)}, f16[264,128]{1,0:T(8,128)(2,1)S(1)}, u32[]{:S(2)}, u32[]{:S(2)}) %collective-permute-start.9) | collective-permute-done | bytes 67616 | tf_op jit(solution)/shard_map/ppermute | solution.py:110
  20.8 0.1 fusion.87
  20.9 0.1 fusion.73
  21.0 0.2 collective-permute-done.7
  21.2 0.0 collective-permute-done.5
  21.3 0.1 fusion.101
  21.4 0.4 %reduce-precision_convert_fusion = (bf16[128,128]{1,0:T(8,128)(2,1)S(1)}, bf16[128,128]{1,0:T(8,128)(2,1)S(1)}, f32[128,128]{1,0:T(8,128)S(1)}) fusion(f32[256,128]{1,0:T(8,128)S(1)} %fusion.87, f32[256,128]{1,0:T(8,128)S(1)} %fusion.73, f32[256,128]{1,0:T(8,128)S(1)} %get-tuple-element.47, f32[256,128]{1,0:T(8,128)S(1)} %get-tuple-element.32, ...), kind=kOutput, calls=%fused_computation.134 | convolution fusion | flops 202833920 | bytes 917504 | tf_op jit(solution)/shard_map/dot_general | solution.py:113
  21.9 0.1 collective-permute-start.11
  22.0 0.0 collective-permute-done.10
  22.0 0.0 copy-start.1
  22.0 0.4 %fusion.135.w_ref = f32[512,128]{1,0:T(8,128)S(1)} fusion(f32[512,128]{1,0:T(8,128)S(1)} %constant_dynamic-update-slice_fusion, f32[128,128]{1,0:T(8,128)S(1)} %copy-done.2), kind=kOutput, calls=%fused_computation.199 | convolution fusion | flops 100663296 | bytes 589824 | tf_op jit(solution)/shard_map/dot_general | solution.py:113
  22.4 0.9 %collective-permute-done.11.rest_0_ = bf16[512,128]{1,0:T(8,128)(2,1)S(1)} collective-permute-done((bf16[512,128]{1,0:T(8,128)(2,1)S(1)}, bf16[512,128]{1,0:T(8,128)(2,1)S(1)}, u32[]{:S(2)}, u32[]{:S(2)}) %collective-permute-start.11) | collective-permute-done | bytes 131104 | tf_op jit(solution)/shard_map/ppermute | solution.py:104
  23.3 0.0 copy-done.1
  23.3 1.4 %shard_map.37 = f32[256,512]{1,0:T(8,128)} custom-call(s32[1]{0:T(128)} %bitcast.h_ref, bf16[256,512]{1,0:T(8,128)(2,1)S(1)} %copy-done.1, bf16[256,128]{1,0:T(8,128)(2,1)S(1)} %copy-done, f32[256,128]{1,0:T(8,128)S(1)} %fusion.134.y_ref, f32[128,128]{1,0:T(8,128)S(1)} %copy-done.2, f32[256,128]{1,0:T(8,128)S(1)} %get-tuple-element.48.p_ref, ...), custom_call_target="tpu_custom_call" | custom-call | flops 134217728 | bytes 786432 | tf_op jit(solution)/shard_map/pallas_call | solution.py:181
  (18 shorter events, 0.3 us)
Async XLA Ops:
  0.0 1.9 %collective-permute-start = (bf16[256,512]{1,0:T(8,128)(2,1)}, bf16[256,512]{1,0:T(8,128)(2,1)S(1)}, u32[]{:S(2)}, u32[]{:S(2)}) collective-permute-start(bf16[256,512]{1,0:T(8,128)(2,1)} %a_ref.1), channel_id=1, source_target_pairs={{0,4},{4,0},{8,12},{12,8},{16,20},{20,16},{24,28},{28,24},{1,5},{5... | collective-permute-start | bytes 786440 | tf_op jit(solution)/shard_map/ppermute | solution.py:104
  0.5 1.5 %collective-permute-start.1 = (bf16[256,128]{1,0:T(8,128)(2,1)}, bf16[256,128]{1,0:T(8,128)(2,1)S(1)}, u32[]{:S(2)}, u32[]{:S(2)}) collective-permute-start(bf16[256,128]{1,0:T(8,128)(2,1)} %v_ref.1), channel_id=1, source_target_pairs={{0,4},{4,0},{8,12},{12,8},{16,20},{20,16},{24,28},{28,24},{1,5},{5... | collective-permute-start | bytes 196616 | tf_op jit(solution)/shard_map/ppermute | solution.py:104
  2.4 4.6 %copy-start = (bf16[256,128]{1,0:T(8,128)(2,1)S(1)}, bf16[256,128]{1,0:T(8,128)(2,1)}, u32[]{:S(2)}) copy-start(bf16[256,128]{1,0:T(8,128)(2,1)} %v_ref.1) | copy-start | bytes 196612
  2.4 4.6 %copy-start.2 = (f32[128,128]{1,0:T(8,128)S(1)}, f32[128,128]{1,0:T(8,128)}, u32[]{:S(2)}) copy-start(f32[128,128]{1,0:T(8,128)} %t_ref.1) | copy-start | bytes 196612
  2.4 6.8 %collective-permute-start.2 = (f16[264,128]{1,0:T(8,128)(2,1)S(1)}, f16[264,128]{1,0:T(8,128)(2,1)S(1)}, u32[]{:S(2)}, u32[]{:S(2)}) collective-permute-start(f16[264,128]{1,0:T(8,128)(2,1)S(1)} %pad_maximum_fusion.3), channel_id=1, source_target_pairs={{0,24},{4,28},{8,16},{12,20},{16,8},{20,12},{24,0},{28,4},{1,25},{... | collective-permute-start | bytes 202760 | tf_op jit(solution)/shard_map/ppermute | solution.py:107
  6.3 4.9 %collective-permute-start.3 = (f16[264,128]{1,0:T(8,128)(2,1)S(1)}, f16[264,128]{1,0:T(8,128)(2,1)S(1)}, u32[]{:S(2)}, u32[]{:S(2)}) collective-permute-start(f16[264,128]{1,0:T(8,128)(2,1)S(1)} %pad_maximum_fusion.3), channel_id=1, source_target_pairs={{0,8},{4,12},{8,0},{12,4},{16,24},{20,28},{24,16},{28,20},{1,9},{5... | collective-permute-start | bytes 202760 | tf_op jit(solution)/shard_map/ppermute | solution.py:107
  6.8 4.4 %collective-permute-start.4 = (f16[264,128]{1,0:T(8,128)(2,1)S(1)}, f16[264,128]{1,0:T(8,128)(2,1)S(1)}, u32[]{:S(2)}, u32[]{:S(2)}) collective-permute-start(f16[264,128]{1,0:T(8,128)(2,1)S(1)} %pad_maximum_fusion.3), channel_id=1, source_target_pairs={{0,16},{4,20},{8,24},{12,28},{16,0},{20,4},{24,8},{28,12},{1,17},{... | collective-permute-start | bytes 202760 | tf_op jit(solution)/shard_map/ppermute | solution.py:107
  7.2 7.3 %collective-permute-start.6 = (bf16[256,128]{1,0:T(8,128)(2,1)S(1)}, bf16[256,128]{1,0:T(8,128)(2,1)S(1)}, u32[]{:S(2)}, u32[]{:S(2)}) collective-permute-start(bf16[256,128]{1,0:T(8,128)(2,1)S(1)} %copy-done), channel_id=1, source_target_pairs={{0,8},{4,12},{8,0},{12,4},{16,24},{20,28},{24,16},{28,20},{1,9},{5... | collective-permute-start | bytes 196616 | tf_op jit(solution)/shard_map/ppermute | solution.py:107
  11.8 7.2 %collective-permute-start.8 = (f16[264,128]{1,0:T(8,128)(2,1)S(1)}, f16[264,128]{1,0:T(8,128)(2,1)S(1)}, u32[]{:S(2)}, u32[]{:S(2)}) collective-permute-start(f16[264,128]{1,0:T(8,128)(2,1)S(1)} %pad_maximum_fusion.4), channel_id=1, source_target_pairs={{0,2},{1,3},{2,0},{3,1},{4,6},{5,7},{6,4},{7,5},{8,10},{9,11},{10,... | collective-permute-start | bytes 202760 | tf_op jit(solution)/shard_map/ppermute | solution.py:110
  14.5 6.3 %collective-permute-start.9 = (f16[264,128]{1,0:T(8,128)(2,1)S(1)}, f16[264,128]{1,0:T(8,128)(2,1)S(1)}, u32[]{:S(2)}, u32[]{:S(2)}) collective-permute-start(f16[264,128]{1,0:T(8,128)(2,1)S(1)} %pad_maximum_fusion.4), channel_id=1, source_target_pairs={{0,3},{1,2},{2,1},{3,0},{4,7},{5,6},{6,5},{7,4},{8,11},{9,10},{10,... | collective-permute-start | bytes 202760 | tf_op jit(solution)/shard_map/ppermute | solution.py:110
  15.9 5.3 %collective-permute-start.5 = (f16[264,128]{1,0:T(8,128)(2,1)S(1)}, f16[264,128]{1,0:T(8,128)(2,1)S(1)}, u32[]{:S(2)}, u32[]{:S(2)}) collective-permute-start(f16[264,128]{1,0:T(8,128)(2,1)S(1)} %pad_maximum_fusion.4), channel_id=1, source_target_pairs={{0,1},{1,0},{2,3},{3,2},{4,5},{5,4},{6,7},{7,6},{8,9},{9,8},{10,11... | collective-permute-start | bytes 202760 | tf_op jit(solution)/shard_map/ppermute | solution.py:110
  16.2 5.0 %collective-permute-start.7 = (bf16[512,128]{1,0:T(8,128)(2,1)S(1)}, bf16[512,128]{1,0:T(8,128)(2,1)S(1)}, u32[]{:S(2)}, u32[]{:S(2)}) collective-permute-start(bf16[512,128]{1,0:T(8,128)(2,1)S(1)} %pad_maximum_fusion.1), channel_id=1, source_target_pairs={{0,16},{4,20},{8,24},{12,28},{16,0},{20,4},{24,8},{28,12},{1,17},{... | collective-permute-start | bytes 393224 | tf_op jit(solution)/shard_map/ppermute | solution.py:107
  19.0 3.0 %collective-permute-start.10 = (f32[256,128]{1,0:T(8,128)S(1)}, f32[256,128]{1,0:T(8,128)S(1)}, u32[]{:S(2)}, u32[]{:S(2)}) collective-permute-start(f32[256,128]{1,0:T(8,128)S(1)} %get-tuple-element.32), channel_id=1, source_target_pairs={{0,4},{4,0},{8,12},{12,8},{16,20},{20,16},{24,28},{28,24},{1,5},{5... | collective-permute-start | bytes 393224 | tf_op jit(solution)/shard_map/ppermute | solution.py:104
  21.9 1.4 %collective-permute-start.11 = (bf16[512,128]{1,0:T(8,128)(2,1)S(1)}, bf16[512,128]{1,0:T(8,128)(2,1)S(1)}, u32[]{:S(2)}, u32[]{:S(2)}) collective-permute-start(bf16[512,128]{1,0:T(8,128)(2,1)S(1)} %pad_maximum_fusion.2), channel_id=1, source_target_pairs={{0,4},{4,0},{8,12},{12,8},{16,20},{20,16},{24,28},{28,24},{1,5},{5... | collective-permute-start | bytes 393224 | tf_op jit(solution)/shard_map/ppermute | solution.py:104
  22.0 1.3 %copy-start.1 = (bf16[256,512]{1,0:T(8,128)(2,1)S(1)}, bf16[256,512]{1,0:T(8,128)(2,1)}, u32[]{:S(2)}) copy-start(bf16[256,512]{1,0:T(8,128)(2,1)} %a_ref.1) | copy-start | bytes 786436

commit v7 on v6

--- a/solution.py
+++ b/solution.py
@@ -1,4 +1,5 @@
 import functools
+import itertools
 
 import jax
 import jax.numpy as jnp
@@ -11,6 +12,11 @@
 LEAST = -100.0
 TILE = 8
 CHUNKS = 2
+SOURCES = (
+    (((0, 3), (3, 2), (0, 0), (0, 1)), ((1, 1), (1, 2), (1, 3), (0, 2)), ((2, 2), (3, 0), (2, 0), (3, 1)), ((3, 3), (2, 3), (1, 0), (2, 1))),
+    (((0, 2), (1, 0), (0, 3), (1, 2)), ((1, 3), (0, 0), (0, 1), (1, 1)), ((2, 3), (3, 3), (3, 1), (2, 2)), ((3, 2), (2, 0), (2, 1), (3, 0))),
+    (((0, 1), (0, 3), (1, 1), (0, 0)), ((1, 2), (1, 3), (3, 0), (1, 0)), ((3, 1), (0, 2), (2, 3), (2, 0)), ((2, 1), (2, 2), (3, 3), (3, 2))),
+)
 
 
 def scale_of(ratio, exponent):
@@ -98,6 +104,7 @@
 def solution(mesh):
     n_row, n_col = mesh.shape["row"], mesh.shape["col"]
     q = n_row // n_col
+    paired = q == 2 and n_col == 4
     highest = lax.Precision.HIGHEST
 
     def member(x, s):
@@ -106,11 +113,30 @@
     def group(x, s):
         return lax.ppermute(x, "row", [(r, r ^ (s * q)) for r in range(n_row)])
 
+    def source(s, k, c):
+        return SOURCES[s - 1][k][c] if n_col == len(SOURCES) + 1 else (k, c ^ s)
+
     def plane(x, s):
-        return lax.ppermute(x, "col", [(c, c ^ s) for c in range(n_col)])
+        pairs = []
+        for k, h, c in itertools.product(range(n_col), range(q), range(n_col)):
+            j, d = source(s, k, c)
+            pairs.append(((j * q + h) * n_col + d, (k * q + h) * n_col + c))
+        return lax.ppermute(x, ("row", "col"), pairs)
+
+    def origin(s, k, c):
+        bits = n_col.bit_length()
+        word = jnp.int32(0)
+        for i in range(n_col):
+            code = sum(source(s, i, j)[1] << (bits * j) for j in range(n_col))
+            word = jnp.where(k == i, jnp.int32(code), word)
+        return jnp.bitwise_and(lax.shift_right_logical(word, bits * c), (1 << bits) - 1)
+
 
     def dot(a, b, dims):
         return lax.dot_general(a, b, (dims, ((), ())), precision=highest, preferred_element_type=jnp.float32)
+
+    def by_index(pieces, me):
+        return [jnp.where(me == 0, pieces[s], pieces[1 - s]) for s in range(2)]
 
     def placed(pieces, me):
         rows = pieces[0].shape[0]
@@ -124,7 +150,7 @@
         band = reflectors.shape[1]
         row, c = lax.axis_index("row"), lax.axis_index("col")
         k, h = lax.div(row, q), lax.rem(row, q)
-        y_rows = dot(reflectors.astype(jnp.float32), factor, ((1,), (1,)))
+        came = [c] + [origin(s, k, c) for s in range(1, n_col)]
 
         def chip_part(tile, vectors):
             half = lax.dynamic_slice_in_dim(tile, h * rows, rows, 1)
@@ -136,23 +162,34 @@
             piece = piece + chip_part(tile, vectors)
         message = encode(piece, jnp.max(jnp.abs(piece), axis=0, keepdims=True))
         top = scale_in(message)
-        others = [group(message, s) for s in range(1, n_col)]
-        pieces, _ = lax.optimization_barrier((reflectors, message))
-        pieces = jnp.concatenate([pieces, group(pieces, 1)], 0)
+        others = [group(message, s) for s in reversed(range(1, n_col))]
+        held, _ = lax.optimization_barrier((reflectors, message))
+        y_rows = dot(held.astype(jnp.float32), factor, ((1,), (1,)))
+        held, _ = lax.optimization_barrier((reflectors, message))
+        if paired:
+            pair, _ = lax.optimization_barrier((jnp.concatenate(by_index([reflectors, vectors], h), 0), message))
+            near = lax.ppermute(
+                pair, "row", [(k * q + h, (k ^ (1 << h)) * q + h) for k in range(n_col) for h in range(q)]
+            )
+            far = group(held, 3)
+        else:
+            got = [group(held, s) for s in range(1, n_col)]
         total, others[-1], y_rows = lax.optimization_barrier((piece, others[-1], y_rows))
         for other in others:
             total = total + decode(other)
             top = top + scale_in(other)
         message = encode(total, top)
-        step = 2
-        while step < n_col:
-            held, _ = lax.optimization_barrier((pieces, message))
-            pieces = jnp.concatenate([pieces, group(held, step)], 0)
-            step *= 2
-        order = sorted(range(1, n_col), key=lambda s: (s < n_col // 2, s))
+        order = list(range(1, n_col))
         mates = {s: plane(message, s) for s in order}
-        held, _ = lax.optimization_barrier((total, mates[order[0]]))
-        p_cols = placed([total] + [member(held, s) for s in range(1, q)], h)
+        if paired:
+            mine = lax.dynamic_slice_in_dim(near, h * rows, rows, 0)
+            theirs = lax.dynamic_slice_in_dim(near, (1 - h) * rows, rows, 0)
+            received = member(jnp.concatenate([total, theirs.astype(jnp.float32)], 0), 1)
+            p_cols = placed([total, received[:rows]], h)
+            got = by_index([mine, received[rows:].astype(jnp.bfloat16)], h) + [far]
+        else:
+            p_cols = placed([total] + [member(total, s) for s in range(1, q)], h)
+        pieces = jnp.concatenate([reflectors] + got, 0)
         w_cols = dot(p_cols, factor, ((1,), (0,)))
         values = {0: total}
         for s in order[:-1]:
@@ -160,16 +197,17 @@
             values[s] = decode(mate)
         last, pieces, values = lax.optimization_barrier((mates[order[-1]], pieces, values))
         values[order[-1]] = decode(last)
-        tiles = jnp.split(pieces, n_col, 0)
-        bit = 1
-        while bit < n_col:
-            swap = ((k ^ c) & bit) != 0
-            tiles = [jnp.where(swap, tiles[s ^ bit], tiles[s]) for s in range(n_col)]
-            bit *= 2
+        pieces = jnp.split(pieces, n_col, 0)
+        tiles = []
+        for s in range(n_col):
+            tile = pieces[0]
+            for t in range(1, n_col):
+                tile = jnp.where((k ^ t) == came[s], pieces[t], tile)
+            tiles.append(tile)
         v_mates = jnp.concatenate(tiles, 0)
         p_rows = total
         for s in order:
-            p_rows = jnp.where((k ^ c) == s, values[s], p_rows)
+            p_rows = jnp.where(came[s] == k, values[s], p_rows)
         p_mates = jnp.concatenate([values[s] for s in range(n_col)], 0)
         gram = dot(v_mates.astype(jnp.float32), p_mates, ((0,), (0,)))
         v_piece = tiles[0]

time: 24.8 us -> 24.4 us (0.984)
  waiting for transfers between devices: 7.09 us -> 4.11 us
  starting transfers between devices: 12.4 us -> 14.7 us
    ppermute x3 -> x4, starting transfers between devices: 4.37 us -> 6.61 us  [the longest x3 6.01 us: plane(): return lax.ppermute(x, ('row', 'col'), pairs)]
    ppermute x3 -> x4, waiting for transfers between devices: 3.59 us -> 2.02 us  [the longest x3 2.02 us: plane(): return lax.ppermute(x, ('row', 'col'), pairs)]
    ppermute x5 -> x4, waiting for transfers between devices: 2.29 us -> 0.97 us  [group(): return lax.ppermute(x, 'row', [(r, r ^ s * q) for r in range(n_row)])]
    ppermute x5 -> x4, starting transfers between devices: 7.41 us -> 7.43 us  [group(): return lax.ppermute(x, 'row', [(r, r ^ s * q) for r in range(n_row)])]
  transfers between devices with their start and end apart: 12 -> 12, of which waited for: 6 -> 4; matrix products, arithmetic and copies ran while one was open for 13% -> 11% of each run, Pallas kernels for 0% -> 0%
where the time goes in v7:
time: 24.4 us; the launch traced here: 24.2 us
  starting transfers between devices  14.7 us (60%)
  waiting for transfers between devices  4.11 us (17%)
  matrix products  2.4 us (10%)
  Pallas kernels  1.37 us (6%)
  other arithmetic  1.21 us (5%)
  between operations  0.37 us (2%)
    ppermute x4, starting transfers between devices, group(): return lax.ppermute(x, 'row', [(r, r ^ s * q) for r in range(n_row)])  7.43 us
    ppermute x3, starting transfers between devices, plane(): return lax.ppermute(x, ('row', 'col'), pairs)  6.01 us
    ppermute x3, waiting for transfers between devices, plane(): return lax.ppermute(x, ('row', 'col'), pairs)  2.02 us
    pallas_call x1, Pallas kernels, shards(): pl.pallas_call(functools.partial(finish, q), out_shape=jax.ShapeDtypeStru...  1.37 us
    dot_general x2, matrix products, chip_part(): lax.dot_general(half, vectors, (((0,), (0,)), ((), ())), preferred_elemen...  1.35 us
    ppermute x4, waiting for transfers between devices, member(): return lax.ppermute(x, 'row', [(r, r ^ s) for r in range(n_row)])  1.12 us
    dot_general x3, matrix products, dot(): lax.dot_general(a, b, (dims, ((), ())), precision=highest, preferred_elem...  1.05 us
    ppermute x4, waiting for transfers between devices, group(): return lax.ppermute(x, 'row', [(r, r ^ s * q) for r in range(n_row)])  0.97 us
  transfers between devices with their start and end apart: 12, of which 4 were waited for; matrix products, arithmetic and copies ran while one was open for 11% of the time, Pallas kernels for 0%

profile of v7, /device:TPU:0, one launch (start us, length us, event | category | flops | bytes accessed | tf_op | source)
XLA Modules:
  0.0 24.2 jit_solution(1703102291034813069)
XLA Ops:
  0.0 0.5 %collective-permute-start = (bf16[256,512]{1,0:T(8,128)(2,1)}, bf16[256,512]{1,0:T(8,128)(2,1)S(1)}, u32[]{:S(2)}, u32[]{:S(2)}) collective-permute-start(bf16[256,512]{1,0:T(8,128)(2,1)} %a_ref.1), channel_id=1, source_target_pairs={{0,4},{4,0},{8,12},{12,8},{16,20},{20,16},{24,28},{28,24},{1,5},{5... | collective-permute-start | bytes 786440 | tf_op jit(solution)/shard_map/ppermute | solution.py:111
  0.5 0.1 collective-permute-start.1
  0.5 1.1 %fusion.106 = f32[256,128]{1,0:T(8,128)S(1)} fusion(bf16[256,128]{1,0:T(8,128)(2,1)} %v_ref.1, bf16[256,512]{1,0:T(8,128)(2,1)} %a_ref.1, s32[]{:T(128)S(6)} %select_n.186), kind=kOutput, calls=%fused_computation.133 | convolution fusion | flops 16777216 | bytes 327684 | tf_op jit(solution)/shard_map/dot_general | solution.py:157
  1.7 0.2 collective-permute-done.1
  1.9 0.0 collective-permute-done
  1.9 0.2 fusion.104
  2.2 0.1 fusion.102
  2.4 0.0 copy-start
  2.4 0.0 copy-start.2
  2.4 3.0 %collective-permute-start.4 = (f16[264,128]{1,0:T(8,128)(2,1)S(1)}, f16[264,128]{1,0:T(8,128)(2,1)S(1)}, u32[]{:S(2)}, u32[]{:S(2)}) collective-permute-start(f16[264,128]{1,0:T(8,128)(2,1)S(1)} %pad_maximum_fusion.4), channel_id=1, source_target_pairs={{0,16},{4,20},{8,24},{12,28},{16,0},{20,4},{24,8},{28,12},{1,17},{... | collective-permute-start | bytes 202760 | tf_op jit(solution)/shard_map/ppermute | solution.py:114
  5.4 1.4 %collective-permute-start.3 = (f16[264,128]{1,0:T(8,128)(2,1)S(1)}, f16[264,128]{1,0:T(8,128)(2,1)S(1)}, u32[]{:S(2)}, u32[]{:S(2)}) collective-permute-start(f16[264,128]{1,0:T(8,128)(2,1)S(1)} %pad_maximum_fusion.4), channel_id=1, source_target_pairs={{0,24},{4,28},{8,16},{12,20},{16,8},{20,12},{24,0},{28,4},{1,25},{... | collective-permute-start | bytes 202760 | tf_op jit(solution)/shard_map/ppermute | solution.py:114
  6.8 0.1 collective-permute-start.2
  6.9 0.0 copy-done
  6.9 2.9 %collective-permute-start.8 = (bf16[256,128]{1,0:T(8,128)(2,1)S(1)}, bf16[256,128]{1,0:T(8,128)(2,1)S(1)}, u32[]{:S(2)}, u32[]{:S(2)}) collective-permute-start(bf16[256,128]{1,0:T(8,128)(2,1)S(1)} %copy-done), channel_id=1, source_target_pairs={{0,24},{4,28},{8,16},{12,20},{16,8},{20,12},{24,0},{28,4},{1,25},{... | collective-permute-start | bytes 196616 | tf_op jit(solution)/shard_map/ppermute | solution.py:114
  9.9 0.0 copy-done.2
  9.9 0.2 fusion.134.y_ref
  10.1 0.6 %collective-permute-start.6 = (bf16[512,128]{1,0:T(8,128)(2,1)S(1)}, bf16[512,128]{1,0:T(8,128)(2,1)S(1)}, u32[]{:S(2)}, u32[]{:S(2)}) collective-permute-start(bf16[512,128]{1,0:T(8,128)(2,1)S(1)} %pad_maximum_fusion.2), channel_id=1, source_target_pairs={{0,8},{4,20},{8,0},{12,28},{16,24},{20,4},{24,16},{28,12},{1,9},{5... | collective-permute-start | bytes 393224 | tf_op jit(solution)/shard_map/ppermute | solution.py:171
  10.8 1.0 %collective-permute-done.2 = f16[264,128]{1,0:T(8,128)(2,1)S(1)} collective-permute-done((f16[264,128]{1,0:T(8,128)(2,1)S(1)}, f16[264,128]{1,0:T(8,128)(2,1)S(1)}, u32[]{:S(2)}, u32[]{:S(2)}) %collective-permute-start.2) | collective-permute-done | bytes 67616 | tf_op jit(solution)/shard_map/ppermute | solution.py:114
  11.7 0.0 collective-permute-done.4
  11.7 0.0 collective-permute-done.3
  11.7 0.1 divide_bitcast_fusion
  11.8 0.3 %constant_dynamic-update-slice_fusion = (f32[512,128]{1,0:T(8,128)S(1)}, f32[256,128]{1,0:T(8,128)S(1)}) fusion(f32[512,128]{1,0:T(8,128)S(1)} %broadcast_in_dim.38, s32[]{:T(128)S(6)} %select_n.186, f32[128]{0:T(128)S(1)} %get-tuple-element.53, f16[264,128]{1,0:T(8,128)(2,1)S(1)} %collective-permute-done.2, f32[128]{0:T(128)S(1)} %get-tuple-element.52, ...), kind=kLoop, calls=%fused_computation.150 | loop fusion | flops 1966080 | bytes 591364 | tf_op jit(solution)/shard_map/dynamic_update_slice | solution.py:145
  12.1 0.1 fusion.103
  12.3 2.2 %collective-permute-start.10 = (f16[264,128]{1,0:T(8,128)(2,1)S(1)}, f16[264,128]{1,0:T(8,128)(2,1)S(1)}, u32[]{:S(2)}, u32[]{:S(2)}) collective-permute-start(f16[264,128]{1,0:T(8,128)(2,1)S(1)} %pad_maximum_fusion.5), channel_id=1, source_target_pairs={{2,0},{8,1},{3,2},{10,3},{6,4},{12,5},{7,6},{14,7},{11,8},{0,9},{1... | collective-permute-start | bytes 202760 | tf_op jit(solution)/shard_map/ppermute | solution.py:124
  14.5 0.8 %collective-permute-start.9 = (f16[264,128]{1,0:T(8,128)(2,1)S(1)}, f16[264,128]{1,0:T(8,128)(2,1)S(1)}, u32[]{:S(2)}, u32[]{:S(2)}) collective-permute-start(f16[264,128]{1,0:T(8,128)(2,1)S(1)} %pad_maximum_fusion.5), channel_id=1, source_target_pairs={{3,0},{26,1},{0,2},{1,3},{7,4},{30,5},{4,6},{5,7},{9,8},{10,9},{11... | collective-permute-start | bytes 202760 | tf_op jit(solution)/shard_map/ppermute | solution.py:124
  15.3 3.0 %collective-permute-start.5 = (f16[264,128]{1,0:T(8,128)(2,1)S(1)}, f16[264,128]{1,0:T(8,128)(2,1)S(1)}, u32[]{:S(2)}, u32[]{:S(2)}) collective-permute-start(f16[264,128]{1,0:T(8,128)(2,1)S(1)} %pad_maximum_fusion.5), channel_id=1, source_target_pairs={{1,0},{3,1},{9,2},{0,3},{5,4},{7,5},{13,6},{4,7},{10,8},{11,9},{24... | collective-permute-start | bytes 202760 | tf_op jit(solution)/shard_map/ppermute | solution.py:124
  18.3 0.0 collective-permute-done.6
  18.4 0.1 collective-permute-start.7
  18.4 0.0 collective-permute-done.10
  18.5 0.1 fusion.87
  18.6 2.0 %collective-permute-done.9 = f16[264,128]{1,0:T(8,128)(2,1)S(1)} collective-permute-done((f16[264,128]{1,0:T(8,128)(2,1)S(1)}, f16[264,128]{1,0:T(8,128)(2,1)S(1)}, u32[]{:S(2)}, u32[]{:S(2)}) %collective-permute-start.9) | collective-permute-done | bytes 67616 | tf_op jit(solution)/shard_map/ppermute | solution.py:124
  20.6 0.1 fusion.73
  20.7 0.0 collective-permute-done.7
  20.7 0.0 collective-permute-done.8
  20.8 0.0 collective-permute-done.5
  20.9 0.1 fusion.101
  21.0 0.4 %reduce-precision_convert_fusion = (bf16[128,128]{1,0:T(8,128)(2,1)S(1)}, bf16[128,128]{1,0:T(8,128)(2,1)S(1)}, f32[128,128]{1,0:T(8,128)S(1)}) fusion(f32[256,128]{1,0:T(8,128)S(1)} %get-tuple-element.49, f32[256,128]{1,0:T(8,128)S(1)} %fusion.87, f32[256,128]{1,0:T(8,128)S(1)} %fusion.73, f32[256,128]{1,0:T(8,128)S(1)} %get-tuple-element.30, ...), kind=kOutput, calls=%fused_computation.137 | convolution fusion | flops 202833920 | bytes 917504 | tf_op jit(solution)/shard_map/dot_general | solution.py:136
  21.5 0.1 collective-permute-start.11
  21.6 0.0 copy-start.1
  21.6 0.4 %fusion.135.w_ref = f32[512,128]{1,0:T(8,128)S(1)} fusion(f32[512,128]{1,0:T(8,128)S(1)} %slice_dynamic-update-slice_fusion, f32[128,128]{1,0:T(8,128)S(1)} %copy-done.2), kind=kOutput, calls=%fused_computation.202 | convolution fusion | flops 100663296 | bytes 589824 | tf_op jit(solution)/shard_map/dot_general | solution.py:136
  21.9 0.9 %collective-permute-done.11.rest_0_ = bf16[512,128]{1,0:T(8,128)(2,1)S(1)} collective-permute-done((bf16[512,128]{1,0:T(8,128)(2,1)S(1)}, bf16[512,128]{1,0:T(8,128)(2,1)S(1)}, u32[]{:S(2)}, u32[]{:S(2)}) %collective-permute-start.11) | collective-permute-done | bytes 131104 | tf_op jit(solution)/shard_map/ppermute | solution.py:111
  22.9 0.0 copy-done.1
  22.9 1.4 %shard_map.37 = f32[256,512]{1,0:T(8,128)} custom-call(s32[1]{0:T(128)} %bitcast.h_ref, bf16[256,512]{1,0:T(8,128)(2,1)S(1)} %copy-done.1, bf16[256,128]{1,0:T(8,128)(2,1)S(1)} %copy-done, f32[256,128]{1,0:T(8,128)S(1)} %fusion.134.y_ref, f32[128,128]{1,0:T(8,128)S(1)} %copy-done.2, f32[256,128]{1,0:T(8,128)S(1)} %get-tuple-element.50.p_ref, ...), custom_call_target="tpu_custom_call" | custom-call | flops 134217728 | bytes 786432 | tf_op jit(solution)/shard_map/pallas_call | solution.py:219
  (23 shorter events, 0.4 us)
Async XLA Ops:
  0.0 1.9 %collective-permute-start = (bf16[256,512]{1,0:T(8,128)(2,1)}, bf16[256,512]{1,0:T(8,128)(2,1)S(1)}, u32[]{:S(2)}, u32[]{:S(2)}) collective-permute-start(bf16[256,512]{1,0:T(8,128)(2,1)} %a_ref.1), channel_id=1, source_target_pairs={{0,4},{4,0},{8,12},{12,8},{16,20},{20,16},{24,28},{28,24},{1,5},{5... | collective-permute-start | bytes 786440 | tf_op jit(solution)/shard_map/ppermute | solution.py:111
  0.5 1.5 %collective-permute-start.1 = (bf16[256,128]{1,0:T(8,128)(2,1)}, bf16[256,128]{1,0:T(8,128)(2,1)S(1)}, u32[]{:S(2)}, u32[]{:S(2)}) collective-permute-start(bf16[256,128]{1,0:T(8,128)(2,1)} %v_ref.1), channel_id=1, source_target_pairs={{0,4},{4,0},{8,12},{12,8},{16,20},{20,16},{24,28},{28,24},{1,5},{5... | collective-permute-start | bytes 196616 | tf_op jit(solution)/shard_map/ppermute | solution.py:111
  2.4 4.6 %copy-start = (bf16[256,128]{1,0:T(8,128)(2,1)S(1)}, bf16[256,128]{1,0:T(8,128)(2,1)}, u32[]{:S(2)}) copy-start(bf16[256,128]{1,0:T(8,128)(2,1)} %v_ref.1) | copy-start | bytes 196612
  2.4 7.5 %copy-start.2 = (f32[128,128]{1,0:T(8,128)S(1)}, f32[128,128]{1,0:T(8,128)}, u32[]{:S(2)}) copy-start(f32[128,128]{1,0:T(8,128)} %t_ref.1) | copy-start | bytes 196612
  2.4 9.3 %collective-permute-start.4 = (f16[264,128]{1,0:T(8,128)(2,1)S(1)}, f16[264,128]{1,0:T(8,128)(2,1)S(1)}, u32[]{:S(2)}, u32[]{:S(2)}) collective-permute-start(f16[264,128]{1,0:T(8,128)(2,1)S(1)} %pad_maximum_fusion.4), channel_id=1, source_target_pairs={{0,16},{4,20},{8,24},{12,28},{16,0},{20,4},{24,8},{28,12},{1,17},{... | collective-permute-start | bytes 202760 | tf_op jit(solution)/shard_map/ppermute | solution.py:114
  5.4 6.3 %collective-permute-start.3 = (f16[264,128]{1,0:T(8,128)(2,1)S(1)}, f16[264,128]{1,0:T(8,128)(2,1)S(1)}, u32[]{:S(2)}, u32[]{:S(2)}) collective-permute-start(f16[264,128]{1,0:T(8,128)(2,1)S(1)} %pad_maximum_fusion.4), channel_id=1, source_target_pairs={{0,24},{4,28},{8,16},{12,20},{16,8},{20,12},{24,0},{28,4},{1,25},{... | collective-permute-start | bytes 202760 | tf_op jit(solution)/shard_map/ppermute | solution.py:114
  6.8 4.9 %collective-permute-start.2 = (f16[264,128]{1,0:T(8,128)(2,1)S(1)}, f16[264,128]{1,0:T(8,128)(2,1)S(1)}, u32[]{:S(2)}, u32[]{:S(2)}) collective-permute-start(f16[264,128]{1,0:T(8,128)(2,1)S(1)} %pad_maximum_fusion.4), channel_id=1, source_target_pairs={{0,8},{4,12},{8,0},{12,4},{16,24},{20,28},{24,16},{28,20},{1,9},{5... | collective-permute-start | bytes 202760 | tf_op jit(solution)/shard_map/ppermute | solution.py:114
  6.9 13.8 %collective-permute-start.8 = (bf16[256,128]{1,0:T(8,128)(2,1)S(1)}, bf16[256,128]{1,0:T(8,128)(2,1)S(1)}, u32[]{:S(2)}, u32[]{:S(2)}) collective-permute-start(bf16[256,128]{1,0:T(8,128)(2,1)S(1)} %copy-done), channel_id=1, source_target_pairs={{0,24},{4,28},{8,16},{12,20},{16,8},{20,12},{24,0},{28,4},{1,25},{... | collective-permute-start | bytes 196616 | tf_op jit(solution)/shard_map/ppermute | solution.py:114
  10.1 8.2 %collective-permute-start.6 = (bf16[512,128]{1,0:T(8,128)(2,1)S(1)}, bf16[512,128]{1,0:T(8,128)(2,1)S(1)}, u32[]{:S(2)}, u32[]{:S(2)}) collective-permute-start(bf16[512,128]{1,0:T(8,128)(2,1)S(1)} %pad_maximum_fusion.2), channel_id=1, source_target_pairs={{0,8},{4,20},{8,0},{12,28},{16,24},{20,4},{24,16},{28,12},{1,9},{5... | collective-permute-start | bytes 393224 | tf_op jit(solution)/shard_map/ppermute | solution.py:171
  12.3 6.1 %collective-permute-start.10 = (f16[264,128]{1,0:T(8,128)(2,1)S(1)}, f16[264,128]{1,0:T(8,128)(2,1)S(1)}, u32[]{:S(2)}, u32[]{:S(2)}) collective-permute-start(f16[264,128]{1,0:T(8,128)(2,1)S(1)} %pad_maximum_fusion.5), channel_id=1, source_target_pairs={{2,0},{8,1},{3,2},{10,3},{6,4},{12,5},{7,6},{14,7},{11,8},{0,9},{1... | collective-permute-start | bytes 202760 | tf_op jit(solution)/shard_map/ppermute | solution.py:124
  14.5 6.1 %collective-permute-start.9 = (f16[264,128]{1,0:T(8,128)(2,1)S(1)}, f16[264,128]{1,0:T(8,128)(2,1)S(1)}, u32[]{:S(2)}, u32[]{:S(2)}) collective-permute-start(f16[264,128]{1,0:T(8,128)(2,1)S(1)} %pad_maximum_fusion.5), channel_id=1, source_target_pairs={{3,0},{26,1},{0,2},{1,3},{7,4},{30,5},{4,6},{5,7},{9,8},{10,9},{11... | collective-permute-start | bytes 202760 | tf_op jit(solution)/shard_map/ppermute | solution.py:124
  15.3 5.5 %collective-permute-start.5 = (f16[264,128]{1,0:T(8,128)(2,1)S(1)}, f16[264,128]{1,0:T(8,128)(2,1)S(1)}, u32[]{:S(2)}, u32[]{:S(2)}) collective-permute-start(f16[264,128]{1,0:T(8,128)(2,1)S(1)} %pad_maximum_fusion.5), channel_id=1, source_target_pairs={{1,0},{3,1},{9,2},{0,3},{5,4},{7,5},{13,6},{4,7},{10,8},{11,9},{24... | collective-permute-start | bytes 202760 | tf_op jit(solution)/shard_map/ppermute | solution.py:124
  18.4 2.3 %collective-permute-start.7 = (f32[512,128]{1,0:T(8,128)S(1)}, f32[512,128]{1,0:T(8,128)S(1)}, u32[]{:S(2)}, u32[]{:S(2)}) collective-permute-start(f32[512,128]{1,0:T(8,128)S(1)} %pad_maximum_fusion), channel_id=1, source_target_pairs={{0,4},{4,0},{8,12},{12,8},{16,20},{20,16},{24,28},{28,24},{1,5},{5... | collective-permute-start | bytes 786440 | tf_op jit(solution)/shard_map/ppermute | solution.py:111
  21.5 1.4 %collective-permute-start.11 = (bf16[512,128]{1,0:T(8,128)(2,1)S(1)}, bf16[512,128]{1,0:T(8,128)(2,1)S(1)}, u32[]{:S(2)}, u32[]{:S(2)}) collective-permute-start(bf16[512,128]{1,0:T(8,128)(2,1)S(1)} %pad_maximum_fusion.3), channel_id=1, source_target_pairs={{0,4},{4,0},{8,12},{12,8},{16,20},{20,16},{24,28},{28,24},{1,5},{5... | collective-permute-start | bytes 393224 | tf_op jit(solution)/shard_map/ppermute | solution.py:111
  21.6 1.3 %copy-start.1 = (bf16[256,512]{1,0:T(8,128)(2,1)S(1)}, bf16[256,512]{1,0:T(8,128)(2,1)}, u32[]{:S(2)}) copy-start(bf16[256,512]{1,0:T(8,128)(2,1)} %a_ref.1) | copy-start | bytes 786436

commit v8 on v7

--- a/solution.py
+++ b/solution.py
@@ -13,8 +13,8 @@
 TILE = 8
 CHUNKS = 2
 SOURCES = (
-    (((0, 3), (3, 2), (0, 0), (0, 1)), ((1, 1), (1, 2), (1, 3), (0, 2)), ((2, 2), (3, 0), (2, 0), (3, 1)), ((3, 3), (2, 3), (1, 0), (2, 1))),
-    (((0, 2), (1, 0), (0, 3), (1, 2)), ((1, 3), (0, 0), (0, 1), (1, 1)), ((2, 3), (3, 3), (3, 1), (2, 2)), ((3, 2), (2, 0), (2, 1), (3, 0))),
+    (((0, 3), (1, 0), (0, 0), (0, 1)), ((1, 1), (3, 2), (1, 3), (0, 2)), ((2, 2), (3, 3), (2, 0), (3, 1)), ((1, 2), (2, 3), (2, 1), (3, 0))),
+    (((0, 2), (3, 2), (0, 3), (1, 2)), ((1, 3), (0, 0), (0, 1), (1, 1)), ((2, 3), (3, 0), (3, 1), (2, 2)), ((3, 3), (2, 0), (1, 0), (2, 1))),
     (((0, 1), (0, 3), (1, 1), (0, 0)), ((1, 2), (1, 3), (3, 0), (1, 0)), ((3, 1), (0, 2), (2, 3), (2, 0)), ((2, 1), (2, 2), (3, 3), (3, 2))),
 )
 

time: 24.4 us -> 24.4 us (level)
  no operation moved by 1% of the time
where the time goes in v8:
time: 24.4 us; the launch traced here: 24.2 us
  starting transfers between devices  14.7 us (60%)
  waiting for transfers between devices  4.11 us (17%)
  matrix products  2.39 us (10%)
  Pallas kernels  1.36 us (6%)
  other arithmetic  1.21 us (5%)
  between operations  0.38 us (2%)
    ppermute x4, starting transfers between devices, group(): return lax.ppermute(x, 'row', [(r, r ^ s * q) for r in range(n_row)])  7.43 us
    ppermute x3, starting transfers between devices, plane(): return lax.ppermute(x, ('row', 'col'), pairs)  6.01 us
    ppermute x3, waiting for transfers between devices, plane(): return lax.ppermute(x, ('row', 'col'), pairs)  2.01 us
    pallas_call x1, Pallas kernels, shards(): pl.pallas_call(functools.partial(finish, q), out_shape=jax.ShapeDtypeStru...  1.36 us
    dot_general x2, matrix products, chip_part(): lax.dot_general(half, vectors, (((0,), (0,)), ((), ())), preferred_elemen...  1.35 us
    ppermute x4, waiting for transfers between devices, member(): return lax.ppermute(x, 'row', [(r, r ^ s) for r in range(n_row)])  1.12 us
    dot_general x3, matrix products, dot(): lax.dot_general(a, b, (dims, ((), ())), precision=highest, preferred_elem...  1.04 us
    ppermute x4, waiting for transfers between devices, group(): return lax.ppermute(x, 'row', [(r, r ^ s * q) for r in range(n_row)])  0.97 us
  transfers between devices with their start and end apart: 12, of which 4 were waited for; matrix products, arithmetic and copies ran while one was open for 11% of the time, Pallas kernels for 0%

profile of v8, /device:TPU:0, one launch (start us, length us, event | category | flops | bytes accessed | tf_op | source)
XLA Modules:
  0.0 24.2 jit_solution(7171016483606904992)
XLA Ops:
  0.0 0.5 %collective-permute-start = (bf16[256,512]{1,0:T(8,128)(2,1)}, bf16[256,512]{1,0:T(8,128)(2,1)S(1)}, u32[]{:S(2)}, u32[]{:S(2)}) collective-permute-start(bf16[256,512]{1,0:T(8,128)(2,1)} %a_ref.1), channel_id=1, source_target_pairs={{0,4},{4,0},{8,12},{12,8},{16,20},{20,16},{24,28},{28,24},{1,5},{5... | collective-permute-start | bytes 786440 | tf_op jit(solution)/shard_map/ppermute | solution.py:111
  0.5 0.1 collective-permute-start.1
  0.5 1.1 %fusion.106 = f32[256,128]{1,0:T(8,128)S(1)} fusion(bf16[256,128]{1,0:T(8,128)(2,1)} %v_ref.1, bf16[256,512]{1,0:T(8,128)(2,1)} %a_ref.1, s32[]{:T(128)S(6)} %select_n.186), kind=kOutput, calls=%fused_computation.133 | convolution fusion | flops 16777216 | bytes 327684 | tf_op jit(solution)/shard_map/dot_general | solution.py:157
  1.7 0.2 collective-permute-done.1
  1.9 0.0 collective-permute-done
  1.9 0.2 fusion.104
  2.2 0.1 fusion.102
  2.4 0.0 copy-start
  2.4 0.0 copy-start.2
  2.4 3.0 %collective-permute-start.4 = (f16[264,128]{1,0:T(8,128)(2,1)S(1)}, f16[264,128]{1,0:T(8,128)(2,1)S(1)}, u32[]{:S(2)}, u32[]{:S(2)}) collective-permute-start(f16[264,128]{1,0:T(8,128)(2,1)S(1)} %pad_maximum_fusion.4), channel_id=1, source_target_pairs={{0,16},{4,20},{8,24},{12,28},{16,0},{20,4},{24,8},{28,12},{1,17},{... | collective-permute-start | bytes 202760 | tf_op jit(solution)/shard_map/ppermute | solution.py:114
  5.4 1.4 %collective-permute-start.3 = (f16[264,128]{1,0:T(8,128)(2,1)S(1)}, f16[264,128]{1,0:T(8,128)(2,1)S(1)}, u32[]{:S(2)}, u32[]{:S(2)}) collective-permute-start(f16[264,128]{1,0:T(8,128)(2,1)S(1)} %pad_maximum_fusion.4), channel_id=1, source_target_pairs={{0,24},{4,28},{8,16},{12,20},{16,8},{20,12},{24,0},{28,4},{1,25},{... | collective-permute-start | bytes 202760 | tf_op jit(solution)/shard_map/ppermute | solution.py:114
  6.8 0.1 collective-permute-start.2
  6.9 0.0 copy-done
  6.9 2.9 %collective-permute-start.8 = (bf16[256,128]{1,0:T(8,128)(2,1)S(1)}, bf16[256,128]{1,0:T(8,128)(2,1)S(1)}, u32[]{:S(2)}, u32[]{:S(2)}) collective-permute-start(bf16[256,128]{1,0:T(8,128)(2,1)S(1)} %copy-done), channel_id=1, source_target_pairs={{0,24},{4,28},{8,16},{12,20},{16,8},{20,12},{24,0},{28,4},{1,25},{... | collective-permute-start | bytes 196616 | tf_op jit(solution)/shard_map/ppermute | solution.py:114
  9.9 0.0 copy-done.2
  9.9 0.2 fusion.134.y_ref
  10.1 0.6 %collective-permute-start.6 = (bf16[512,128]{1,0:T(8,128)(2,1)S(1)}, bf16[512,128]{1,0:T(8,128)(2,1)S(1)}, u32[]{:S(2)}, u32[]{:S(2)}) collective-permute-start(bf16[512,128]{1,0:T(8,128)(2,1)S(1)} %pad_maximum_fusion.2), channel_id=1, source_target_pairs={{0,8},{4,20},{8,0},{12,28},{16,24},{20,4},{24,16},{28,12},{1,9},{5... | collective-permute-start | bytes 393224 | tf_op jit(solution)/shard_map/ppermute | solution.py:171
  10.8 1.0 %collective-permute-done.2 = f16[264,128]{1,0:T(8,128)(2,1)S(1)} collective-permute-done((f16[264,128]{1,0:T(8,128)(2,1)S(1)}, f16[264,128]{1,0:T(8,128)(2,1)S(1)}, u32[]{:S(2)}, u32[]{:S(2)}) %collective-permute-start.2) | collective-permute-done | bytes 67616 | tf_op jit(solution)/shard_map/ppermute | solution.py:114
  11.7 0.0 collective-permute-done.4
  11.7 0.0 collective-permute-done.3
  11.7 0.1 divide_bitcast_fusion
  11.8 0.3 %constant_dynamic-update-slice_fusion = (f32[512,128]{1,0:T(8,128)S(1)}, f32[256,128]{1,0:T(8,128)S(1)}) fusion(f32[512,128]{1,0:T(8,128)S(1)} %broadcast_in_dim.38, s32[]{:T(128)S(6)} %select_n.186, f32[128]{0:T(128)S(1)} %get-tuple-element.53, f16[264,128]{1,0:T(8,128)(2,1)S(1)} %collective-permute-done.2, f32[128]{0:T(128)S(1)} %get-tuple-element.52, ...), kind=kLoop, calls=%fused_computation.150 | loop fusion | flops 1966080 | bytes 591364 | tf_op jit(solution)/shard_map/dynamic_update_slice | solution.py:145
  12.1 0.1 fusion.103
  12.3 2.2 %collective-permute-start.10 = (f16[264,128]{1,0:T(8,128)(2,1)S(1)}, f16[264,128]{1,0:T(8,128)(2,1)S(1)}, u32[]{:S(2)}, u32[]{:S(2)}) collective-permute-start(f16[264,128]{1,0:T(8,128)(2,1)S(1)} %pad_maximum_fusion.5), channel_id=1, source_target_pairs={{2,0},{26,1},{3,2},{10,3},{6,4},{30,5},{7,6},{14,7},{11,8},{0,9},{... | collective-permute-start | bytes 202760 | tf_op jit(solution)/shard_map/ppermute | solution.py:124
  14.5 0.8 %collective-permute-start.9 = (f16[264,128]{1,0:T(8,128)(2,1)S(1)}, f16[264,128]{1,0:T(8,128)(2,1)S(1)}, u32[]{:S(2)}, u32[]{:S(2)}) collective-permute-start(f16[264,128]{1,0:T(8,128)(2,1)S(1)} %pad_maximum_fusion.5), channel_id=1, source_target_pairs={{3,0},{8,1},{0,2},{1,3},{7,4},{12,5},{4,6},{5,7},{9,8},{26,9},{11,... | collective-permute-start | bytes 202760 | tf_op jit(solution)/shard_map/ppermute | solution.py:124
  15.3 3.0 %collective-permute-start.5 = (f16[264,128]{1,0:T(8,128)(2,1)S(1)}, f16[264,128]{1,0:T(8,128)(2,1)S(1)}, u32[]{:S(2)}, u32[]{:S(2)}) collective-permute-start(f16[264,128]{1,0:T(8,128)(2,1)S(1)} %pad_maximum_fusion.5), channel_id=1, source_target_pairs={{1,0},{3,1},{9,2},{0,3},{5,4},{7,5},{13,6},{4,7},{10,8},{11,9},{24... | collective-permute-start | bytes 202760 | tf_op jit(solution)/shard_map/ppermute | solution.py:124
  18.3 0.0 collective-permute-done.6
  18.4 0.1 collective-permute-start.7
  18.4 0.0 collective-permute-done.10
  18.5 0.1 fusion.87
  18.6 2.0 %collective-permute-done.9 = f16[264,128]{1,0:T(8,128)(2,1)S(1)} collective-permute-done((f16[264,128]{1,0:T(8,128)(2,1)S(1)}, f16[264,128]{1,0:T(8,128)(2,1)S(1)}, u32[]{:S(2)}, u32[]{:S(2)}) %collective-permute-start.9) | collective-permute-done | bytes 67616 | tf_op jit(solution)/shard_map/ppermute | solution.py:124
  20.6 0.1 fusion.73
  20.7 0.0 collective-permute-done.7
  20.7 0.0 collective-permute-done.8
  20.8 0.0 collective-permute-done.5
  20.9 0.1 fusion.101
  21.0 0.4 %reduce-precision_convert_fusion = (bf16[128,128]{1,0:T(8,128)(2,1)S(1)}, bf16[128,128]{1,0:T(8,128)(2,1)S(1)}, f32[128,128]{1,0:T(8,128)S(1)}) fusion(f32[256,128]{1,0:T(8,128)S(1)} %get-tuple-element.49, f32[256,128]{1,0:T(8,128)S(1)} %fusion.87, f32[256,128]{1,0:T(8,128)S(1)} %fusion.73, f32[256,128]{1,0:T(8,128)S(1)} %get-tuple-element.30, ...), kind=kOutput, calls=%fused_computation.137 | convolution fusion | flops 202833920 | bytes 917504 | tf_op jit(solution)/shard_map/dot_general | solution.py:136
  21.4 0.1 collective-permute-start.11
  21.6 0.0 copy-start.1
  21.6 0.4 %fusion.135.w_ref = f32[512,128]{1,0:T(8,128)S(1)} fusion(f32[512,128]{1,0:T(8,128)S(1)} %slice_dynamic-update-slice_fusion, f32[128,128]{1,0:T(8,128)S(1)} %copy-done.2), kind=kOutput, calls=%fused_computation.202 | convolution fusion | flops 100663296 | bytes 589824 | tf_op jit(solution)/shard_map/dot_general | solution.py:136
  21.9 0.9 %collective-permute-done.11.rest_0_ = bf16[512,128]{1,0:T(8,128)(2,1)S(1)} collective-permute-done((bf16[512,128]{1,0:T(8,128)(2,1)S(1)}, bf16[512,128]{1,0:T(8,128)(2,1)S(1)}, u32[]{:S(2)}, u32[]{:S(2)}) %collective-permute-start.11) | collective-permute-done | bytes 131104 | tf_op jit(solution)/shard_map/ppermute | solution.py:111
  22.9 0.0 copy-done.1
  22.9 1.4 %shard_map.37 = f32[256,512]{1,0:T(8,128)} custom-call(s32[1]{0:T(128)} %bitcast.h_ref, bf16[256,512]{1,0:T(8,128)(2,1)S(1)} %copy-done.1, bf16[256,128]{1,0:T(8,128)(2,1)S(1)} %copy-done, f32[256,128]{1,0:T(8,128)S(1)} %fusion.134.y_ref, f32[128,128]{1,0:T(8,128)S(1)} %copy-done.2, f32[256,128]{1,0:T(8,128)S(1)} %get-tuple-element.50.p_ref, ...), custom_call_target="tpu_custom_call" | custom-call | flops 134217728 | bytes 786432 | tf_op jit(solution)/shard_map/pallas_call | solution.py:219
  (23 shorter events, 0.4 us)
Async XLA Ops:
  0.0 1.9 %collective-permute-start = (bf16[256,512]{1,0:T(8,128)(2,1)}, bf16[256,512]{1,0:T(8,128)(2,1)S(1)}, u32[]{:S(2)}, u32[]{:S(2)}) collective-permute-start(bf16[256,512]{1,0:T(8,128)(2,1)} %a_ref.1), channel_id=1, source_target_pairs={{0,4},{4,0},{8,12},{12,8},{16,20},{20,16},{24,28},{28,24},{1,5},{5... | collective-permute-start | bytes 786440 | tf_op jit(solution)/shard_map/ppermute | solution.py:111
  0.5 1.5 %collective-permute-start.1 = (bf16[256,128]{1,0:T(8,128)(2,1)}, bf16[256,128]{1,0:T(8,128)(2,1)S(1)}, u32[]{:S(2)}, u32[]{:S(2)}) collective-permute-start(bf16[256,128]{1,0:T(8,128)(2,1)} %v_ref.1), channel_id=1, source_target_pairs={{0,4},{4,0},{8,12},{12,8},{16,20},{20,16},{24,28},{28,24},{1,5},{5... | collective-permute-start | bytes 196616 | tf_op jit(solution)/shard_map/ppermute | solution.py:111
  2.4 4.6 %copy-start = (bf16[256,128]{1,0:T(8,128)(2,1)S(1)}, bf16[256,128]{1,0:T(8,128)(2,1)}, u32[]{:S(2)}) copy-start(bf16[256,128]{1,0:T(8,128)(2,1)} %v_ref.1) | copy-start | bytes 196612
  2.4 7.5 %copy-start.2 = (f32[128,128]{1,0:T(8,128)S(1)}, f32[128,128]{1,0:T(8,128)}, u32[]{:S(2)}) copy-start(f32[128,128]{1,0:T(8,128)} %t_ref.1) | copy-start | bytes 196612
  2.4 9.3 %collective-permute-start.4 = (f16[264,128]{1,0:T(8,128)(2,1)S(1)}, f16[264,128]{1,0:T(8,128)(2,1)S(1)}, u32[]{:S(2)}, u32[]{:S(2)}) collective-permute-start(f16[264,128]{1,0:T(8,128)(2,1)S(1)} %pad_maximum_fusion.4), channel_id=1, source_target_pairs={{0,16},{4,20},{8,24},{12,28},{16,0},{20,4},{24,8},{28,12},{1,17},{... | collective-permute-start | bytes 202760 | tf_op jit(solution)/shard_map/ppermute | solution.py:114
  5.4 6.3 %collective-permute-start.3 = (f16[264,128]{1,0:T(8,128)(2,1)S(1)}, f16[264,128]{1,0:T(8,128)(2,1)S(1)}, u32[]{:S(2)}, u32[]{:S(2)}) collective-permute-start(f16[264,128]{1,0:T(8,128)(2,1)S(1)} %pad_maximum_fusion.4), channel_id=1, source_target_pairs={{0,24},{4,28},{8,16},{12,20},{16,8},{20,12},{24,0},{28,4},{1,25},{... | collective-permute-start | bytes 202760 | tf_op jit(solution)/shard_map/ppermute | solution.py:114
  6.8 4.9 %collective-permute-start.2 = (f16[264,128]{1,0:T(8,128)(2,1)S(1)}, f16[264,128]{1,0:T(8,128)(2,1)S(1)}, u32[]{:S(2)}, u32[]{:S(2)}) collective-permute-start(f16[264,128]{1,0:T(8,128)(2,1)S(1)} %pad_maximum_fusion.4), channel_id=1, source_target_pairs={{0,8},{4,12},{8,0},{12,4},{16,24},{20,28},{24,16},{28,20},{1,9},{5... | collective-permute-start | bytes 202760 | tf_op jit(solution)/shard_map/ppermute | solution.py:114
  6.9 13.8 %collective-permute-start.8 = (bf16[256,128]{1,0:T(8,128)(2,1)S(1)}, bf16[256,128]{1,0:T(8,128)(2,1)S(1)}, u32[]{:S(2)}, u32[]{:S(2)}) collective-permute-start(bf16[256,128]{1,0:T(8,128)(2,1)S(1)} %copy-done), channel_id=1, source_target_pairs={{0,24},{4,28},{8,16},{12,20},{16,8},{20,12},{24,0},{28,4},{1,25},{... | collective-permute-start | bytes 196616 | tf_op jit(solution)/shard_map/ppermute | solution.py:114
  10.1 8.2 %collective-permute-start.6 = (bf16[512,128]{1,0:T(8,128)(2,1)S(1)}, bf16[512,128]{1,0:T(8,128)(2,1)S(1)}, u32[]{:S(2)}, u32[]{:S(2)}) collective-permute-start(bf16[512,128]{1,0:T(8,128)(2,1)S(1)} %pad_maximum_fusion.2), channel_id=1, source_target_pairs={{0,8},{4,20},{8,0},{12,28},{16,24},{20,4},{24,16},{28,12},{1,9},{5... | collective-permute-start | bytes 393224 | tf_op jit(solution)/shard_map/ppermute | solution.py:171
  12.3 6.1 %collective-permute-start.10 = (f16[264,128]{1,0:T(8,128)(2,1)S(1)}, f16[264,128]{1,0:T(8,128)(2,1)S(1)}, u32[]{:S(2)}, u32[]{:S(2)}) collective-permute-start(f16[264,128]{1,0:T(8,128)(2,1)S(1)} %pad_maximum_fusion.5), channel_id=1, source_target_pairs={{2,0},{26,1},{3,2},{10,3},{6,4},{30,5},{7,6},{14,7},{11,8},{0,9},{... | collective-permute-start | bytes 202760 | tf_op jit(solution)/shard_map/ppermute | solution.py:124
  14.5 6.1 %collective-permute-start.9 = (f16[264,128]{1,0:T(8,128)(2,1)S(1)}, f16[264,128]{1,0:T(8,128)(2,1)S(1)}, u32[]{:S(2)}, u32[]{:S(2)}) collective-permute-start(f16[264,128]{1,0:T(8,128)(2,1)S(1)} %pad_maximum_fusion.5), channel_id=1, source_target_pairs={{3,0},{8,1},{0,2},{1,3},{7,4},{12,5},{4,6},{5,7},{9,8},{26,9},{11,... | collective-permute-start | bytes 202760 | tf_op jit(solution)/shard_map/ppermute | solution.py:124
  15.3 5.5 %collective-permute-start.5 = (f16[264,128]{1,0:T(8,128)(2,1)S(1)}, f16[264,128]{1,0:T(8,128)(2,1)S(1)}, u32[]{:S(2)}, u32[]{:S(2)}) collective-permute-start(f16[264,128]{1,0:T(8,128)(2,1)S(1)} %pad_maximum_fusion.5), channel_id=1, source_target_pairs={{1,0},{3,1},{9,2},{0,3},{5,4},{7,5},{13,6},{4,7},{10,8},{11,9},{24... | collective-permute-start | bytes 202760 | tf_op jit(solution)/shard_map/ppermute | solution.py:124
  18.4 2.3 %collective-permute-start.7 = (f32[512,128]{1,0:T(8,128)S(1)}, f32[512,128]{1,0:T(8,128)S(1)}, u32[]{:S(2)}, u32[]{:S(2)}) collective-permute-start(f32[512,128]{1,0:T(8,128)S(1)} %pad_maximum_fusion), channel_id=1, source_target_pairs={{0,4},{4,0},{8,12},{12,8},{16,20},{20,16},{24,28},{28,24},{1,5},{5... | collective-permute-start | bytes 786440 | tf_op jit(solution)/shard_map/ppermute | solution.py:111
  21.4 1.4 %collective-permute-start.11 = (bf16[512,128]{1,0:T(8,128)(2,1)S(1)}, bf16[512,128]{1,0:T(8,128)(2,1)S(1)}, u32[]{:S(2)}, u32[]{:S(2)}) collective-permute-start(bf16[512,128]{1,0:T(8,128)(2,1)S(1)} %pad_maximum_fusion.3), channel_id=1, source_target_pairs={{0,4},{4,0},{8,12},{12,8},{16,20},{20,16},{24,28},{28,24},{1,5},{5... | collective-permute-start | bytes 393224 | tf_op jit(solution)/shard_map/ppermute | solution.py:111
  21.6 1.3 %copy-start.1 = (bf16[256,512]{1,0:T(8,128)(2,1)S(1)}, bf16[256,512]{1,0:T(8,128)(2,1)}, u32[]{:S(2)}) copy-start(bf16[256,512]{1,0:T(8,128)(2,1)} %a_ref.1) | copy-start | bytes 786436

commit v9 on v7

--- a/solution.py
+++ b/solution.py
@@ -208,8 +208,15 @@
         p_rows = total
         for s in order:
             p_rows = jnp.where(came[s] == k, values[s], p_rows)
-        p_mates = jnp.concatenate([values[s] for s in range(n_col)], 0)
-        gram = dot(v_mates.astype(jnp.float32), p_mates, ((0,), (0,)))
+        parts = [lax.reduce_precision(values[s], 8, 7) for s in range(n_col)]
+        terms = [
+            jnp.concatenate([parts[s].astype(jnp.bfloat16), (values[s] - parts[s]).astype(jnp.bfloat16)], 1)
+            for s in range(n_col)
+        ]
+        gram = lax.dot_general(
+            v_mates, jnp.concatenate(terms, 0), (((0,), (0,)), ((), ())), preferred_element_type=jnp.float32
+        )
+        gram = gram[:, :band] + gram[:, band:]
         v_piece = tiles[0]
         high = lax.reduce_precision(gram, 8, 7)
         packed = jnp.concatenate([high.astype(jnp.bfloat16), (gram - high).astype(jnp.bfloat16), v_piece], 0)

time: 24.4 us -> 24.3 us (level)
    dot_general x3 -> x2, matrix products: 1.05 us -> 0.6 us  [dot(): lax.dot_general(a, b, (dims, ((), ())), precision=highest, preferred_elem...]
    dot_general x0 -> x1, matrix products: none -> 0.27 us  [shards(): lax.dot_general(v_mates, jnp.concatenate(terms, 0), (((0,), (0,)), ((), (...]
where the time goes in v9:
time: 24.3 us; the launch traced here: 24.2 us
  starting transfers between devices  14.7 us (60%)
  waiting for transfers between devices  4.1 us (17%)
  matrix products  2.22 us (9%)
  Pallas kernels  1.37 us (6%)
  other arithmetic  1.31 us (5%)
  between operations  0.41 us (2%)
    ppermute x4, starting transfers between devices, group(): return lax.ppermute(x, 'row', [(r, r ^ s * q) for r in range(n_row)])  7.43 us
    ppermute x3, starting transfers between devices, plane(): return lax.ppermute(x, ('row', 'col'), pairs)  6.01 us
    ppermute x3, waiting for transfers between devices, plane(): return lax.ppermute(x, ('row', 'col'), pairs)  2.02 us
    pallas_call x1, Pallas kernels, shards(): pl.pallas_call(functools.partial(finish, q), out_shape=jax.ShapeDtypeStru...  1.37 us
    dot_general x2, matrix products, chip_part(): lax.dot_general(half, vectors, (((0,), (0,)), ((), ())), preferred_elemen...  1.35 us
    ppermute x4, waiting for transfers between devices, member(): return lax.ppermute(x, 'row', [(r, r ^ s) for r in range(n_row)])  1.12 us
    ppermute x4, waiting for transfers between devices, group(): return lax.ppermute(x, 'row', [(r, r ^ s * q) for r in range(n_row)])  0.97 us
    ppermute x4, starting transfers between devices, member(): return lax.ppermute(x, 'row', [(r, r ^ s) for r in range(n_row)])  0.65 us
  transfers between devices with their start and end apart: 12, of which 4 were waited for; matrix products, arithmetic and copies ran while one was open for 11% of the time, Pallas kernels for 0%

profile of v9, /device:TPU:0, one launch (start us, length us, event | category | flops | bytes accessed | tf_op | source)
XLA Modules:
  0.0 24.2 jit_solution(10255266603127607445)
XLA Ops:
  0.0 0.5 %collective-permute-start = (bf16[256,512]{1,0:T(8,128)(2,1)}, bf16[256,512]{1,0:T(8,128)(2,1)S(1)}, u32[]{:S(2)}, u32[]{:S(2)}) collective-permute-start(bf16[256,512]{1,0:T(8,128)(2,1)} %a_ref.1), channel_id=1, source_target_pairs={{0,4},{4,0},{8,12},{12,8},{16,20},{20,16},{24,28},{28,24},{1,5},{5... | collective-permute-start | bytes 786440 | tf_op jit(solution)/shard_map/ppermute | solution.py:111
  0.5 0.1 collective-permute-start.1
  0.5 1.1 %fusion.118 = f32[256,128]{1,0:T(8,128)S(1)} fusion(bf16[256,128]{1,0:T(8,128)(2,1)} %v_ref.1, bf16[256,512]{1,0:T(8,128)(2,1)} %a_ref.1, s32[]{:T(128)S(6)} %select_n.186), kind=kOutput, calls=%fused_computation.153 | convolution fusion | flops 16777216 | bytes 327684 | tf_op jit(solution)/shard_map/dot_general | solution.py:157
  1.7 0.2 collective-permute-done.1
  1.9 0.0 collective-permute-done
  1.9 0.2 fusion.116
  2.2 0.1 fusion.114
  2.4 0.0 copy-start
  2.4 0.0 copy-start.2
  2.4 3.0 %collective-permute-start.4 = (f16[264,128]{1,0:T(8,128)(2,1)S(1)}, f16[264,128]{1,0:T(8,128)(2,1)S(1)}, u32[]{:S(2)}, u32[]{:S(2)}) collective-permute-start(f16[264,128]{1,0:T(8,128)(2,1)S(1)} %pad_maximum_fusion.4), channel_id=1, source_target_pairs={{0,16},{4,20},{8,24},{12,28},{16,0},{20,4},{24,8},{28,12},{1,17},{... | collective-permute-start | bytes 202760 | tf_op jit(solution)/shard_map/ppermute | solution.py:114
  5.4 1.4 %collective-permute-start.3 = (f16[264,128]{1,0:T(8,128)(2,1)S(1)}, f16[264,128]{1,0:T(8,128)(2,1)S(1)}, u32[]{:S(2)}, u32[]{:S(2)}) collective-permute-start(f16[264,128]{1,0:T(8,128)(2,1)S(1)} %pad_maximum_fusion.4), channel_id=1, source_target_pairs={{0,24},{4,28},{8,16},{12,20},{16,8},{20,12},{24,0},{28,4},{1,25},{... | collective-permute-start | bytes 202760 | tf_op jit(solution)/shard_map/ppermute | solution.py:114
  6.8 0.1 collective-permute-start.2
  6.9 0.0 copy-done
  6.9 2.9 %collective-permute-start.8 = (bf16[256,128]{1,0:T(8,128)(2,1)S(1)}, bf16[256,128]{1,0:T(8,128)(2,1)S(1)}, u32[]{:S(2)}, u32[]{:S(2)}) collective-permute-start(bf16[256,128]{1,0:T(8,128)(2,1)S(1)} %copy-done), channel_id=1, source_target_pairs={{0,24},{4,28},{8,16},{12,20},{16,8},{20,12},{24,0},{28,4},{1,25},{... | collective-permute-start | bytes 196616 | tf_op jit(solution)/shard_map/ppermute | solution.py:114
  9.9 0.0 copy-done.2
  9.9 0.2 fusion.145.y_ref
  10.1 0.6 %collective-permute-start.6 = (bf16[512,128]{1,0:T(8,128)(2,1)S(1)}, bf16[512,128]{1,0:T(8,128)(2,1)S(1)}, u32[]{:S(2)}, u32[]{:S(2)}) collective-permute-start(bf16[512,128]{1,0:T(8,128)(2,1)S(1)} %pad_maximum_fusion.2), channel_id=1, source_target_pairs={{0,8},{4,20},{8,0},{12,28},{16,24},{20,4},{24,16},{28,12},{1,9},{5... | collective-permute-start | bytes 393224 | tf_op jit(solution)/shard_map/ppermute | solution.py:171
  10.8 1.0 %collective-permute-done.2 = f16[264,128]{1,0:T(8,128)(2,1)S(1)} collective-permute-done((f16[264,128]{1,0:T(8,128)(2,1)S(1)}, f16[264,128]{1,0:T(8,128)(2,1)S(1)}, u32[]{:S(2)}, u32[]{:S(2)}) %collective-permute-start.2) | collective-permute-done | bytes 67616 | tf_op jit(solution)/shard_map/ppermute | solution.py:114
  11.7 0.0 collective-permute-done.4
  11.7 0.0 collective-permute-done.3
  11.7 0.1 divide_bitcast_fusion
  11.8 0.3 %constant_dynamic-update-slice_fusion = (f32[512,128]{1,0:T(8,128)S(1)}, f32[256,128]{1,0:T(8,128)S(1)}) fusion(f32[512,128]{1,0:T(8,128)S(1)} %broadcast_in_dim.38, s32[]{:T(128)S(6)} %select_n.186, f32[128]{0:T(128)S(1)} %get-tuple-element.62, f16[264,128]{1,0:T(8,128)(2,1)S(1)} %collective-permute-done.2, f32[128]{0:T(128)S(1)} %get-tuple-element.61, ...), kind=kLoop, calls=%fused_computation.171 | loop fusion | flops 1966080 | bytes 591364 | tf_op jit(solution)/shard_map/dynamic_update_slice | solution.py:145
  12.1 0.1 fusion.115
  12.3 2.2 %collective-permute-start.10 = (f16[264,128]{1,0:T(8,128)(2,1)S(1)}, f16[264,128]{1,0:T(8,128)(2,1)S(1)}, u32[]{:S(2)}, u32[]{:S(2)}) collective-permute-start(f16[264,128]{1,0:T(8,128)(2,1)S(1)} %pad_maximum_fusion.5), channel_id=1, source_target_pairs={{2,0},{8,1},{3,2},{10,3},{6,4},{12,5},{7,6},{14,7},{11,8},{0,9},{1... | collective-permute-start | bytes 202760 | tf_op jit(solution)/shard_map/ppermute | solution.py:124
  14.5 0.8 %collective-permute-start.9 = (f16[264,128]{1,0:T(8,128)(2,1)S(1)}, f16[264,128]{1,0:T(8,128)(2,1)S(1)}, u32[]{:S(2)}, u32[]{:S(2)}) collective-permute-start(f16[264,128]{1,0:T(8,128)(2,1)S(1)} %pad_maximum_fusion.5), channel_id=1, source_target_pairs={{3,0},{26,1},{0,2},{1,3},{7,4},{30,5},{4,6},{5,7},{9,8},{10,9},{11... | collective-permute-start | bytes 202760 | tf_op jit(solution)/shard_map/ppermute | solution.py:124
  15.3 3.0 %collective-permute-start.5 = (f16[264,128]{1,0:T(8,128)(2,1)S(1)}, f16[264,128]{1,0:T(8,128)(2,1)S(1)}, u32[]{:S(2)}, u32[]{:S(2)}) collective-permute-start(f16[264,128]{1,0:T(8,128)(2,1)S(1)} %pad_maximum_fusion.5), channel_id=1, source_target_pairs={{1,0},{3,1},{9,2},{0,3},{5,4},{7,5},{13,6},{4,7},{10,8},{11,9},{24... | collective-permute-start | bytes 202760 | tf_op jit(solution)/shard_map/ppermute | solution.py:124
  18.3 0.0 collective-permute-done.6
  18.4 0.1 collective-permute-start.7
  18.4 0.0 collective-permute-done.10
  18.5 0.1 fusion.95
  18.6 2.0 %collective-permute-done.9 = f16[264,128]{1,0:T(8,128)(2,1)S(1)} collective-permute-done((f16[264,128]{1,0:T(8,128)(2,1)S(1)}, f16[264,128]{1,0:T(8,128)(2,1)S(1)}, u32[]{:S(2)}, u32[]{:S(2)}) %collective-permute-start.9) | collective-permute-done | bytes 67616 | tf_op jit(solution)/shard_map/ppermute | solution.py:124
  20.6 0.1 fusion.81
  20.7 0.0 collective-permute-done.7
  20.7 0.0 collective-permute-done.8
  20.8 0.0 collective-permute-done.5
  20.9 0.2 reduce-precision_convert_fusion.2
  21.1 0.3 %fusion = f32[128,256]{1,0:T(8,128)S(1)} fusion(bf16[256,128]{1,0:T(8,128)(2,1)S(1)} %get-tuple-element.59, bf16[256,128]{1,0:T(8,128)(2,1)S(1)} %get-tuple-element.58, bf16[256,128]{1,0:T(8,128)(2,1)S(1)} %get-tuple-element.55, bf16[256,128]{1,0:T(8,128)(2,1)S(1)} %get-tuple-element.54, bf16[256,128]{1,0:T(8,128)(2,1)S(1)} %get-tuple-element.52, ...), kind=kOutput, calls=%fused_computation | convolution fusion | flops 72351744 | bytes 917504 | tf_op jit(solution)/shard_map/dot_general | solution.py:216
  21.4 0.1 collective-permute-start.11
  21.5 0.0 copy-start.1
  21.5 0.4 %fusion.146.w_ref = f32[512,128]{1,0:T(8,128)S(1)} fusion(f32[512,128]{1,0:T(8,128)S(1)} %slice_dynamic-update-slice_fusion, f32[128,128]{1,0:T(8,128)S(1)} %copy-done.2), kind=kOutput, calls=%fused_computation.222 | convolution fusion | flops 100663296 | bytes 589824 | tf_op jit(solution)/shard_map/dot_general | solution.py:136
  21.9 0.9 %collective-permute-done.11.rest_0_ = bf16[512,128]{1,0:T(8,128)(2,1)S(1)} collective-permute-done((bf16[512,128]{1,0:T(8,128)(2,1)S(1)}, bf16[512,128]{1,0:T(8,128)(2,1)S(1)}, u32[]{:S(2)}, u32[]{:S(2)}) %collective-permute-start.11) | collective-permute-done | bytes 131104 | tf_op jit(solution)/shard_map/ppermute | solution.py:111
  22.8 0.0 copy-done.1
  22.8 1.4 %shard_map.37 = f32[256,512]{1,0:T(8,128)} custom-call(s32[1]{0:T(128)} %bitcast.h_ref, bf16[256,512]{1,0:T(8,128)(2,1)S(1)} %copy-done.1, bf16[256,128]{1,0:T(8,128)(2,1)S(1)} %copy-done, f32[256,128]{1,0:T(8,128)S(1)} %fusion.145.y_ref, f32[128,128]{1,0:T(8,128)S(1)} %copy-done.2, f32[256,128]{1,0:T(8,128)S(1)} %get-tuple-element.53.p_ref, ...), custom_call_target="tpu_custom_call" | custom-call | flops 134217728 | bytes 786432 | tf_op jit(solution)/shard_map/pallas_call | solution.py:226
  (26 shorter events, 0.5 us)
Async XLA Ops:
  0.0 1.9 %collective-permute-start = (bf16[256,512]{1,0:T(8,128)(2,1)}, bf16[256,512]{1,0:T(8,128)(2,1)S(1)}, u32[]{:S(2)}, u32[]{:S(2)}) collective-permute-start(bf16[256,512]{1,0:T(8,128)(2,1)} %a_ref.1), channel_id=1, source_target_pairs={{0,4},{4,0},{8,12},{12,8},{16,20},{20,16},{24,28},{28,24},{1,5},{5... | collective-permute-start | bytes 786440 | tf_op jit(solution)/shard_map/ppermute | solution.py:111
  0.5 1.5 %collective-permute-start.1 = (bf16[256,128]{1,0:T(8,128)(2,1)}, bf16[256,128]{1,0:T(8,128)(2,1)S(1)}, u32[]{:S(2)}, u32[]{:S(2)}) collective-permute-start(bf16[256,128]{1,0:T(8,128)(2,1)} %v_ref.1), channel_id=1, source_target_pairs={{0,4},{4,0},{8,12},{12,8},{16,20},{20,16},{24,28},{28,24},{1,5},{5... | collective-permute-start | bytes 196616 | tf_op jit(solution)/shard_map/ppermute | solution.py:111
  2.4 4.6 %copy-start = (bf16[256,128]{1,0:T(8,128)(2,1)S(1)}, bf16[256,128]{1,0:T(8,128)(2,1)}, u32[]{:S(2)}) copy-start(bf16[256,128]{1,0:T(8,128)(2,1)} %v_ref.1) | copy-start | bytes 196612
  2.4 7.5 %copy-start.2 = (f32[128,128]{1,0:T(8,128)S(1)}, f32[128,128]{1,0:T(8,128)}, u32[]{:S(2)}) copy-start(f32[128,128]{1,0:T(8,128)} %t_ref.1) | copy-start | bytes 196612
  2.4 9.3 %collective-permute-start.4 = (f16[264,128]{1,0:T(8,128)(2,1)S(1)}, f16[264,128]{1,0:T(8,128)(2,1)S(1)}, u32[]{:S(2)}, u32[]{:S(2)}) collective-permute-start(f16[264,128]{1,0:T(8,128)(2,1)S(1)} %pad_maximum_fusion.4), channel_id=1, source_target_pairs={{0,16},{4,20},{8,24},{12,28},{16,0},{20,4},{24,8},{28,12},{1,17},{... | collective-permute-start | bytes 202760 | tf_op jit(solution)/shard_map/ppermute | solution.py:114
  5.4 6.3 %collective-permute-start.3 = (f16[264,128]{1,0:T(8,128)(2,1)S(1)}, f16[264,128]{1,0:T(8,128)(2,1)S(1)}, u32[]{:S(2)}, u32[]{:S(2)}) collective-permute-start(f16[264,128]{1,0:T(8,128)(2,1)S(1)} %pad_maximum_fusion.4), channel_id=1, source_target_pairs={{0,24},{4,28},{8,16},{12,20},{16,8},{20,12},{24,0},{28,4},{1,25},{... | collective-permute-start | bytes 202760 | tf_op jit(solution)/shard_map/ppermute | solution.py:114
  6.8 4.9 %collective-permute-start.2 = (f16[264,128]{1,0:T(8,128)(2,1)S(1)}, f16[264,128]{1,0:T(8,128)(2,1)S(1)}, u32[]{:S(2)}, u32[]{:S(2)}) collective-permute-start(f16[264,128]{1,0:T(8,128)(2,1)S(1)} %pad_maximum_fusion.4), channel_id=1, source_target_pairs={{0,8},{4,12},{8,0},{12,4},{16,24},{20,28},{24,16},{28,20},{1,9},{5... | collective-permute-start | bytes 202760 | tf_op jit(solution)/shard_map/ppermute | solution.py:114
  6.9 13.8 %collective-permute-start.8 = (bf16[256,128]{1,0:T(8,128)(2,1)S(1)}, bf16[256,128]{1,0:T(8,128)(2,1)S(1)}, u32[]{:S(2)}, u32[]{:S(2)}) collective-permute-start(bf16[256,128]{1,0:T(8,128)(2,1)S(1)} %copy-done), channel_id=1, source_target_pairs={{0,24},{4,28},{8,16},{12,20},{16,8},{20,12},{24,0},{28,4},{1,25},{... | collective-permute-start | bytes 196616 | tf_op jit(solution)/shard_map/ppermute | solution.py:114
  10.1 8.2 %collective-permute-start.6 = (bf16[512,128]{1,0:T(8,128)(2,1)S(1)}, bf16[512,128]{1,0:T(8,128)(2,1)S(1)}, u32[]{:S(2)}, u32[]{:S(2)}) collective-permute-start(bf16[512,128]{1,0:T(8,128)(2,1)S(1)} %pad_maximum_fusion.2), channel_id=1, source_target_pairs={{0,8},{4,20},{8,0},{12,28},{16,24},{20,4},{24,16},{28,12},{1,9},{5... | collective-permute-start | bytes 393224 | tf_op jit(solution)/shard_map/ppermute | solution.py:171
  12.3 6.1 %collective-permute-start.10 = (f16[264,128]{1,0:T(8,128)(2,1)S(1)}, f16[264,128]{1,0:T(8,128)(2,1)S(1)}, u32[]{:S(2)}, u32[]{:S(2)}) collective-permute-start(f16[264,128]{1,0:T(8,128)(2,1)S(1)} %pad_maximum_fusion.5), channel_id=1, source_target_pairs={{2,0},{8,1},{3,2},{10,3},{6,4},{12,5},{7,6},{14,7},{11,8},{0,9},{1... | collective-permute-start | bytes 202760 | tf_op jit(solution)/shard_map/ppermute | solution.py:124
  14.5 6.1 %collective-permute-start.9 = (f16[264,128]{1,0:T(8,128)(2,1)S(1)}, f16[264,128]{1,0:T(8,128)(2,1)S(1)}, u32[]{:S(2)}, u32[]{:S(2)}) collective-permute-start(f16[264,128]{1,0:T(8,128)(2,1)S(1)} %pad_maximum_fusion.5), channel_id=1, source_target_pairs={{3,0},{26,1},{0,2},{1,3},{7,4},{30,5},{4,6},{5,7},{9,8},{10,9},{11... | collective-permute-start | bytes 202760 | tf_op jit(solution)/shard_map/ppermute | solution.py:124
  15.3 5.5 %collective-permute-start.5 = (f16[264,128]{1,0:T(8,128)(2,1)S(1)}, f16[264,128]{1,0:T(8,128)(2,1)S(1)}, u32[]{:S(2)}, u32[]{:S(2)}) collective-permute-start(f16[264,128]{1,0:T(8,128)(2,1)S(1)} %pad_maximum_fusion.5), channel_id=1, source_target_pairs={{1,0},{3,1},{9,2},{0,3},{5,4},{7,5},{13,6},{4,7},{10,8},{11,9},{24... | collective-permute-start | bytes 202760 | tf_op jit(solution)/shard_map/ppermute | solution.py:124
  18.4 2.3 %collective-permute-start.7 = (f32[512,128]{1,0:T(8,128)S(1)}, f32[512,128]{1,0:T(8,128)S(1)}, u32[]{:S(2)}, u32[]{:S(2)}) collective-permute-start(f32[512,128]{1,0:T(8,128)S(1)} %pad_maximum_fusion), channel_id=1, source_target_pairs={{0,4},{4,0},{8,12},{12,8},{16,20},{20,16},{24,28},{28,24},{1,5},{5... | collective-permute-start | bytes 786440 | tf_op jit(solution)/shard_map/ppermute | solution.py:111
  21.4 1.4 %collective-permute-start.11 = (bf16[512,128]{1,0:T(8,128)(2,1)S(1)}, bf16[512,128]{1,0:T(8,128)(2,1)S(1)}, u32[]{:S(2)}, u32[]{:S(2)}) collective-permute-start(bf16[512,128]{1,0:T(8,128)(2,1)S(1)} %pad_maximum_fusion.3), channel_id=1, source_target_pairs={{0,4},{4,0},{8,12},{12,8},{16,20},{20,16},{24,28},{28,24},{1,5},{5... | collective-permute-start | bytes 393224 | tf_op jit(solution)/shard_map/ppermute | solution.py:111
  21.5 1.3 %copy-start.1 = (bf16[256,512]{1,0:T(8,128)(2,1)S(1)}, bf16[256,512]{1,0:T(8,128)(2,1)}, u32[]{:S(2)}) copy-start(bf16[256,512]{1,0:T(8,128)(2,1)} %a_ref.1) | copy-start | bytes 786436
